TPU v7x, 32 devices: a whole 2x2x4 slice. The times are simulated.
32 devices in a mesh: dp: 4 (over z), seq: 2 (over y), shard: 4 (over x, core).
Axes of the slice: x: 2, y: 2, z: 4, core: 2. Of those that a mesh axis runs over, the one named last changes fastest.
Arguments:
- tokens: bfloat16 [16, 1024, 768], P(('dp', 'shard'), 'seq'), may hold values from -18 to 18
- cotangent: bfloat16 [16, 1024, 768], P(('dp', 'shard'), 'seq'), may hold values from -6 to 6
- previous_logits: float32 [16, 1024, 12], P(('dp', 'shard'), 'seq'), may hold values from -2 to 2
- routes: int32 [16, 1024, 2], P(('dp', 'shard'), 'seq'), may hold values from 0 to 11, all different within a row
- priority: int32 [16, 2, 512], P(('dp', 'shard'), 'seq'), may hold values from 0 to 511, each once within a row
- attention_master: float32 [4, 768, 768], P(None, ('dp', 'seq', 'shard')), may hold values from -2 to 2
- vector_master: float32 [16, 768], P(None, ('dp', 'seq', 'shard')), may hold values from -6 to 6
- expert_master: float32 [8, 3, 768, 2048], P('shard', None, ('dp', 'seq')), may hold values from -5 to 5
- mixing_master: float32 [12, 12], replicated, may hold values from -1.75 to 1.75
- attention_first: float32 [4, 768, 768], P(None, ('dp', 'seq', 'shard')), may hold values from -16 to 16
- vector_first: float32 [16, 768], P(None, ('dp', 'seq', 'shard')), may hold values from -16 to 16
- expert_first: float32 [8, 3, 768, 2048], P('shard', None, ('dp', 'seq')), may hold values from -16 to 16
- mixing_first: float32 [12, 12], replicated, may hold values from -16 to 16
- attention_second: float32 [4, 768, 768], P(None, ('dp', 'seq', 'shard')), may hold values from 0 to 1.6384
- vector_second: float32 [16, 768], P(None, ('dp', 'seq', 'shard')), may hold values from 0 to 1.6384
- expert_second: float32 [8, 3, 768, 2048], P('shard', None, ('dp', 'seq')), may hold values from 0 to 1.6384
- mixing_second: float32 [12, 12], replicated, may hold values from 16.384 to 65.536
Outputs:
- block_output: bfloat16 [16, 1024, 768], P(('dp', 'shard'), 'seq')
- input_gradient: float32 [16, 1024, 768], P(('dp', 'shard'), 'seq')
- new_attention: float32 [4, 768, 768], P(None, ('dp', 'seq', 'shard'))
- new_vector: float32 [16, 768], P(None, ('dp', 'seq', 'shard'))
- new_expert: float32 [8, 3, 768, 2048], P('shard', None, ('dp', 'seq'))
- new_mixing: float32 [12, 12], replicated
- moment_attention: float32 [4, 768, 768], P(None, ('dp', 'seq', 'shard'))
- moment_vector: float32 [16, 768], P(None, ('dp', 'seq', 'shard'))
- moment_expert: float32 [8, 3, 768, 2048], P('shard', None, ('dp', 'seq'))
- moment_mixing: float32 [12, 12], replicated
- square_attention: float32 [4, 768, 768], P(None, ('dp', 'seq', 'shard'))
- square_vector: float32 [16, 768], P(None, ('dp', 'seq', 'shard'))
- square_expert: float32 [8, 3, 768, 2048], P('shard', None, ('dp', 'seq'))
- square_mixing: float32 [12, 12], replicated
- tensor_norms: float32 [2, 33], replicated
Inputs may be any that keep to these rules, and one draw needn't show every extreme that they name: `routes`: each row names 2 different experts; 0 .. 7 are feed-forward experts, 8 the zero expert, 9 the copy expert, 10 and 11 the constant experts; every expert is named by some row. Each priority[s, c, :] is a permutation of 0 .. 511.
All inputs are finite; a program needn't handle non-finite values.
Results may differ from a plain program's by a relative error of at most 0.024.
The roundings to bfloat16 on the way count: a program that leaves them out, or rounds other values in their place, can miss the bound.
Values may be sent and summed in bfloat16 or wider, within the bound.
No kernel may reach another device: no remote copies, remote signals or barrier semaphores. Data moves between devices by JAX's collectives and lax.ppermute only.
A program may use at most 512 MiB of HBM per device.

v0:
```python
import jax
import jax.numpy as jnp
from jax import lax
from jax.sharding import PartitionSpec as P

HEADS = 12
HDIM = 64
NFFN = 8
TOP = 2
STEP = 4
NEXP = 12


beta_one = 0.9
beta_two = 0.999
adam_eps = 1e-06
weight_decay = 0.01
learn_rate = 0.25
norm_eps = 1e-06
rope_base = 10000.0


def exact_dot(left, right):
    return jnp.dot(left, right, precision=lax.Precision.HIGHEST, preferred_element_type=jnp.float32)


def exact_einsum(form, left, right):
    return jnp.einsum(
        form, left, right, precision=lax.Precision.HIGHEST, preferred_element_type=jnp.float32
    )


def root_norm(values, gain):
    return values * lax.rsqrt(jnp.mean(values * values, axis=-1, keepdims=True) + norm_eps) * gain


def rotary_tables(positions):
    freqs = rope_base ** (-jnp.arange(0, HDIM, 2).astype(jnp.float32) / HDIM)
    angles = positions[:, None] * freqs[None, :]
    cosine = jnp.concatenate([jnp.cos(angles), jnp.cos(angles)], axis=-1)
    sine_table = jnp.concatenate([jnp.sin(angles), jnp.sin(angles)], axis=-1)
    return (cosine, sine_table)


def rotate(values, cosine, sine_table):
    half_size = values.shape[-1] // 2
    turned = jnp.concatenate([-values[..., half_size:], values[..., :half_size]], axis=-1)
    return values * cosine[:, None, :] + turned * sine_table[:, None, :]


def softmax_rows(logits):
    row_top = jnp.max(logits, axis=-1, keepdims=True)
    expd_values = jnp.exp(logits - row_top)
    return expd_values / jnp.sum(expd_values, axis=-1, keepdims=True)


def swiglu(gate_pre, up_pre):
    return gate_pre * jax.nn.sigmoid(gate_pre) * up_pre


def placement(route_rows, order_rows, capacity):
    hits = jnp.sum(jax.nn.one_hot(route_rows, NEXP, dtype=jnp.float32), axis=-2)
    before = (order_rows[:, None, :] < order_rows[:, :, None]).astype(jnp.float32)
    counts = exact_einsum("gtu,gue->gte", before, hits)
    slot_counts = jnp.take_along_axis(counts, route_rows, axis=-1)
    kept_mask = (route_rows < NFFN) & (slot_counts < capacity)
    return (slot_counts, kept_mask)


def moments(weight, first, second, grad):
    first_new = beta_one * first + (1.0 - beta_one) * grad
    second_new = beta_two * second + (1.0 - beta_two) * grad * grad
    step_value = (
        first_new
        / (1.0 - beta_one**STEP)
        / (jnp.sqrt(second_new / (1.0 - beta_two**STEP)) + adam_eps)
        + weight_decay * weight
    )
    return (first_new, second_new, step_value)


def tensor_squares(attention_x, vector_x, expert_x, owner):
    vector_parts = jnp.stack(
        [
            jnp.sum(vector_x[0] * vector_x[0]),
            jnp.sum(vector_x[1] * vector_x[1]),
            jnp.sum(vector_x[2:4] * vector_x[2:4]),
            jnp.sum(vector_x[4:] * vector_x[4:]),
        ]
    )
    expert_parts = exact_dot(owner, jnp.sum(expert_x * expert_x, axis=(2, 3))).reshape(-1)
    return jnp.concatenate(
        [jnp.sum(attention_x * attention_x, axis=(1, 2)), vector_parts, expert_parts]
    )


def apply_ratio(weights, steps, ratios, expert_first_index, local_experts):
    attention_w, vector_w, expert_w, mixing_w = weights
    attention_s, vector_s, expert_s, mixing_s = steps
    attention_ratio = ratios[0:4][:, None, None]
    vector_ratio = jnp.concatenate(
        [
            ratios[4:6],
            jnp.broadcast_to(ratios[6:7], (2,)),
            jnp.broadcast_to(ratios[7:8], (vector_w.shape[0] - 4,)),
        ]
    )[:, None]
    expert_ratio = lax.dynamic_slice_in_dim(
        ratios[8 : 8 + 3 * NFFN].reshape(NFFN, 3), expert_first_index, local_experts, 0
    )[:, :, None, None]
    mixing_ratio = ratios[8 + 3 * NFFN]
    return (
        attention_w - learn_rate * attention_ratio * attention_s,
        vector_w - learn_rate * vector_ratio * vector_s,
        expert_w - learn_rate * expert_ratio * expert_s,
        mixing_w - learn_rate * mixing_ratio * mixing_s,
    )


def shards(
    tokens,
    cotangent,
    previous_logits,
    routes,
    priority,
    attention_master,
    vector_master,
    expert_master,
    mixing_master,
    attention_first,
    vector_first,
    expert_first,
    mixing_first,
    attention_second,
    vector_second,
    expert_second,
    mixing_second,
):
    attention_all, vector_all = (
        lax.all_gather(
            attention_master.astype(jnp.bfloat16), ("dp", "seq", "shard"), axis=1, tiled=True
        ),
        lax.all_gather(
            vector_master.astype(jnp.bfloat16), ("dp", "seq", "shard"), axis=1, tiled=True
        ),
    )
    expert_rows = lax.all_gather(
        expert_master.astype(jnp.bfloat16), ("dp", "seq"), axis=2, tiled=True
    )
    expert_use = lax.all_gather(expert_rows, "shard", axis=0, tiled=True)
    local_experts = expert_master.shape[0]
    expert_first_index = lax.axis_index("shard") * local_experts
    owner = (
        jnp.arange(NFFN)[:, None] == (expert_first_index + jnp.arange(local_experts))[None, :]
    ).astype(jnp.float32)
    inputs = tokens[0].astype(jnp.float32)
    row_count, model_width = inputs.shape
    positions = (lax.axis_index("seq") * row_count + jnp.arange(row_count)).astype(jnp.float32)
    cosine, sine_table = rotary_tables(positions)
    normed, norm_pull = jax.vjp(root_norm, inputs, vector_all[0].astype(jnp.float32))
    normed_low = normed.astype(jnp.bfloat16)
    query_pre = jnp.dot(normed_low, attention_all[0], preferred_element_type=jnp.float32).reshape(
        row_count, HEADS, HDIM
    )
    key_pre = jnp.dot(normed_low, attention_all[1], preferred_element_type=jnp.float32).reshape(
        row_count, HEADS, HDIM
    )
    query_rot, rope_pull = jax.vjp(lambda values: rotate(values, cosine, sine_table), query_pre)
    key_rot = rotate(key_pre, cosine, sine_table)
    value_send = jnp.dot(normed_low, attention_all[2], preferred_element_type=jnp.float32).astype(
        jnp.bfloat16
    )
    query_send = query_rot.reshape(row_count, model_width).astype(jnp.bfloat16)
    key_send = key_rot.reshape(row_count, model_width).astype(jnp.bfloat16)
    query_heads, key_heads, value_heads = (
        lax.all_to_all(query_send, "seq", split_axis=1, concat_axis=0, tiled=True),
        lax.all_to_all(key_send, "seq", split_axis=1, concat_axis=0, tiled=True),
        lax.all_to_all(value_send, "seq", split_axis=1, concat_axis=0, tiled=True),
    )
    seq_length = query_heads.shape[0]
    local_heads = query_heads.shape[1] // HDIM
    query_heads = query_heads.reshape(seq_length, local_heads, HDIM)
    key_heads = key_heads.reshape(seq_length, local_heads, HDIM)
    value_heads = value_heads.reshape(seq_length, local_heads, HDIM)
    block_rows = min(512, seq_length)
    block_count = seq_length // block_rows
    key_positions = jnp.arange(seq_length)
    score_scale = HDIM ** (-0.5)

    def block_scores(first_row):
        query_block = lax.slice_in_dim(query_heads, first_row, first_row + block_rows, axis=0)
        raw_scores = (
            jnp.einsum("qhd,khd->hqk", query_block, key_heads, preferred_element_type=jnp.float32)
            * score_scale
        )
        causal = (first_row + jnp.arange(block_rows))[:, None] >= key_positions[None, :]
        return (jnp.where(causal[None], raw_scores, -1e30), query_block)

    mixed_blocks = []
    lse_blocks = []
    for block_index in range(block_count):
        scores, query_block = block_scores(block_index * block_rows)
        row_top = jnp.max(scores, axis=-1, keepdims=True)
        row_total = jnp.sum(jnp.exp(scores - row_top), axis=-1, keepdims=True)
        log_total = row_top + jnp.log(row_total)
        weights_block = jnp.exp(scores - log_total)
        mixed_blocks.append(
            jnp.einsum(
                "hqk,khd->qhd",
                weights_block.astype(jnp.bfloat16),
                value_heads,
                preferred_element_type=jnp.float32,
            )
        )
        lse_blocks.append(log_total)
    mixed_heads = (
        jnp.concatenate(mixed_blocks, axis=0)
        .reshape(seq_length, local_heads * HDIM)
        .astype(jnp.bfloat16)
    )
    mixed_tokens = lax.all_to_all(mixed_heads, "seq", split_axis=0, concat_axis=1, tiled=True)
    branch = jnp.dot(mixed_tokens, attention_all[3], preferred_element_type=jnp.float32)
    resid = inputs + branch
    normed_two, norm_two_pull = jax.vjp(root_norm, resid, vector_all[1].astype(jnp.float32))
    expert_in = normed_two.astype(jnp.bfloat16)
    router = vector_all[4:]
    previous = previous_logits[0]
    logits = jnp.dot(expert_in, router.T, preferred_element_type=jnp.float32) + exact_dot(
        previous, mixing_master
    )
    gates, gate_pull = jax.vjp(softmax_rows, logits)
    route_rows = routes[0]
    picked = jnp.take_along_axis(gates, route_rows, axis=1)
    expert_total = logits.shape[1]
    capacity = 9 * row_count * TOP // (8 * expert_total)
    slot_counts, kept_mask = placement(route_rows[None], priority[0], capacity)
    slot_counts = slot_counts[0]
    kept_mask = kept_mask[0]
    slot_index = route_rows * capacity + slot_counts.astype(jnp.int32)
    safe_index = jnp.where(kept_mask, slot_index, 0)
    dispatch = (
        (safe_index[:, :, None] == jnp.arange(NFFN * capacity)[None, None, :])
        & kept_mask[:, :, None]
    ).astype(jnp.bfloat16)
    taken = (
        jnp.einsum("tks,td->sd", dispatch, expert_in, preferred_element_type=jnp.float32)
        .astype(jnp.bfloat16)
        .reshape(NFFN, capacity, model_width)
    )
    gate_pre = jnp.einsum(
        "ecd,edf->ecf", taken, expert_use[:, 0], preferred_element_type=jnp.float32
    )
    up_pre = jnp.einsum("ecd,edf->ecf", taken, expert_use[:, 1], preferred_element_type=jnp.float32)
    hidden, swiglu_pull = jax.vjp(swiglu, gate_pre, up_pre)
    hidden_low = hidden.astype(jnp.bfloat16)
    result_local = jnp.einsum(
        "ecf,edf->ecd", hidden_low, expert_use[:, 2], preferred_element_type=jnp.float32
    ).astype(jnp.bfloat16)
    result = result_local.reshape(NFFN * capacity, model_width)
    consts = vector_all[2:4].astype(jnp.float32)
    chosen = []
    for which_slot in range(TOP):
        route_col = route_rows[:, which_slot][:, None]
        ffn_part = jnp.where(
            kept_mask[:, which_slot][:, None],
            jnp.take(result, safe_index[:, which_slot], axis=0).astype(jnp.float32),
            0.0,
        )
        entry = ffn_part + jnp.where(route_col == NFFN + 1, normed_two, 0.0)
        entry = entry + jnp.where(route_col == NFFN + 2, consts[0][None, :], 0.0)
        entry = entry + jnp.where(route_col == NFFN + 3, consts[1][None, :], 0.0)
        chosen.append(entry)
    mixture = picked[:, 0:1] * chosen[0]
    which_slot = 1
    mixture = mixture + picked[:, which_slot : which_slot + 1] * chosen[which_slot]
    block_output = (resid + mixture).astype(jnp.bfloat16)
    upstream = cotangent[0].astype(jnp.float32)
    expert_ids = jnp.arange(expert_total)[None, :]
    dgates = jnp.zeros_like(gates)
    dnormed_two = jnp.zeros_like(normed_two)
    dconst_one = jnp.zeros((model_width,), jnp.float32)
    dconst_two = jnp.zeros((model_width,), jnp.float32)
    dresult_rows = []
    for which_slot in range(TOP):
        route_col = route_rows[:, which_slot][:, None]
        dpicked = jnp.sum(upstream * chosen[which_slot], axis=-1)
        dgates = dgates + jnp.where(route_col == expert_ids, dpicked[:, None], 0.0)
        dvalue = picked[:, which_slot : which_slot + 1] * upstream
        dnormed_two = dnormed_two + jnp.where(route_col == NFFN + 1, dvalue, 0.0)
        dconst_one = dconst_one + jnp.sum(jnp.where(route_col == NFFN + 2, dvalue, 0.0), axis=0)
        dconst_two = dconst_two + jnp.sum(jnp.where(route_col == NFFN + 3, dvalue, 0.0), axis=0)
        dresult_rows.append(
            jnp.where(kept_mask[:, which_slot][:, None], dvalue, 0.0).astype(jnp.bfloat16)
        )
    dresult = (
        jnp.einsum(
            "tks,tkd->sd",
            dispatch,
            jnp.stack(dresult_rows, axis=1),
            preferred_element_type=jnp.float32,
        )
        .astype(jnp.bfloat16)
        .reshape(NFFN, capacity, model_width)
    )
    dweight_down = jnp.einsum(
        "ecd,ecf->edf", dresult, hidden_low, preferred_element_type=jnp.float32
    )
    dhidden = jnp.einsum(
        "ecd,edf->ecf", dresult, expert_use[:, 2], preferred_element_type=jnp.float32
    )
    dgate_pre, dup_pre = swiglu_pull(dhidden)
    dgate_low = dgate_pre.astype(jnp.bfloat16)
    dup_low = dup_pre.astype(jnp.bfloat16)
    dweight_gate = jnp.einsum("ecd,ecf->edf", taken, dgate_low, preferred_element_type=jnp.float32)
    dweight_up = jnp.einsum("ecd,ecf->edf", taken, dup_low, preferred_element_type=jnp.float32)
    dtaken_local = jnp.einsum(
        "ecf,edf->ecd", dgate_low, expert_use[:, 0], preferred_element_type=jnp.float32
    )
    dtaken_local = (
        dtaken_local
        + jnp.einsum("ecf,edf->ecd", dup_low, expert_use[:, 1], preferred_element_type=jnp.float32)
    ).astype(jnp.bfloat16)
    dtaken = dtaken_local.reshape(NFFN * capacity, model_width)
    for which_slot in range(TOP):
        dnormed_two = dnormed_two + jnp.where(
            kept_mask[:, which_slot][:, None],
            jnp.take(dtaken, safe_index[:, which_slot], axis=0).astype(jnp.float32),
            0.0,
        )
    dlogits = gate_pull(dgates)[0]
    dnormed_two = dnormed_two + exact_dot(dlogits, router.astype(jnp.float32))
    drouter = exact_dot(dlogits.T, expert_in.astype(jnp.float32))
    dmixing_local = exact_dot(previous.T, dlogits)
    dresid_norm, dgain_two = norm_two_pull(dnormed_two)
    dresid = upstream + dresid_norm
    dbranch_low = dresid.astype(jnp.bfloat16)
    dweight_out = jnp.einsum(
        "td,te->de", mixed_tokens, dbranch_low, preferred_element_type=jnp.float32
    )
    dmixed = jnp.einsum(
        "te,de->td", dbranch_low, attention_all[3], preferred_element_type=jnp.float32
    ).astype(jnp.bfloat16)
    dmixed_heads = lax.all_to_all(dmixed, "seq", split_axis=1, concat_axis=0, tiled=True).reshape(
        seq_length, local_heads, HDIM
    )
    dquery_blocks = []
    dkey_heads = jnp.zeros((seq_length, local_heads, HDIM), jnp.float32)
    dvalue_heads = jnp.zeros((seq_length, local_heads, HDIM), jnp.float32)
    for block_index in range(block_count):
        first_row = block_index * block_rows
        scores, query_block = block_scores(first_row)
        weights_block = jnp.exp(scores - lse_blocks[block_index])
        dmixed_block = lax.slice_in_dim(dmixed_heads, first_row, first_row + block_rows, axis=0)
        dweights = jnp.einsum(
            "qhd,khd->hqk", dmixed_block, value_heads, preferred_element_type=jnp.float32
        )
        row_delta = jnp.sum(weights_block * dweights, axis=-1, keepdims=True)
        dscores = (weights_block * (dweights - row_delta)).astype(jnp.bfloat16)
        dquery_blocks.append(
            jnp.einsum("hqk,khd->qhd", dscores, key_heads, preferred_element_type=jnp.float32)
            * score_scale
        )
        dkey_heads = (
            dkey_heads
            + jnp.einsum("hqk,qhd->khd", dscores, query_block, preferred_element_type=jnp.float32)
            * score_scale
        )
        dvalue_heads = dvalue_heads + jnp.einsum(
            "hqk,qhd->khd",
            weights_block.astype(jnp.bfloat16),
            dmixed_block,
            preferred_element_type=jnp.float32,
        )
    dquery_send = (
        jnp.concatenate(dquery_blocks, axis=0)
        .reshape(seq_length, local_heads * HDIM)
        .astype(jnp.bfloat16)
    )
    dkey_send = dkey_heads.reshape(seq_length, local_heads * HDIM).astype(jnp.bfloat16)
    dvalue_send = dvalue_heads.reshape(seq_length, local_heads * HDIM).astype(jnp.bfloat16)
    dquery_tok, dkey_tok, dvalue_tok = (
        lax.all_to_all(dquery_send, "seq", split_axis=0, concat_axis=1, tiled=True),
        lax.all_to_all(dkey_send, "seq", split_axis=0, concat_axis=1, tiled=True),
        lax.all_to_all(dvalue_send, "seq", split_axis=0, concat_axis=1, tiled=True),
    )
    dquery_pre = (
        rope_pull(dquery_tok.astype(jnp.float32).reshape(row_count, HEADS, HDIM))[0]
        .reshape(row_count, model_width)
        .astype(jnp.bfloat16)
    )
    dkey_pre = (
        rope_pull(dkey_tok.astype(jnp.float32).reshape(row_count, HEADS, HDIM))[0]
        .reshape(row_count, model_width)
        .astype(jnp.bfloat16)
    )
    dweight_query = jnp.einsum(
        "td,te->de", normed_low, dquery_pre, preferred_element_type=jnp.float32
    )
    dweight_key = jnp.einsum("td,te->de", normed_low, dkey_pre, preferred_element_type=jnp.float32)
    dweight_value = jnp.einsum(
        "td,te->de", normed_low, dvalue_tok, preferred_element_type=jnp.float32
    )
    dnormed = jnp.einsum(
        "te,de->td", dquery_pre, attention_all[0], preferred_element_type=jnp.float32
    )
    dnormed = dnormed + jnp.einsum(
        "te,de->td", dkey_pre, attention_all[1], preferred_element_type=jnp.float32
    )
    dnormed = dnormed + jnp.einsum(
        "te,de->td", dvalue_tok, attention_all[2], preferred_element_type=jnp.float32
    )
    dinputs_norm, dgain_one = norm_pull(dnormed)
    input_gradient = dresid + dinputs_norm
    attention_grad = jnp.stack([dweight_query, dweight_key, dweight_value, dweight_out])
    vector_grad = jnp.concatenate(
        [dgain_one[None], dgain_two[None], dconst_one[None], dconst_two[None], drouter], axis=0
    )
    attention_sum, vector_sum = (
        lax.psum_scatter(attention_grad, ("dp", "seq", "shard"), scatter_dimension=1, tiled=True),
        lax.psum_scatter(vector_grad, ("dp", "seq", "shard"), scatter_dimension=1, tiled=True),
    )
    gate_share, up_share, down_share = (
        lax.psum_scatter(dweight_gate, "shard", scatter_dimension=0, tiled=True),
        lax.psum_scatter(dweight_up, "shard", scatter_dimension=0, tiled=True),
        lax.psum_scatter(dweight_down, "shard", scatter_dimension=0, tiled=True),
    )
    expert_local = jnp.stack([gate_share, up_share, down_share], axis=1)
    expert_sum = lax.psum_scatter(expert_local, ("dp", "seq"), scatter_dimension=2, tiled=True)
    attention_m, attention_s, attention_u = moments(
        attention_master, attention_first, attention_second, attention_sum
    )
    vector_m, vector_s, vector_u = moments(vector_master, vector_first, vector_second, vector_sum)
    expert_m, expert_s, expert_u = moments(expert_master, expert_first, expert_second, expert_sum)
    partial_squares = jnp.stack(
        [
            tensor_squares(attention_master, vector_master, expert_master, owner),
            tensor_squares(attention_u, vector_u, expert_u, owner),
        ]
    )
    summed_squares, mixing_grad = lax.psum((partial_squares, dmixing_local), ("dp", "seq", "shard"))
    mixing_m, mixing_s, mixing_u = moments(mixing_master, mixing_first, mixing_second, mixing_grad)
    mixing_squares = jnp.stack(
        [jnp.sum(mixing_master * mixing_master), jnp.sum(mixing_u * mixing_u)]
    )
    tensor_norms = jnp.sqrt(jnp.concatenate([summed_squares, mixing_squares[:, None]], axis=1))
    ratios = tensor_norms[0] / (tensor_norms[1] + norm_eps)
    new_attention, new_vector, new_expert, new_mixing = apply_ratio(
        (attention_master, vector_master, expert_master, mixing_master),
        (attention_u, vector_u, expert_u, mixing_u),
        ratios,
        expert_first_index,
        local_experts,
    )
    return (
        block_output[None],
        input_gradient[None],
        new_attention,
        new_vector,
        new_expert,
        new_mixing,
        attention_m,
        vector_m,
        expert_m,
        mixing_m,
        attention_s,
        vector_s,
        expert_s,
        mixing_s,
        tensor_norms,
    )


def solution(mesh):
    return jax.shard_map(
        shards,
        mesh=mesh,
        in_specs=(
            P(("dp", "shard"), "seq", None),
            P(("dp", "shard"), "seq", None),
            P(("dp", "shard"), "seq", None),
            P(("dp", "shard"), "seq", None),
            P(("dp", "shard"), "seq", None),
            P(None, ("dp", "seq", "shard"), None),
            P(None, ("dp", "seq", "shard")),
            P("shard", None, ("dp", "seq"), None),
            P(),
            P(None, ("dp", "seq", "shard"), None),
            P(None, ("dp", "seq", "shard")),
            P("shard", None, ("dp", "seq"), None),
            P(),
            P(None, ("dp", "seq", "shard"), None),
            P(None, ("dp", "seq", "shard")),
            P("shard", None, ("dp", "seq"), None),
            P(),
        ),
        out_specs=(
            P(("dp", "shard"), "seq", None),
            P(("dp", "shard"), "seq", None),
            P(None, ("dp", "seq", "shard"), None),
            P(None, ("dp", "seq", "shard")),
            P("shard", None, ("dp", "seq"), None),
            P(),
            P(None, ("dp", "seq", "shard"), None),
            P(None, ("dp", "seq", "shard")),
            P("shard", None, ("dp", "seq"), None),
            P(),
            P(None, ("dp", "seq", "shard"), None),
            P(None, ("dp", "seq", "shard")),
            P("shard", None, ("dp", "seq"), None),
            P(),
            P(),
        ),
        check_vma=False,
    )
```

profile of v0, /device:TPU:0, one launch (start us, length us, event | category | flops | bytes accessed | tf_op | source)
XLA Modules:
  0.0 2824.3 jit_solution(12360470689022916089)
XLA Ops:
  7.2 4.1 copy.291
  13.0 363.6 %all-gather.7.cloned.1.call-done = bf16[2,3,768,2048]{3,2,0,1:T(8,128)(2,1)} async-done(((bf16[2,3,96,2048]{3,2,0,1:T(8,128)(2,1)}), bf16[2,3,768,2048]{3,2,0,1:T(8,128)(2,1)}) %all-gather.7.cloned.1.call-update) | async-done | bytes 18874384 | tf_op jit(solution)/shard_map/all_gather | solution.py:147
  377.4 41.1 %all-gather = bf16[32,24,16]{1,2,0:T(8,128)(2,1)S(1)} all-gather(bf16[1,24,16]{1,2,0:T(8,128)(2,1)S(1)} %convert_bitcast_fusion.3), channel_id=1, replica_groups=mesh['dp'=4,'seq'=2,'shard'=4] {'dp','seq','shard'}, dimensions={0}, use_global_device_ids=true | all-gather | bytes 25344 | tf_op jit(solution)/shard_map/all_gather | solution.py:143
  419.4 24.3 all-gather.5.cloned.1.call-done
  446.9 4.3 all-to-all-start
  462.8 3.7 all-to-all-start.2
  467.2 10.0 all-to-all-done.2
  477.1 4.7 all-to-all-start.1
  482.2 8.6 gather_fusion.1
  491.7 3.3 copy.231
  505.8 3.7 exponential_reduce_fusion
  511.9 4.2 exponential_reduce_fusion.1
  516.5 3.3 fusion.77
  519.9 7.8 fusion.76
  529.3 3.5 all-to-all-start.3
  534.7 8.0 all-to-all-done.3
  547.7 8.8 gather_fusion
  559.8 326.0 %all-gather.9.cloned.1.call-done = bf16[8,3,768,2048]{3,2,0,1:T(8,128)(2,1)} async-done(((bf16[2,3,768,2048]{3,2,0,1:T(8,128)(2,1)}), bf16[8,3,768,2048]{3,2,0,1:T(8,128)(2,1)}) %all-gather.9.cloned.1.call-update) | async-done | bytes 75497488 | tf_op jit(solution)/shard_map/all_gather | solution.py:150
  885.8 10.3 fusion.1
  896.1 13.2 fusion.3
  909.2 18.6 multiply_convert_fusion.2
  927.9 21.4 fusion.171
  949.4 33.3 %fusion.170 = f32[8,768,2048]{2,1,0:T(8,128)} fusion(bf16[8,96,768]{2,1,0:T(8,128)(2,1)S(1)} %bitcast.345, bf16[8,96,2048]{2,1,0:T(8,128)(2,1)} %get-tuple-element.156), kind=kOutput, calls=%fused_computation.329 | convolution fusion | flops 2415919104 | bytes 54657024 | tf_op jit(solution)/shard_map/ecd,ecf->edf/dot_general | solution.py:315
  982.7 31.8 %fusion.169 = f32[8,768,2048]{2,1,0:T(8,128)} fusion(bf16[8,96,768]{2,1,0:T(8,128)(2,1)S(1)} %bitcast.346, bf16[8,96,2048]{2,1,0:T(8,128)(2,1)} %get-tuple-element.157), kind=kOutput, calls=%fused_computation.328 | convolution fusion | flops 2415919104 | bytes 54657024 | tf_op jit(solution)/shard_map/ecd,ecf->edf/dot_general | solution.py:314
  1017.2 14.2 fusion.71
  1031.4 2.7 gather_fusion.2
  1034.1 2.7 gather_fusion.3
  1036.8 14.6 fusion
  1051.4 14.4 add_convert_fusion
  1065.9 2.7 gather_fusion.5
  1068.6 3.0 gather_fusion.4
  1071.8 4.9 fusion.57
  1081.3 2.8 convolution_convert_fusion.1
  1084.2 14.5 all_to_all.110
  1102.3 10.7 multiply_reduce_fusion.1
  1113.1 10.3 multiply_convert_fusion.1
  1126.3 7.1 multiply_reduce_fusion
  1133.4 6.9 multiply_convert_fusion
  1145.1 3.3 convert_element_type.328
  1150.5 4.5 all-to-all-start.6
  1155.1 5.0 fusion.78
  1160.1 7.6 fusion.144
  1173.5 4.3 all-to-all-start.5
  1177.8 7.8 fusion.73
  1189.3 3.7 all-to-all-start.7
  1193.4 3.6 convolution_bitcast_fusion
  1210.7 3.8 pad_maximum_fusion.1
  1214.6 78.0 %reduce-scatter.13.cloned.1.call-done = f32[2,768,2048]{2,1,0:T(8,128)} async-done(((f32[8,768,2048]{2,1,0:T(8,128)}), f32[2,768,2048]{2,1,0:T(8,128)}) %reduce-scatter.13.cloned.1.call-update) | async-done | bytes 12582928 | tf_op jit(solution)/shard_map/reduce_scatter | solution.py:425
  1292.6 345.8 %reduce-scatter.11.cloned.1.call-done = f32[2,768,2048]{2,1,0:T(8,128)} async-done(((f32[8,768,2048]{2,1,0:T(8,128)}), f32[2,768,2048]{2,1,0:T(8,128)}) %reduce-scatter.11.cloned.1.call-update) | async-done | bytes 12582928 | tf_op jit(solution)/shard_map/reduce_scatter | solution.py:424
  1638.5 345.7 %reduce-scatter.9.cloned.1.call-done = f32[2,768,2048]{2,1,0:T(8,128)} async-done(((f32[8,768,2048]{2,1,0:T(8,128)}), f32[2,768,2048]{2,1,0:T(8,128)}) %reduce-scatter.9.cloned.1.call-update) | async-done | bytes 12582928 | tf_op jit(solution)/shard_map/reduce_scatter | solution.py:423
  1984.1 27.7 pad_maximum_fusion
  2013.5 3.3 multiply_reduce_fusion.3
  2025.2 4.4 fusion.97
  2034.1 3.7 fusion.43
  2038.0 43.1 %all-reduce.4 = f32[16,768]{1,0:T(8,128)S(1)} all-reduce(f32[16,768]{1,0:T(8,128)S(1)} %concatenate.46), channel_id=3, replica_groups=mesh['dp'=4,'seq'=2,'shard'=4] {'dp','seq','shard'}, use_global_device_ids=true, to_apply=%region_33.35.clone | all-reduce | flops 12288 | bytes 98304
  2083.8 3.0 fusion.61
  2086.8 41.5 %reduce-scatter.7.cloned.1.call-done = f32[4,24,768]{2,1,0:T(8,128)} async-done(((f32[4,768,768]{2,1,0:T(8,128)}), f32[4,24,768]{2,1,0:T(8,128)}) %reduce-scatter.7.cloned.1.call-update) | async-done | bytes 294928 | tf_op jit(solution)/shard_map/reduce_scatter | solution.py:419
  2132.2 604.4 %reduce-scatter.15.cloned.1.call-done = f32[2,3,96,2048]{3,2,0,1:T(8,128)} async-done(((f32[2,3,768,2048]{3,2,0,1:T(8,128)}), f32[2,3,96,2048]{3,2,0,1:T(8,128)}) %reduce-scatter.15.cloned.1.call-update) | async-done | bytes 4718608 | tf_op jit(solution)/shard_map/reduce_scatter | solution.py:428
  2736.6 12.0 multiply_reduce_fusion.2
  2748.8 2.7 concatenate.47
  2751.5 39.5 %all-reduce.5 = (f32[12,12]{0,1:T(8,128)S(1)}, f32[2,32]{1,0:T(2,128)S(1)}) all-reduce(f32[12,12]{0,1:T(8,128)S(1)} %copy-done.100, f32[2,32]{1,0:T(2,128)S(1)} %pad_maximum_fusion.6), channel_id=1, replica_groups=mesh['dp'=4,'seq'=2,'shard'=4] {'dp','seq','shard'}, use_global_device_ids=true, to_apply=%region_45.47 | all-reduce | flops 208 | bytes 1664 | tf_op jit(solution)/shard_map/psum | solution.py:440
  2796.1 4.8 multiply_subtract_fusion
  2806.2 5.1 copy.261
  2811.3 5.1 copy.263
  (495 shorter events, 120.1 us)
Async XLA Ops:
  7.2 369.5 %all-gather.7.cloned.1.call-start = ((), (), s32[]{:S(2)}) async-start(), calls=%async_computation.14 | async-start | bytes 21233664 | tf_op jit(solution)/shard_map/all_gather | solution.py:147
  11.4 432.4 %all-gather.5.cloned.1.call-start = ((), (), s32[]{:S(2)}) async-start(), calls=%async_computation.13 | async-start | bytes 4866048 | tf_op jit(solution)/shard_map/all_gather | solution.py:140
  13.0 872.8 %all-gather.9.cloned.1.call-start = ((), (), s32[]{:S(2)}) async-start(), calls=%async_computation.15 | async-start | bytes 94371840 | tf_op jit(solution)/shard_map/all_gather | solution.py:150
  376.7 42.5 %copy-start.4 = (bf16[1,512,768]{2,1,0:T(8,128)(2,1)S(1)}, bf16[1,512,768]{2,1,0:T(8,128)(2,1)}, u32[]{:S(2)}) copy-start(bf16[1,512,768]{2,1,0:T(8,128)(2,1)} %param.19) | copy-start | bytes 2359300
  418.7 126.8 %copy-start.74 = (bf16[768,16]{0,1:T(8,128)(2,1)}, bf16[768,16]{0,1:T(8,128)(2,1)S(1)}, u32[]{:S(2)}) copy-start(bf16[768,16]{0,1:T(8,128)(2,1)S(1)} %reshape.746) | copy-start | bytes 73732
  418.8 39.1 %copy-start.70 = (f32[768]{0:T(1024)}, f32[768]{0:T(1024)S(1)}, u32[]{:S(2)}) copy-start(f32[768]{0:T(1024)S(1)} %get-tuple-element.121) | copy-start | bytes 9220
  418.8 126.5 %copy-start.76 = (f32[768]{0:T(1024)}, f32[768]{0:T(1024)S(1)}, u32[]{:S(2)}) copy-start(f32[768]{0:T(1024)S(1)} %get-tuple-element.120) | copy-start | bytes 9220
  419.2 40.6 %copy-start.46 = (f32[512,64]{0,1:T(8,128)}, f32[512,64]{0,1:T(8,128)S(1)}, u32[]{:S(2)}) copy-start(f32[512,64]{0,1:T(8,128)S(1)} %get-tuple-element.210) | copy-start | bytes 393220
  419.2 40.6 %copy-start.48 = (f32[512,64]{0,1:T(8,128)}, f32[512,64]{0,1:T(8,128)S(1)}, u32[]{:S(2)}) copy-start(f32[512,64]{0,1:T(8,128)S(1)} %get-tuple-element.211) | copy-start | bytes 393220
  419.4 27.4 copy-start.107
  419.4 38.5 %copy-start.84 = (f32[512]{0:T(512)}, f32[512]{0:T(512)S(1)}, u32[]{:S(2)}) copy-start(f32[512]{0:T(512)S(1)} %fusion.133) | copy-start | bytes 6148
  446.9 15.9 all-to-all-start
  462.8 14.4 all-to-all-start.2
  477.1 24.8 all-to-all-start.1
  491.4 28.5 %copy-start.16 = (pred[512,1024]{1,0:T(8,128)(4,1)}, pred[512,1024]{1,0:T(8,128)(4,1)S(1)}, u32[]{:S(2)}) copy-start(pred[512,1024]{1,0:T(8,128)(4,1)S(1)} %iota_compare_fusion.2) | copy-start | bytes 1572868
  491.7 24.7 copy-start.14
  497.6 22.3 copy-start.20
  529.3 13.4 all-to-all-start.3
  532.9 759.7 %reduce-scatter.13.cloned.1.call-start = ((), (), s32[]{:S(2)}) async-start(), calls=%async_computation.19 | async-start | bytes 62914560 | tf_op jit(solution)/shard_map/reduce_scatter | solution.py:425
  533.9 23.0 copy-start.121
  533.9 23.0 copy-start.124
  949.3 689.2 %reduce-scatter.11.cloned.1.call-start = ((), (), s32[]{:S(2)}) async-start(), calls=%async_computation.18 | async-start | bytes 62914560 | tf_op jit(solution)/shard_map/reduce_scatter | solution.py:424
  982.7 1001.4 %reduce-scatter.9.cloned.1.call-start = ((), (), s32[]{:S(2)}) async-start(), calls=%async_computation.17 | async-start | bytes 62914560 | tf_op jit(solution)/shard_map/reduce_scatter | solution.py:423
  1014.6 16.8 copy-start.117
  1015.4 56.4 %copy-start.91 = (f32[768]{0:T(1024)}, f32[768]{0:T(1024)S(1)}, u32[]{:S(2)}) copy-start(f32[768]{0:T(1024)S(1)} %get-tuple-element.126) | copy-start | bytes 9220
  1015.4 56.4 %copy-start.93 = (f32[768]{0:T(1024)}, f32[768]{0:T(1024)S(1)}, u32[]{:S(2)}) copy-start(f32[768]{0:T(1024)S(1)} %get-tuple-element.127) | copy-start | bytes 9220
  1084.2 18.2 copy-start.17
  1084.2 18.2 copy-start.21
  1084.2 18.2 copy-start.68
  1102.3 23.9 slice-start
  1102.3 23.9 slice-start.1
  1113.1 13.1 slice-start.2
  1150.5 22.9 all-to-all-start.6
  1155.1 12.7 slice-start.3
  1173.5 15.8 all-to-all-start.5
  1189.3 14.2 all-to-all-start.7
  1192.9 935.3 %reduce-scatter.7.cloned.1.call-start = ((), (), s32[]{:S(2)}) async-start(), calls=%async_computation.16 | async-start | bytes 9732096 | tf_op jit(solution)/shard_map/reduce_scatter | solution.py:419
  1214.6 1522.0 %reduce-scatter.15.cloned.1.call-start = ((), (), s32[]{:S(2)}) async-start(), calls=%async_computation.20 | async-start | bytes 42467328 | tf_op jit(solution)/shard_map/reduce_scatter | solution.py:428
  2013.3 11.7 copy-start.78
  2013.3 11.7 copy-start.90
  2013.3 11.7 copy-start.92
  2013.3 11.7 copy-start.94
  2013.3 11.7 copy-start.103
  2013.4 11.7 copy-start.106
  2013.4 11.7 copy-start.123
  2013.4 11.7 copy-start.126
  2013.4 11.7 copy-start.128
  2013.4 11.7 copy-start.130
  2013.4 11.7 copy-start.140
  2034.1 47.1 %copy-start.131 = (f32[16,24]{1,0:T(8,128)S(1)}, f32[16,24]{1,0:T(8,128)}, u32[]{:S(2)}) copy-start(f32[16,24]{1,0:T(8,128)} %param.29) | copy-start | bytes 4612
  2034.1 47.1 %copy-start.132 = (f32[16,24]{1,0:T(8,128)S(1)}, f32[16,24]{1,0:T(8,128)}, u32[]{:S(2)}) copy-start(f32[16,24]{1,0:T(8,128)} %param.33) | copy-start | bytes 4612
  2034.1 49.6 %copy-start.108 = (f32[512]{0:T(512)S(1)}, f32[512]{0:T(512)}, u32[]{:S(2)}) copy-start(f32[512]{0:T(512)} %copy-done.107) | copy-start | bytes 6148
  2034.1 49.6 %copy-start.11 = (f32[512,768]{1,0:T(8,128)S(1)}, f32[512,768]{1,0:T(8,128)}, u32[]{:S(2)}) copy-start(f32[512,768]{1,0:T(8,128)} %copy-done.10) | copy-start | bytes 4718596
  2083.7 44.6 %copy-start.42 = (f32[4,24,768]{2,1,0:T(8,128)S(1)}, f32[4,24,768]{2,1,0:T(8,128)}, u32[]{:S(2)}) copy-start(f32[4,24,768]{2,1,0:T(8,128)} %param.24) | copy-start | bytes 884740
  2083.8 44.5 %copy-start.58 = (f32[4,24,768]{2,1,0:T(8,128)S(1)}, f32[4,24,768]{2,1,0:T(8,128)}, u32[]{:S(2)}) copy-start(f32[4,24,768]{2,1,0:T(8,128)} %param.28) | copy-start | bytes 884740
  2083.8 44.5 %copy-start.59 = (f32[4,24,768]{2,1,0:T(8,128)S(1)}, f32[4,24,768]{2,1,0:T(8,128)}, u32[]{:S(2)}) copy-start(f32[4,24,768]{2,1,0:T(8,128)} %param.32) | copy-start | bytes 884740
  2083.8 45.8 %copy-start.150 = (f32[24]{0:T(128)S(1)}, f32[24]{0:T(128)}, u32[]{:S(2)}) copy-start(f32[24]{0:T(128)} %reshape.676) | copy-start | bytes 292
  2129.6 686.8 %copy-start.52 = (f32[4,24,768]{2,1,0:T(8,128)}, f32[4,24,768]{2,1,0:T(8,128)S(1)}, u32[]{:S(2)}) copy-start(f32[4,24,768]{2,1,0:T(8,128)S(1)} %get-tuple-element.148) | copy-start | bytes 884740
  2129.6 686.8 %copy-start.53 = (f32[4,24,768]{2,1,0:T(8,128)}, f32[4,24,768]{2,1,0:T(8,128)S(1)}, u32[]{:S(2)}) copy-start(f32[4,24,768]{2,1,0:T(8,128)S(1)} %get-tuple-element.149) | copy-start | bytes 884740
  2132.1 616.4 %copy-start.152 = (s32[2]{0:T(128)S(1)}, s32[2]{0:T(128)}, u32[]{:S(2)}) copy-start(s32[2]{0:T(128)} %copy-done.151) | copy-start | bytes 28
  2132.1 619.3 %copy-start.100 = (f32[12,12]{0,1:T(8,128)S(1)}, f32[12,12]{0,1:T(8,128)}, u32[]{:S(2)}) copy-start(f32[12,12]{0,1:T(8,128)} %convolution_bitcast_fusion.4) | copy-start | bytes 1732
  2132.2 658.9 %copy-start.81 = (f32[12,12]{0,1:T(8,128)S(1)}, f32[12,12]{0,1:T(8,128)}, u32[]{:S(2)}) copy-start(f32[12,12]{0,1:T(8,128)} %copy.254) | copy-start | bytes 1732
  2132.2 658.8 %copy-start.98 = (f32[12,12]{0,1:T(8,128)S(1)}, f32[12,12]{0,1:T(8,128)}, u32[]{:S(2)}) copy-start(f32[12,12]{0,1:T(8,128)} %copy.252) | copy-start | bytes 1732
  2132.2 658.8 %copy-start.99 = (f32[12,12]{0,1:T(8,128)S(1)}, f32[12,12]{0,1:T(8,128)}, u32[]{:S(2)}) copy-start(f32[12,12]{0,1:T(8,128)} %copy.253) | copy-start | bytes 1732
  (111 other events, 575.1 us)
Sparse Core Ops, SparseCore 0:
  11.5 365.1 all-gather.6
  380.2 63.5 all-gather.4
  445.4 440.3 all-gather.8
  949.4 343.1 reduce-scatter.12
  1295.3 343.1 reduce-scatter.10
  1640.9 343.1 reduce-scatter.8
  1991.0 137.2 reduce-scatter.6
  2132.1 604.3 reduce-scatter.14
where the time goes:
time: 2830 us; the launch traced here: 2820 us
  waiting for transfers between devices  2150 us (76%)
  matrix products  263 us (9%)
  blocking collectives  138 us (5%)
  other arithmetic  117 us (4%)
  local copies, waits for them, and re-layouts  109 us (4%)
  starting transfers between devices  29.4 us (1%)
    reduce_scatter x1, waiting for transfers between devices, shards(): lax.psum_scatter(expert_local, ('dp', 'seq'), scatter_dimension=2, tiled=...  604 us
    all_gather x1, waiting for transfers between devices, shards(): lax.all_gather(expert_master.astype(jnp.bfloat16), ('dp', 'seq'), axis=2,...  364 us
    reduce_scatter x1, waiting for transfers between devices, shards(): lax.psum_scatter(dweight_up, 'shard', scatter_dimension=0, tiled=True)  346 us
    reduce_scatter x1, waiting for transfers between devices, shards(): lax.psum_scatter(dweight_gate, 'shard', scatter_dimension=0, tiled=True)  346 us
    all_gather x1, waiting for transfers between devices, shards(): expert_use = lax.all_gather(expert_rows, 'shard', axis=0, tiled=True)  326 us
    reduce_scatter x1, waiting for transfers between devices, shards(): lax.psum_scatter(dweight_down, 'shard', scatter_dimension=0, tiled=True)  78 us
  transfers between devices with their start and end apart: 15, of which 12 were waited for; matrix products, arithmetic and copies ran while one was open for 13% of the time, Pallas kernels for 0%

commit v1 on v0

v1 whole, which is shorter than its diff:
```python
import jax
import jax.numpy as jnp
from jax import lax
from jax.sharding import PartitionSpec as P

HEADS = 12
HDIM = 64
NFFN = 8
TOP = 2
STEP = 4
NEXP = 12

beta_one = 0.9
beta_two = 0.999
adam_eps = 1e-06
weight_decay = 0.01
learn_rate = 0.25
norm_eps = 1e-06
rope_base = 10000.0

bf16 = jnp.bfloat16
f32 = jnp.float32


def exact_dot(left, right):
    return jnp.dot(left, right, precision=lax.Precision.HIGHEST, preferred_element_type=f32)


def dot_nn(left, right):
    return lax.dot_general(left, right, (((1,), (0,)), ((), ())), preferred_element_type=f32)


def dot_nt(left, right):
    return lax.dot_general(left, right, (((1,), (1,)), ((), ())), preferred_element_type=f32)


def dot_tn(left, right):
    return lax.dot_general(left, right, (((0,), (0,)), ((), ())), preferred_element_type=f32)


def rotary_tables(positions):
    freqs = rope_base ** (-jnp.arange(0, HDIM, 2).astype(f32) / HDIM)
    angles = positions[:, None] * freqs[None, :]
    cosine = jnp.concatenate([jnp.cos(angles), jnp.cos(angles)], axis=-1)
    sine_table = jnp.concatenate([jnp.sin(angles), jnp.sin(angles)], axis=-1)
    return (cosine, sine_table)


def rotate(values, cosine, sine_table):
    half_size = values.shape[-1] // 2
    turned = jnp.concatenate([-values[..., half_size:], values[..., :half_size]], axis=-1)
    return values * cosine[:, None, :] + turned * sine_table[:, None, :]


def rotate_back(values, cosine, sine_table):
    half_size = values.shape[-1] // 2
    scaled = values * sine_table[:, None, :]
    turned = jnp.concatenate([scaled[..., half_size:], -scaled[..., :half_size]], axis=-1)
    return values * cosine[:, None, :] + turned


def softmax_rows(logits):
    row_top = jnp.max(logits, axis=-1, keepdims=True)
    expd_values = jnp.exp(logits - row_top)
    return expd_values / jnp.sum(expd_values, axis=-1, keepdims=True)


def moments(weight, first, second, grad):
    first_new = beta_one * first + (1.0 - beta_one) * grad
    second_new = beta_two * second + (1.0 - beta_two) * grad * grad
    step_value = (
        first_new
        / (1.0 - beta_one**STEP)
        / (jnp.sqrt(second_new / (1.0 - beta_two**STEP)) + adam_eps)
        + weight_decay * weight
    )
    return (first_new, second_new, step_value)


def swap_seq(value):
    return lax.ppermute(value, "seq", [(0, 1), (1, 0)])


def in_order(own, other, which, axis):
    low = jnp.where(which == 0, own, other)
    high = jnp.where(which == 0, other, own)
    return jnp.concatenate([low, high], axis=axis)


def pairs_dp(count, step):
    return [(i, (i + step) % count) for i in range(count)]


def pairs_x(count, step):
    return [(i, (i + 2 * step) % count) for i in range(count)]


def pairs_core(count):
    return [(i, i ^ 1) for i in range(count)]


def gather_steps(value, axis_name, pairs_of, place, count):
    out = jnp.zeros((count,) + value.shape, value.dtype)
    out = lax.dynamic_update_index_in_dim(out, value, place, 0)
    for step in range(1, count):
        got = lax.ppermute(value, axis_name, pairs_of(step))
        out = lax.dynamic_update_index_in_dim(out, got, (place - step) % count, 0)
    return out


def scatter_steps(value, axis_name, pairs_of, place, count):
    total = lax.dynamic_index_in_dim(value, place, 0, keepdims=False).astype(f32)
    for step in range(1, count):
        block = lax.dynamic_index_in_dim(value, (place + step) % count, 0, keepdims=False)
        total = total + lax.ppermute(block, axis_name, pairs_of(step)).astype(f32)
    return total


def sum_everywhere(value, sizes):
    for axis_name in ("shard", "seq", "dp"):
        bit = 1
        while bit < sizes[axis_name]:
            value = value + lax.ppermute(
                value, axis_name, [(i, i ^ bit) for i in range(sizes[axis_name])]
            )
            bit *= 2
    return value


def causal_blocks(seq_length):
    block_rows = min(512, seq_length)
    return [(start, start + block_rows) for start in range(0, seq_length, block_rows)]


def attention_forward(query, key, value):
    length = query.shape[1]
    outs, sums = [], []
    for start, end in causal_blocks(length):
        raw = jnp.einsum(
            "hqd,hkd->hqk", query[:, start:end], key[:, :end], preferred_element_type=f32
        ) * (HDIM**-0.5)
        causal = (start + jnp.arange(end - start))[:, None] >= jnp.arange(end)[None, :]
        scores = jnp.where(causal[None], raw, -1e30)
        row_top = jnp.max(scores, axis=-1, keepdims=True)
        row_total = jnp.sum(jnp.exp(scores - row_top), axis=-1, keepdims=True)
        log_total = row_top + jnp.log(row_total)
        soft = jnp.exp(scores - log_total).astype(bf16)
        outs.append(jnp.einsum("hqk,hkd->hqd", soft, value[:, :end], preferred_element_type=f32))
        sums.append(log_total)
    return jnp.concatenate(outs, axis=1), jnp.concatenate(sums, axis=1)


def attention_backward(query, key, value, sums, dout):
    heads, length, width = query.shape
    dqs = []
    dkey = jnp.zeros((heads, length, width), f32)
    dvalue = jnp.zeros((heads, length, width), f32)
    for start, end in causal_blocks(length):
        raw = jnp.einsum(
            "hqd,hkd->hqk", query[:, start:end], key[:, :end], preferred_element_type=f32
        ) * (HDIM**-0.5)
        causal = (start + jnp.arange(end - start))[:, None] >= jnp.arange(end)[None, :]
        scores = jnp.where(causal[None], raw, -1e30)
        soft = jnp.exp(scores - sums[:, start:end])
        dsoft = jnp.einsum(
            "hqd,hkd->hqk", dout[:, start:end], value[:, :end], preferred_element_type=f32
        )
        delta = jnp.sum(soft * dsoft, axis=-1, keepdims=True)
        dscores = (soft * (dsoft - delta)).astype(bf16)
        dqs.append(
            jnp.einsum("hqk,hkd->hqd", dscores, key[:, :end], preferred_element_type=f32)
            * (HDIM**-0.5)
        )
        dkey = dkey.at[:, :end].add(
            jnp.einsum("hqk,hqd->hkd", dscores, query[:, start:end], preferred_element_type=f32)
            * (HDIM**-0.5)
        )
        dvalue = dvalue.at[:, :end].add(
            jnp.einsum(
                "hqk,hqd->hkd", soft.astype(bf16), dout[:, start:end], preferred_element_type=f32
            )
        )
    return jnp.concatenate(dqs, axis=1), dkey, dvalue


def heads_first(value, heads):
    length = value.shape[0]
    return value.reshape(length, heads, HDIM).transpose(1, 0, 2)


def heads_last(value):
    heads, length, width = value.shape
    return value.transpose(1, 0, 2).reshape(length, heads * width)


def make_shards(sizes):
    n_dp, n_seq, n_shard = sizes["dp"], sizes["seq"], sizes["shard"]
    n_x = n_shard // 2

    def shards(
        tokens,
        cotangent,
        previous_logits,
        routes,
        priority,
        attention_master,
        vector_master,
        expert_master,
        mixing_master,
        attention_first,
        vector_first,
        expert_first,
        mixing_first,
        attention_second,
        vector_second,
        expert_second,
        mixing_second,
    ):
        z, y, s = lax.axis_index("dp"), lax.axis_index("seq"), lax.axis_index("shard")
        x_place, core = s // 2, s % 2
        row_count, model_width = tokens.shape[1], tokens.shape[2]
        half_width = model_width // 2
        local_experts = expert_master.shape[0]
        spread = local_experts == n_seq
        ep_axes = ("seq", "shard") if spread else ("shard",)
        own_rows = attention_master.shape[1]

        expert_low = expert_master.astype(bf16)
        if spread:
            kept_low = lax.dynamic_index_in_dim(expert_low, y, 0, keepdims=False)
            sent_low = lax.dynamic_index_in_dim(expert_low, 1 - y, 0, keepdims=False)
            rows_low = in_order(kept_low, swap_seq(sent_low), y, 1)
            expert_use = lax.all_gather(rows_low, "dp", axis=1, tiled=True)
        else:
            expert_use = lax.all_gather(expert_low[0], ("dp", "seq"), axis=1, tiled=True)

        attention_low = attention_master.astype(bf16)
        vector_low = vector_master.astype(bf16).T
        vector_pad = 128 - vector_low.shape[1]

        def weight_pack(which):
            columns = lax.dynamic_slice_in_dim(attention_low[:3], which * half_width, half_width, 2)
            return jnp.concatenate(
                [columns[0], columns[1], columns[2], attention_low[3], jnp.pad(vector_low, ((0, 0), (0, vector_pad)))],
                axis=1,
            )

        packed = in_order(
            weight_pack(y)[None], swap_seq(weight_pack(1 - y))[None], y, 0
        )
        packed = gather_steps(packed, "dp", lambda k: pairs_dp(n_dp, k), z, n_dp)
        packed = gather_steps(packed, "shard", lambda k: pairs_x(n_shard, k), x_place, n_x)
        packed = in_order(
            packed[None], lax.ppermute(packed, "shard", pairs_core(n_shard))[None], core, 0
        )
        packed = packed.transpose(2, 3, 1, 0, 4, 5).reshape(model_width, -1)
        qkv_weight = packed[:, : 3 * half_width]
        out_weight = packed[:, 3 * half_width : 3 * half_width + model_width]
        vector_all = packed[:, 3 * half_width + model_width :][:, : 4 + NEXP].T

        route_rows = routes[0]
        order = priority[0, 0]
        capacity = 9 * row_count * TOP // (8 * NEXP)
        expert_ids = jnp.arange(NEXP)[None, :]
        hit_each = [route_rows[:, j : j + 1] == expert_ids for j in range(TOP)]
        hits = (hit_each[0] | hit_each[1]).astype(bf16)
        before = (order[None, :] < order[:, None]).astype(bf16)
        counts = dot_nn(before, hits)
        kept, dispatch = [], []
        block_ids = jnp.arange(NFFN * capacity)[None, :]
        for j in range(TOP):
            slot = jnp.sum(jnp.where(hit_each[j], counts, 0.0), axis=1, keepdims=True).astype(
                jnp.int32
            )
            route = route_rows[:, j : j + 1]
            keep = (route < NFFN) & (slot < capacity)
            block = (route % n_seq) * n_shard + route // n_seq if spread else route
            kept.append(keep)
            dispatch.append(
                ((block_ids == block * capacity + slot) & keep).astype(bf16)
            )
        dispatch_both = dispatch[0] + dispatch[1]

        upstream = cotangent[0].astype(f32)
        dout_rows = dot_tn(dispatch_both, cotangent[0]).astype(bf16)
        dout_rows = lax.all_to_all(
            dout_rows.reshape(NFFN, capacity, model_width), ep_axes, 0, 0, tiled=True
        ).reshape(NFFN * capacity, model_width)

        tokens_other = swap_seq(tokens[0])
        tokens_all = in_order(tokens[0], tokens_other, y, 0).astype(f32)
        seq_length = tokens_all.shape[0]
        local_heads = HEADS // n_seq
        gain_one = vector_all[0].astype(f32)[None, :]
        gain_two = vector_all[1].astype(f32)[None, :]
        rho_all = lax.rsqrt(jnp.mean(tokens_all * tokens_all, axis=-1, keepdims=True) + norm_eps)
        normed = (tokens_all * rho_all * gain_one).astype(bf16)
        cosine, sine_table = rotary_tables(jnp.arange(seq_length).astype(f32))
        qkv = dot_nn(normed, qkv_weight)
        query = rotate(qkv[:, :half_width].reshape(seq_length, local_heads, HDIM), cosine, sine_table)
        key = rotate(
            qkv[:, half_width : 2 * half_width].reshape(seq_length, local_heads, HDIM),
            cosine,
            sine_table,
        )
        query = query.astype(bf16).transpose(1, 0, 2)
        key = key.astype(bf16).transpose(1, 0, 2)
        value = heads_first(qkv[:, 2 * half_width :].astype(bf16), local_heads)
        mixed, log_sums = attention_forward(query, key, value)
        mixed = heads_last(mixed.astype(bf16))
        mixed_keep = lax.dynamic_slice_in_dim(mixed, y * row_count, row_count, 0)
        mixed_send = lax.dynamic_slice_in_dim(mixed, (1 - y) * row_count, row_count, 0)
        mixed_tokens = in_order(mixed_keep, swap_seq(mixed_send), y, 1)

        inputs = tokens[0].astype(f32)
        resid = inputs + dot_nn(mixed_tokens, out_weight)
        rho_two = lax.rsqrt(jnp.mean(resid * resid, axis=-1, keepdims=True) + norm_eps)
        normed_two = resid * rho_two * gain_two
        expert_in = normed_two.astype(bf16)
        router = vector_all[4:]
        previous = previous_logits[0]
        logits = dot_nt(expert_in, router) + exact_dot(previous, mixing_master)
        gates = softmax_rows(logits)
        picked = [
            jnp.sum(jnp.where(hit_each[j], gates, 0.0), axis=1, keepdims=True) for j in range(TOP)
        ]

        taken = dot_tn(dispatch_both, expert_in).astype(bf16)
        taken = lax.all_to_all(
            taken.reshape(NFFN, capacity, model_width), ep_axes, 0, 0, tiled=True
        ).reshape(NFFN * capacity, model_width)
        gate_rows = (
            exact_dot(dispatch[0].astype(f32).T, picked[0])
            + exact_dot(dispatch[1].astype(f32).T, picked[1])
        ).reshape(NFFN, capacity)
        gate_rows = lax.all_to_all(gate_rows, ep_axes, 0, 0, tiled=True).reshape(
            NFFN * capacity, 1
        )

        gate_pre = dot_nn(taken, expert_use[0])
        up_pre = dot_nn(taken, expert_use[1])
        sig = jax.nn.sigmoid(gate_pre)
        hidden = (gate_pre * sig * up_pre).astype(bf16)
        result = dot_nt(hidden, expert_use[2]).astype(bf16)
        result = lax.all_to_all(
            result.reshape(NFFN, capacity, model_width), ep_axes, 0, 0, tiled=True
        ).reshape(NFFN * capacity, model_width)
        dresult = (gate_rows * dout_rows.astype(f32)).astype(bf16)
        dhidden = dot_nn(dresult, expert_use[2])
        dgate_low = (dhidden * up_pre * sig * (1.0 + gate_pre * (1.0 - sig))).astype(bf16)
        dup_low = (dhidden * gate_pre * sig).astype(bf16)
        dtaken = (dot_nt(dgate_low, expert_use[0]) + dot_nt(dup_low, expert_use[1])).astype(bf16)
        dtaken = lax.all_to_all(
            dtaken.reshape(NFFN, capacity, model_width), ep_axes, 0, 0, tiled=True
        ).reshape(NFFN * capacity, model_width)
        dexpert = jnp.stack(
            [
                dot_tn(taken, dgate_low).astype(bf16),
                dot_tn(taken, dup_low).astype(bf16),
                dot_tn(dresult, hidden).astype(bf16),
            ]
        )
        if spread:
            dexpert = lax.psum_scatter(dexpert, "dp", scatter_dimension=1, tiled=True)
            dexpert = dexpert.reshape(3, n_seq, -1, dexpert.shape[2])
            kept_part = lax.dynamic_index_in_dim(dexpert, y, 1, keepdims=False)
            sent_part = lax.dynamic_index_in_dim(dexpert, 1 - y, 1, keepdims=False)
            expert_sum = in_order(kept_part[None], swap_seq(sent_part)[None], y, 0)
        else:
            expert_sum = lax.psum_scatter(
                dexpert, ("dp", "seq"), scatter_dimension=1, tiled=True
            )[None]
        expert_sum = expert_sum.astype(f32)

        consts = vector_all[2:4].astype(f32)
        chosen = []
        for j in range(TOP):
            route = route_rows[:, j : j + 1]
            entry = dot_nn(dispatch[j], result) + jnp.where(route == NFFN + 1, normed_two, 0.0)
            entry = entry + jnp.where(route == NFFN + 2, consts[0:1], 0.0)
            entry = entry + jnp.where(route == NFFN + 3, consts[1:2], 0.0)
            chosen.append(entry)
        block_output = (resid + picked[0] * chosen[0] + picked[1] * chosen[1]).astype(bf16)
        dgates = jnp.zeros_like(gates)
        dnormed_two = dot_nn(dispatch_both, dtaken)
        dconst_one = jnp.zeros((1, model_width), f32)
        dconst_two = jnp.zeros((1, model_width), f32)
        for j in range(TOP):
            route = route_rows[:, j : j + 1]
            dpicked = jnp.sum(upstream * chosen[j], axis=-1, keepdims=True)
            dgates = dgates + jnp.where(hit_each[j], dpicked, 0.0)
            dvalue = picked[j] * upstream
            dnormed_two = dnormed_two + jnp.where(route == NFFN + 1, dvalue, 0.0)
            dconst_one = dconst_one + jnp.sum(
                jnp.where(route == NFFN + 2, dvalue, 0.0), axis=0, keepdims=True
            )
            dconst_two = dconst_two + jnp.sum(
                jnp.where(route == NFFN + 3, dvalue, 0.0), axis=0, keepdims=True
            )
        dlogits = gates * (dgates - jnp.sum(gates * dgates, axis=-1, keepdims=True))
        dnormed_two = dnormed_two + exact_dot(dlogits, router.astype(f32))
        drouter = exact_dot(dlogits.T, expert_in.astype(f32))
        dmixing = exact_dot(previous.T, dlogits)
        scaled_two = dnormed_two * gain_two
        dresid = upstream + (
            rho_two * scaled_two
            - resid * (rho_two * rho_two * rho_two) * jnp.mean(resid * scaled_two, -1, keepdims=True)
        )
        dgain_two = jnp.sum(dnormed_two * resid * rho_two, axis=0, keepdims=True)
        dbranch_low = dresid.astype(bf16)
        dweight_out = dot_tn(mixed_tokens, dbranch_low)
        dout_sum = lax.psum_scatter(
            dweight_out, ("dp", "seq", "shard"), scatter_dimension=0, tiled=True
        )
        dmixed = dot_nt(dbranch_low, out_weight).astype(bf16)
        dmixed_keep = lax.dynamic_slice_in_dim(dmixed, y * half_width, half_width, 1)
        dmixed_send = lax.dynamic_slice_in_dim(dmixed, (1 - y) * half_width, half_width, 1)
        dmixed_heads = heads_first(in_order(dmixed_keep, swap_seq(dmixed_send), y, 0), local_heads)

        dquery, dkey, dvalue_heads = attention_backward(query, key, value, log_sums, dmixed_heads)
        dquery = dquery.astype(bf16).astype(f32).transpose(1, 0, 2)
        dkey = dkey.astype(bf16).astype(f32).transpose(1, 0, 2)
        dqkv = jnp.concatenate(
            [
                rotate_back(dquery, cosine, sine_table).astype(bf16).reshape(seq_length, -1),
                rotate_back(dkey, cosine, sine_table).astype(bf16).reshape(seq_length, -1),
                heads_last(dvalue_heads.astype(bf16)),
            ],
            axis=1,
        )
        dnormed_all = dot_nt(dqkv, qkv_weight)
        dnormed_keep = lax.dynamic_slice_in_dim(dnormed_all, y * row_count, row_count, 0)
        dnormed_send = lax.dynamic_slice_in_dim(dnormed_all, (1 - y) * row_count, row_count, 0)
        dnormed = dnormed_keep + swap_seq(dnormed_send.astype(bf16)).astype(f32)
        rho_one = lax.rsqrt(jnp.mean(inputs * inputs, axis=-1, keepdims=True) + norm_eps)
        scaled_one = dnormed * gain_one
        input_gradient = dresid + (
            rho_one * scaled_one
            - inputs * (rho_one * rho_one * rho_one) * jnp.mean(inputs * scaled_one, -1, keepdims=True)
        )
        dgain_one = jnp.sum(dnormed * inputs * rho_one, axis=0, keepdims=True)

        dweight_qkv = dot_tn(normed, dqkv)
        dvector = jnp.concatenate([dgain_one, dgain_two, dconst_one, dconst_two, drouter], axis=0)
        dpack = jnp.concatenate(
            [dweight_qkv, jnp.pad(dvector.T, ((0, 0), (0, vector_pad)))], axis=1
        )
        columns = dpack.shape[1]
        dpack = dpack.reshape(n_dp, n_seq, n_x, 2, own_rows, columns).transpose(3, 2, 0, 1, 4, 5)
        core_keep = lax.dynamic_index_in_dim(dpack, core, 0, keepdims=False)
        core_send = lax.dynamic_index_in_dim(dpack, 1 - core, 0, keepdims=False)
        dpack = core_keep + lax.ppermute(core_send, "shard", pairs_core(n_shard))
        dpack = scatter_steps(
            dpack.astype(bf16), "shard", lambda k: pairs_x(n_shard, k), x_place, n_x
        )
        dpack = scatter_steps(dpack.astype(bf16), "dp", lambda k: pairs_dp(n_dp, k), z, n_dp)
        part_keep = lax.dynamic_index_in_dim(dpack, y, 0, keepdims=False)
        part_send = lax.dynamic_index_in_dim(dpack, 1 - y, 0, keepdims=False)
        part_got = swap_seq(part_send)
        qkv_both = in_order(
            part_keep[:, : 3 * half_width].reshape(own_rows, 3, half_width),
            part_got[:, : 3 * half_width].reshape(own_rows, 3, half_width),
            y,
            2,
        ).transpose(1, 0, 2)
        attention_sum = jnp.concatenate([qkv_both, dout_sum[None]], axis=0)
        vector_sum = (part_keep + part_got)[:, 3 * half_width : 3 * half_width + 4 + NEXP].T

        attention_m, attention_s, attention_u = moments(
            attention_master, attention_first, attention_second, attention_sum
        )
        vector_m, vector_s, vector_u = moments(
            vector_master, vector_first, vector_second, vector_sum
        )
        expert_m, expert_s, expert_u = moments(
            expert_master, expert_first, expert_second, expert_sum
        )

        def squares(attention_x, vector_x, expert_x):
            vector_parts = jnp.sum(vector_x * vector_x, axis=1)
            expert_parts = lax.dynamic_update_slice_in_dim(
                jnp.zeros((NFFN * 3,), f32),
                jnp.sum(expert_x * expert_x, axis=(2, 3)).reshape(-1),
                s * local_experts * 3,
                0,
            )
            return jnp.concatenate(
                [
                    jnp.sum(attention_x * attention_x, axis=(1, 2)),
                    vector_parts[0:2],
                    jnp.sum(vector_parts[2:4])[None],
                    jnp.sum(vector_parts[4:])[None],
                    expert_parts,
                ]
            )

        count = 8 + 3 * NFFN
        small = jnp.concatenate(
            [
                squares(attention_master, vector_master, expert_master),
                squares(attention_u, vector_u, expert_u),
                dmixing.reshape(-1),
            ]
        )
        used = small.shape[0]
        small = jnp.pad(small, (0, -used % 128)).reshape(-1, 128)
        small = sum_everywhere(small, sizes).reshape(-1)
        summed_squares = small[: 2 * count].reshape(2, count)
        mixing_grad = small[2 * count : used].reshape(NEXP, NEXP)
        mixing_m, mixing_s, mixing_u = moments(
            mixing_master, mixing_first, mixing_second, mixing_grad
        )
        mixing_squares = jnp.stack(
            [jnp.sum(mixing_master * mixing_master), jnp.sum(mixing_u * mixing_u)]
        )
        tensor_norms = jnp.sqrt(jnp.concatenate([summed_squares, mixing_squares[:, None]], axis=1))
        ratios = learn_rate * (tensor_norms[0] / (tensor_norms[1] + norm_eps))
        vector_ratio = jnp.concatenate(
            [
                ratios[4:6],
                jnp.broadcast_to(ratios[6:7], (2,)),
                jnp.broadcast_to(ratios[7:8], (NEXP,)),
            ]
        )[:, None]
        expert_ratio = lax.dynamic_slice_in_dim(
            ratios[8:count].reshape(NFFN, 3), s * local_experts, local_experts, 0
        )[:, :, None, None]
        return (
            block_output[None],
            input_gradient[None],
            attention_master - ratios[0:4][:, None, None] * attention_u,
            vector_master - vector_ratio * vector_u,
            expert_master - expert_ratio * expert_u,
            mixing_master - ratios[count] * mixing_u,
            attention_m,
            vector_m,
            expert_m,
            mixing_m,
            attention_s,
            vector_s,
            expert_s,
            mixing_s,
            tensor_norms,
        )

    return shards


def solution(mesh):
    tokens_spec = P(("dp", "shard"), "seq", None)
    attention_spec = P(None, ("dp", "seq", "shard"), None)
    vector_spec = P(None, ("dp", "seq", "shard"))
    expert_spec = P("shard", None, ("dp", "seq"), None)
    weights = (attention_spec, vector_spec, expert_spec, P())
    return jax.shard_map(
        make_shards(dict(mesh.shape)),
        mesh=mesh,
        in_specs=(tokens_spec,) * 5 + weights * 3,
        out_specs=(tokens_spec,) * 2 + weights * 3 + (P(),),
        check_vma=False,
    )
```

time: 2830 us -> 615 us (0.22)
  waiting for transfers between devices: 2150 us -> 250 us
  blocking collectives: 138 us -> 0 us
  matrix products: 263 us -> 134 us
  local copies, waits for them, and re-layouts: 109 us -> 47.9 us
    reduce_scatter x5 -> x2, waiting for transfers between devices: 1420 us -> 78 us  [the longest x1 78 us: shards(): lax.psum_scatter(dweight_out, ('dp', 'seq', 'shard'), scatter_dimension=0...]
    all_gather x3 -> x1, waiting for transfers between devices: 714 us -> 65.3 us  [shards(): expert_use = lax.all_gather(rows_low, 'dp', axis=1, tiled=True)]
    dot_general x37 -> x34, matrix products: 259 us -> 130 us  [the longest x9 36.4 us: dot_nn(): lax.dot_general(left, right, (((1,), (0,)), ((), ())), preferred_element_...]
    ppermute x0 -> x23, waiting for transfers between devices: none -> 86.1 us  [the longest x8 44.3 us: swap_seq(): return lax.ppermute(value, 'seq', [(0, 1), (1, 0)])]
    unnamed x1 -> x0, blocking collectives: 43.1 us -> none
    all_gather x1 -> x0, blocking collectives: 41.1 us -> none  [shards(): lax.all_gather(vector_master.astype(jnp.bfloat16), ('dp', 'seq', 'shard')...]
    psum x1 -> x0, blocking collectives: 39.5 us -> none  [shards(): lax.psum((partial_squares, dmixing_local), ('dp', 'seq', 'shard'))]
    ppermute x0 -> x23, starting transfers between devices: none -> 34.1 us  [the longest x8 12 us: swap_seq(): return lax.ppermute(value, 'seq', [(0, 1), (1, 0)])]
  transfers between devices with their start and end apart: 15 -> 31, of which waited for: 12 -> 20; matrix products, arithmetic and copies ran while one was open for 13% -> 36% of each run, Pallas kernels for 0% -> 0%
where the time goes in v1:
time: 615 us; the launch traced here: 605 us
  waiting for transfers between devices  250 us (41%)
  matrix products  134 us (22%)
  other arithmetic  101 us (16%)
  starting transfers between devices  55.4 us (9%)
  local copies, waits for them, and re-layouts  47.9 us (8%)
  between operations  16.5 us (3%)
    reduce_scatter x1, waiting for transfers between devices, shards(): lax.psum_scatter(dweight_out, ('dp', 'seq', 'shard'), scatter_dimension=0...  78 us
    all_gather x1, waiting for transfers between devices, shards(): expert_use = lax.all_gather(rows_low, 'dp', axis=1, tiled=True)  65.3 us
    ppermute x8, waiting for transfers between devices, swap_seq(): return lax.ppermute(value, 'seq', [(0, 1), (1, 0)])  44.3 us
    dot_general x9, matrix products, dot_nn(): lax.dot_general(left, right, (((1,), (0,)), ((), ())), preferred_element_...  36.4 us
    dot_general x7, matrix products, dot_tn(): lax.dot_general(left, right, (((0,), (0,)), ((), ())), preferred_element_...  28.4 us
    dot_general x6, matrix products, dot_nt(): lax.dot_general(left, right, (((1,), (1,)), ((), ())), preferred_element_...  20.2 us
    ppermute x4, waiting for transfers between devices, scatter_steps(): total = total + lax.ppermute(block, axis_name, pairs_of(step)).astype(f32)  19.3 us
    unnamed x323, local copies, waits for them, and re-layouts  15 us
  transfers between devices with their start and end apart: 31, of which 20 were waited for; matrix products, arithmetic and copies ran while one was open for 36% of the time, Pallas kernels for 0%

profile of v1, /device:TPU:0, one launch (start us, length us, event | category | flops | bytes accessed | tf_op | source)
XLA Modules:
  0.0 605.4 jit_solution(3026136337245011733)
XLA Ops:
  9.1 3.0 collective-permute-start.1
  12.3 2.7 convert_element_type.267
  19.7 2.6 collective-permute-start.3
  23.7 4.1 collective-permute-done.2
  27.9 6.4 %collective-permute-done.3 = bf16[2,24,2048]{2,1,0:T(8,128)(2,1)S(1)} collective-permute-done((bf16[2,24,2048]{2,1,0:T(8,128)(2,1)S(1)}, bf16[2,24,2048]{2,1,0:T(8,128)(2,1)S(1)}, u32[]{:S(2)}, u32[]{:S(2)}) %collective-permute-start.3) | collective-permute-done | bytes 196640 | tf_op jit(solution)/shard_map/ppermute | solution.py:106
  38.2 19.0 %collective-permute-done.8 = bf16[3,96,2048]{2,1,0:T(8,128)(2,1)} collective-permute-done((bf16[3,96,2048]{2,1,0:T(8,128)(2,1)}, bf16[3,96,2048]{2,1,0:T(8,128)(2,1)}, u32[]{:S(2)}, u32[]{:S(2)}) %collective-permute-start.8) | collective-permute-done | bytes 1179680 | tf_op jit(solution)/shard_map/ppermute | solution.py:81
  66.8 2.5 select_bitcast_fusion.1
  71.3 2.3 fusion.70
  77.1 3.2 fusion.179
  84.8 2.4 fusion
  87.2 4.1 exponential_reduce_fusion
  93.2 2.6 exponential_reduce_fusion.1
  97.6 7.8 %convolution_convert_fusion.7 = bf16[6,512,64]{1,2,0:T(8,128)(2,1)S(1)} fusion(bf16[6,1024,64]{1,2,0:T(8,128)(2,1)S(1)} %bitcast.302, f32[6,512,1024]{2,1,0:T(8,128)} %copy-done, f32[6,512]{1,0:T(8,128)S(1)} %log_add_fusion, pred[512,1024]{1,0:T(8,128)(4,1)S(1)} %copy-done.5), kind=kOutput, calls=%fused_computation.152 | convolution fusion | flops 415432704 | bytes 14299136 | tf_op jit(solution)/shard_map/hqk,hkd->hqd/dot_general | solution.py:148
  109.1 8.5 %collective-permute-done.7 = bf16[512,384]{1,0:T(8,128)(2,1)} collective-permute-done((bf16[512,384]{1,0:T(8,128)(2,1)S(1)}, bf16[512,384]{1,0:T(8,128)(2,1)}, u32[]{:S(2)}, u32[]{:S(2)}) %collective-permute-start.7) | collective-permute-done | bytes 393248 | tf_op jit(solution)/shard_map/ppermute | solution.py:81
  127.0 4.0 all-to-all-start.2
  133.3 2.3 all-to-all-done.2
  136.2 3.6 all-to-all-start.3
  141.8 2.9 convolution_convert_fusion.4
  146.5 9.9 %all-to-all-done.3 = bf16[8,96,768]{2,1,0:T(8,128)(2,1)S(1)} async-done(((bf16[8,96,768]{2,1,0:T(8,128)(2,1)}), bf16[8,96,768]{2,1,0:T(8,128)(2,1)S(1)}, u32[]{:S(2)}, u32[]{:S(2)}) %all-to-all-start.3) | async-done | bytes 1179680 | tf_op jit(solution)/shard_map/all_to_all | solution.py:286
  156.5 4.3 all-to-all-start
  163.3 65.3 %all-gather.2.cloned.1.call-done = bf16[3,768,2048]{2,1,0:T(8,128)(2,1)} async-done(((bf16[3,192,2048]{2,1,0:T(8,128)(2,1)}), bf16[3,768,2048]{2,1,0:T(8,128)(2,1)}) %all-gather.2.cloned.1.call-update) | async-done | bytes 9437200 | tf_op jit(solution)/shard_map/all_gather | solution.py:233
  228.6 7.4 %fusion.16 = f32[768,2048]{1,0:T(8,128)} fusion(bf16[768,768]{1,0:T(8,128)(2,1)} %bitcast.325, bf16[3,768,2048]{2,1,0:T(8,128)(2,1)} %all-gather.2.cloned.1.call-done), kind=kOutput, calls=%fused_computation.58 | convolution fusion | flops 2415919104 | bytes 10616832 | tf_op jit(solution)/shard_map/dot_general | solution.py:30
  236.1 5.0 fusion.15
  241.1 9.1 %multiply_convert_fusion.3 = (bf16[768,2048]{1,0:T(8,128)(2,1)}, bf16[768,2048]{1,0:T(8,128)(2,1)S(1)}, bf16[768,2048]{1,0:T(8,128)(2,1)}) fusion(f32[768,2048]{1,0:T(8,128)} %fusion.16, f32[768,2048]{1,0:T(8,128)S(1)} %fusion.15, bf16[768,768]{1,0:T(8,128)(2,1)} %bitcast.44, bf16[3,768,2048]{2,1,0:T(8,128)(2,1)S(1)} %copy-done.140), kind=kOutput, calls=%fused_computation.12 | convolution fusion | flops 2441084928 | bytes 26345472 | tf_op jit(solution)/shard_map/dot_general | solution.py:30
  250.2 3.7 fusion.72
  253.9 4.4 all-to-all-start.1
  258.5 4.9 fusion.11
  263.5 4.3 fusion.10
  267.8 4.2 fusion.9
  272.0 4.2 pad_maximum_fusion
  276.2 5.6 fusion.14
  281.9 5.6 add_convert_fusion
  287.5 4.4 all-to-all-start.4
  292.6 2.5 select_add_fusion
  295.2 5.0 fusion.38
  300.3 8.4 %all-to-all-done.4 = bf16[8,96,768]{2,1,0:T(8,128)(2,1)} async-done(((bf16[8,96,768]{2,1,0:T(8,128)(2,1)}), bf16[8,96,768]{2,1,0:T(8,128)(2,1)}, u32[]{:S(2)}, u32[]{:S(2)}) %all-to-all-start.4) | async-done | bytes 1179680 | tf_op jit(solution)/shard_map/all_to_all | solution.py:353
  308.8 2.5 fusion.107
  311.3 2.6 multiply_reduce_fusion.4
  314.4 2.7 convolution_convert_fusion.5
  318.5 6.5 %collective-permute-done.9 = bf16[512,384]{1,0:T(8,128)(2,1)S(1)} collective-permute-done((bf16[512,384]{1,0:T(8,128)(2,1)S(1)}, bf16[512,384]{1,0:T(8,128)(2,1)S(1)}, u32[]{:S(2)}, u32[]{:S(2)}) %collective-permute-start.9) | collective-permute-done | bytes 393248 | tf_op jit(solution)/shard_map/ppermute | solution.py:81
  325.7 6.9 %multiply_reduce_fusion.1 = (f32[6,512]{1,0:T(8,128)}, f32[6,512,512]{1,2,0:T(8,128)}) fusion(f32[6,512,512]{1,2,0:T(8,128)} %copy-done.1, f32[6,512]{1,0:T(8,128)S(1)} %log_add_fusion.1, pred[512,512]{0,1:T(8,128)(4,1)S(1)} %copy-done.27, bf16[6,1024,64]{1,2,0:T(8,128)(2,1)S(1)} %bitcast.303, bf16[6,1024,64]{1,2,0:T(8,128)(2,1)S(1)} %bitcast.311), kind=kOutput, calls=%fused_computation.10 | convolution fusion | flops 209187840 | bytes 13660160 | tf_op jit(solution)/shard_map/hqd,hkd->hqk/dot_general | solution.py:165
  332.6 4.9 multiply_convert_fusion.1
  337.5 2.5 fusion.74
  340.0 3.1 convolution_multiply_fusion.1
  343.2 7.5 %multiply_reduce_fusion = (f32[6,512]{1,0:T(8,128)S(1)}, f32[6,512,1024]{2,1,0:T(8,128)}) fusion(f32[6,512,1024]{2,1,0:T(8,128)S(1)} %bitcast.292, f32[6,512]{1,0:T(8,128)S(1)} %copy-done.60, pred[512,1024]{1,0:T(8,128)(4,1)S(1)} %copy-done.6, bf16[6,1024,64]{1,2,0:T(8,128)(2,1)S(1)} %bitcast.304, bf16[6,1024,64]{1,2,0:T(8,128)(2,1)S(1)} %bitcast.312), kind=kOutput, calls=%fused_computation.1 | convolution fusion | flops 418378752 | bytes 26898432 | tf_op jit(solution)/shard_map/hqd,hkd->hqk/dot_general | solution.py:165
  350.7 10.0 %multiply_convert_fusion = bf16[6,512,1024]{2,1,0:T(8,128)(2,1)} fusion(f32[6,512,1024]{2,1,0:T(8,128)} %get-tuple-element.235, f32[6,512,1024]{2,1,0:T(8,128)S(1)} %bitcast.292, f32[6,512]{1,0:T(8,128)S(1)} %get-tuple-element.234, f32[6,512]{1,0:T(8,128)S(1)} %copy-done.60, pred[512,1024]{1,0:T(8,128)(4,1)S(1)} %copy-done.6), kind=kLoop, calls=%fused_computation | loop fusion | flops 18874368 | bytes 32006144 | tf_op jit(solution)/shard_map/convert_element_type | solution.py:169
  360.7 4.2 add_convert_fusion.2
  372.0 3.5 add_convert_fusion.1
  383.4 6.6 %fusion.93 = f32[768,1152]{1,0:T(8,128)} fusion(bf16[1024,384]{0,1:T(8,128)(2,1)} %bitcast.362, bf16[1024,384]{0,1:T(8,128)(2,1)} %bitcast.329, bf16[1024,384]{0,1:T(8,128)(2,1)} %bitcast.327, f32[768]{0:T(1024)S(1)} %copy-done.71, f32[1024]{0:T(1024)S(1)} %copy-done.124, bf16[512,768]{1,0:T(8,128)(2,1)} %copy-done.37, bf16[512,768]{1,0:T(8,128)(2,1)S(1)} %copy-done.36), kind=kOutput, calls=%fused_computation.173 | convolution fusion | flops 1824522240 | bytes 7478272 | tf_op jit(solution)/shard_map/dot_general | solution.py:38
  390.0 7.6 %collective-permute-done.10 = bf16[512,768]{1,0:T(8,128)(2,1)S(1)} collective-permute-done((bf16[512,768]{1,0:T(8,128)(2,1)}, bf16[512,768]{1,0:T(8,128)(2,1)S(1)}, u32[]{:S(2)}, u32[]{:S(2)}) %collective-permute-start.10) | collective-permute-done | bytes 786464 | tf_op jit(solution)/shard_map/ppermute | solution.py:81
  399.2 2.3 select_maximum_fusion
  404.6 4.3 collective-permute-done.11
  408.9 2.4 fusion.26
  412.2 6.0 collective-permute-start.12
  418.2 3.3 fusion.113
  421.6 8.5 %collective-permute-done.12 = bf16[4,2,24,1280]{3,2,1,0:T(8,128)(2,1)} collective-permute-done((bf16[4,2,24,1280]{3,2,1,0:T(8,128)(2,1)}, bf16[4,2,24,1280]{3,2,1,0:T(8,128)(2,1)}, u32[]{:S(2)}, u32[]{:S(2)}) %collective-permute-start.12) | collective-permute-done | bytes 491552 | tf_op jit(solution)/shard_map/ppermute | solution.py:115
  437.3 8.8 %collective-permute-done.14 = bf16[2,24,1280]{2,1,0:T(8,128)(2,1)S(1)} collective-permute-done((bf16[2,24,1280]{2,1,0:T(8,128)(2,1)S(1)}, bf16[2,24,1280]{2,1,0:T(8,128)(2,1)S(1)}, u32[]{:S(2)}, u32[]{:S(2)}) %collective-permute-start.14) | collective-permute-done | bytes 122912 | tf_op jit(solution)/shard_map/ppermute | solution.py:115
  449.8 2.6 collective-permute-done.16
  459.7 2.5 dynamic-slice_bitcast_fusion
  467.1 78.0 %reduce-scatter.3.cloned.1.call-done = f32[24,768]{1,0:T(8,128)} async-done(((f32[768,768]{1,0:T(8,128)}), f32[24,768]{1,0:T(8,128)}) %reduce-scatter.3.cloned.1.call-update) | async-done | bytes 73744 | tf_op jit(solution)/shard_map/reduce_scatter | solution.py:412
  549.1 11.2 %multiply_reduce_fusion.2 = (f32[2,3]{1,0:T(2,128)S(1)}, f32[2,3]{1,0:T(2,128)S(1)}, f32[2,3,96,2048]{3,2,1,0:T(8,128)}, f32[2,3,96,2048]{3,2,1,0:T(8,128)}) fusion(f32[2,3,96,2048]{3,2,1,0:T(8,128)} %param.36, bf16[1,3,96,2048]{3,2,1,0:T(8,128)(2,1)S(1)} %get-tuple-element.163, bf16[1,3,96,2048]{3,2,1,0:T(8,128)(2,1)S(1)} %get-tuple-element.162, ...), kind=kLoop, calls=%fused_computation.23 | loop fusion | flops 22413300 | bytes 25952304 | tf_op jit(solution)/shard_map/reduce_sum | solution.py:483
  560.9 2.7 concatenate.107
  577.0 3.1 fusion.46
  587.4 9.8 %multiply_subtract_fusion = f32[2,3,96,2048]{3,2,1,0:T(8,128)} fusion(f32[2,3,96,2048]{3,2,1,0:T(8,128)} %param.36, f32[2,3]{1,0:T(2,128)S(1)} %constant_dynamic-slice_fusion, f32[2,3,96,2048]{3,2,1,0:T(8,128)} %get-tuple-element.150, f32[2,3,96,2048]{3,2,1,0:T(8,128)} %get-tuple-element.149), kind=kLoop, calls=%fused_computation.22 | loop fusion | flops 9437184 | bytes 18874392 | tf_op jit(solution)/shard_map/sub | solution.py:533
  (518 shorter events, 130.1 us)
Async XLA Ops:
  7.2 221.5 %all-gather.2.cloned.1.call-start = ((), (), s32[]{:S(2)}) async-start(), calls=%async_computation.7 | async-start | bytes 11796480 | tf_op jit(solution)/shard_map/all_gather | solution.py:233
  9.1 8.9 %collective-permute-start.1 = (bf16[24,2048]{1,0:T(8,128)(2,1)S(1)}, bf16[24,2048]{1,0:T(8,128)(2,1)S(1)}, u32[]{:S(2)}, u32[]{:S(2)}) collective-permute-start(bf16[24,2048]{1,0:T(8,128)(2,1)S(1)} %get-tuple-element.207), channel_id=1, source_target_pairs={{0,4},{4,0},{1,5},{5,1},{2,6},{6,2},{3,7},{7,3},{8,12},{12,8},{9,1... | collective-permute-start | bytes 294920 | tf_op jit(solution)/shard_map/ppermute | solution.py:81
  12.2 53.0 %collective-permute-start = (bf16[512,768]{1,0:T(8,128)(2,1)}, bf16[512,768]{1,0:T(8,128)(2,1)}, u32[]{:S(2)}, u32[]{:S(2)}) collective-permute-start(bf16[512,768]{1,0:T(8,128)(2,1)} %bitcast.300), channel_id=1, source_target_pairs={{0,4},{4,0},{1,5},{5,1},{2,6},{6,2},{3,7},{7,3},{8,12},{12,8},{9,1... | collective-permute-start | bytes 2359304 | tf_op jit(solution)/shard_map/ppermute | solution.py:81
  16.1 41.2 %collective-permute-start.8 = (bf16[3,96,2048]{2,1,0:T(8,128)(2,1)}, bf16[3,96,2048]{2,1,0:T(8,128)(2,1)}, u32[]{:S(2)}, u32[]{:S(2)}) collective-permute-start(bf16[3,96,2048]{2,1,0:T(8,128)(2,1)} %dynamic-slice_bitcast_fusion.1), channel_id=1, source_target_pairs={{0,4},{4,0},{1,5},{5,1},{2,6},{6,2},{3,7},{7,3},{8,12},{12,8},{9,1... | collective-permute-start | bytes 3538952 | tf_op jit(solution)/shard_map/ppermute | solution.py:81
  18.1 9.8 %collective-permute-start.2 = (bf16[2,24,2048]{2,1,0:T(8,128)(2,1)S(1)}, bf16[2,24,2048]{2,1,0:T(8,128)(2,1)S(1)}, u32[]{:S(2)}, u32[]{:S(2)}) collective-permute-start(bf16[2,24,2048]{2,1,0:T(8,128)(2,1)S(1)} %pad_maximum_fusion.17), channel_id=1, source_target_pairs={{0,8},{8,16},{16,24},{24,0},{1,9},{9,17},{17,25},{25,1},{2,10},{10... | collective-permute-start | bytes 589832 | tf_op jit(solution)/shard_map/ppermute | solution.py:106
  19.7 14.6 %collective-permute-start.3 = (bf16[2,24,2048]{2,1,0:T(8,128)(2,1)S(1)}, bf16[2,24,2048]{2,1,0:T(8,128)(2,1)S(1)}, u32[]{:S(2)}, u32[]{:S(2)}) collective-permute-start(bf16[2,24,2048]{2,1,0:T(8,128)(2,1)S(1)} %pad_maximum_fusion.17), channel_id=1, source_target_pairs={{0,16},{8,24},{16,0},{24,8},{1,17},{9,25},{17,1},{25,9},{2,18},{10... | collective-permute-start | bytes 589832 | tf_op jit(solution)/shard_map/ppermute | solution.py:106
  22.3 12.0 %collective-permute-start.4 = (bf16[2,24,2048]{2,1,0:T(8,128)(2,1)S(1)}, bf16[2,24,2048]{2,1,0:T(8,128)(2,1)S(1)}, u32[]{:S(2)}, u32[]{:S(2)}) collective-permute-start(bf16[2,24,2048]{2,1,0:T(8,128)(2,1)S(1)} %pad_maximum_fusion.17), channel_id=1, source_target_pairs={{0,24},{8,0},{16,8},{24,16},{1,25},{9,1},{17,9},{25,17},{2,26},{10... | collective-permute-start | bytes 589832 | tf_op jit(solution)/shard_map/ppermute | solution.py:106
  34.3 25.9 %collective-permute-start.5 = (bf16[4,2,24,2048]{3,2,1,0:T(8,128)(2,1)S(1)}, bf16[4,2,24,2048]{3,2,1,0:T(8,128)(2,1)}, u32[]{:S(2)}, u32[]{:S(2)}) collective-permute-start(bf16[4,2,24,2048]{3,2,1,0:T(8,128)(2,1)S(1)} %bitcast_dynamic-update-slice_fusion.2), channel_id=1, source_target_pairs={{0,2},{1,3},{2,0},{3,1},{4,6},{5,7},{6,4},{7,5},{8,10},{9,11},{10,... | collective-permute-start | bytes 2359304 | tf_op jit(solution)/shard_map/ppermute | solution.py:106
  62.4 4.4 collective-permute-start.6
  62.5 29.3 %copy-start.25 = (pred[512,512]{0,1:T(8,128)(4,1)}, pred[512,512]{0,1:T(8,128)(4,1)S(1)}, u32[]{:S(2)}) copy-start(pred[512,512]{0,1:T(8,128)(4,1)S(1)} %iota_compare_fusion.4) | copy-start | bytes 786436
  95.8 229.9 %copy-start.61 = (f32[6,512]{1,0:T(8,128)}, f32[6,512]{1,0:T(8,128)S(1)}, u32[]{:S(2)}) copy-start(f32[6,512]{1,0:T(8,128)S(1)} %log_add_fusion.1) | copy-start | bytes 36868
  105.5 14.0 %copy-start.8 = (bf16[1,512,768]{2,1,0:T(8,128)(2,1)S(1)}, bf16[1,512,768]{2,1,0:T(8,128)(2,1)}, u32[]{:S(2)}) copy-start(bf16[1,512,768]{2,1,0:T(8,128)(2,1)} %param.29) | copy-start | bytes 2359300
  105.8 11.8 %collective-permute-start.7 = (bf16[512,384]{1,0:T(8,128)(2,1)S(1)}, bf16[512,384]{1,0:T(8,128)(2,1)}, u32[]{:S(2)}, u32[]{:S(2)}) collective-permute-start(bf16[512,384]{1,0:T(8,128)(2,1)S(1)} %copy.200), channel_id=1, source_target_pairs={{0,4},{4,0},{1,5},{5,1},{2,6},{6,2},{3,7},{7,3},{8,12},{12,8},{9,1... | collective-permute-start | bytes 1179656 | tf_op jit(solution)/shard_map/ppermute | solution.py:81
  123.1 18.7 %copy-start.10 = (bf16[512,768]{1,0:T(8,128)(2,1)}, bf16[512,768]{1,0:T(8,128)(2,1)S(1)}, u32[]{:S(2)}) copy-start(bf16[512,768]{1,0:T(8,128)(2,1)S(1)} %fusion.75) | copy-start | bytes 2359300
  123.7 9.5 %copy-start.56 = (f32[512,12]{0,1:T(8,128)}, f32[512,12]{0,1:T(8,128)S(1)}, u32[]{:S(2)}) copy-start(f32[512,12]{0,1:T(8,128)S(1)} %get-tuple-element.232) | copy-start | bytes 73732
  127.0 8.5 %all-to-all-start.2 = ((f32[8,1,96]{2,1,0:T(1,128)}), f32[8,1,96]{2,1,0:T(1,128)S(1)}, u32[]{:S(2)}, u32[]{:S(2)}) async-start(f32[8,1,96]{2,1,0:T(1,128)} %all_to_all.20), calls=%async_computation.2 | async-start | bytes 8192 | tf_op jit(solution)/shard_map/all_to_all | solution.py:336
  136.2 20.3 %all-to-all-start.3 = ((bf16[8,96,768]{2,1,0:T(8,128)(2,1)}), bf16[8,96,768]{2,1,0:T(8,128)(2,1)S(1)}, u32[]{:S(2)}, u32[]{:S(2)}) async-start(bf16[8,96,768]{2,1,0:T(8,128)(2,1)} %bitcast.324), calls=%async_computation.3 | async-start | bytes 2359296 | tf_op jit(solution)/shard_map/all_to_all | solution.py:286
  144.7 16.1 %copy-start.75 = (f32[8,1,96]{2,1,0:T(1,128)S(1)}, f32[8,1,96]{2,1,0:T(1,128)}, u32[]{:S(2)}) copy-start(f32[8,1,96]{2,1,0:T(1,128)} %copy-done.74) | copy-start | bytes 9220
  156.5 79.6 %all-to-all-start = ((bf16[8,96,768]{2,1,0:T(8,128)(2,1)}), bf16[8,96,768]{2,1,0:T(8,128)(2,1)}, u32[]{:S(2)}, u32[]{:S(2)}) async-start(bf16[8,96,768]{2,1,0:T(8,128)(2,1)} %bitcast.323), calls=%async_computation | async-start | bytes 2359296 | tf_op jit(solution)/shard_map/all_to_all | solution.py:329
  253.9 33.6 %all-to-all-start.1 = ((bf16[8,96,768]{2,1,0:T(8,128)(2,1)}), bf16[8,96,768]{2,1,0:T(8,128)(2,1)}, u32[]{:S(2)}, u32[]{:S(2)}) async-start(bf16[8,96,768]{2,1,0:T(8,128)(2,1)} %bitcast.50), calls=%async_computation.1 | async-start | bytes 2359296 | tf_op jit(solution)/shard_map/all_to_all | solution.py:345
  258.3 201.4 %reduce-scatter.5.cloned.1.call-start = ((), (), s32[]{:S(2)}) async-start(), calls=%async_computation.9 | async-start | bytes 11796480 | tf_op jit(solution)/shard_map/reduce_scatter | solution.py:364
  287.5 21.2 %all-to-all-start.4 = ((bf16[8,96,768]{2,1,0:T(8,128)(2,1)}), bf16[8,96,768]{2,1,0:T(8,128)(2,1)}, u32[]{:S(2)}, u32[]{:S(2)}) async-start(bf16[8,96,768]{2,1,0:T(8,128)(2,1)} %bitcast.322), calls=%async_computation.4 | async-start | bytes 2359296 | tf_op jit(solution)/shard_map/all_to_all | solution.py:353
  291.9 253.2 %reduce-scatter.3.cloned.1.call-start = ((), (), s32[]{:S(2)}) async-start(), calls=%async_computation.8 | async-start | bytes 2433024 | tf_op jit(solution)/shard_map/reduce_scatter | solution.py:412
  300.2 13.7 %copy-start.100 = (f32[512]{0:T(512)}, f32[512]{0:T(512)S(1)}, u32[]{:S(2)}) copy-start(f32[512]{0:T(512)S(1)} %get-tuple-element.119) | copy-start | bytes 6148
  300.2 13.7 %copy-start.103 = (f32[512]{0:T(512)}, f32[512]{0:T(512)S(1)}, u32[]{:S(2)}) copy-start(f32[512]{0:T(512)S(1)} %get-tuple-element.120) | copy-start | bytes 6148
  300.2 11.1 %copy-start.22 = (bf16[16,768]{0,1:T(8,128)(2,1)S(1)}, bf16[16,768]{0,1:T(8,128)(2,1)}, u32[]{:S(2)}) copy-start(bf16[16,768]{0,1:T(8,128)(2,1)} %copy-done.20) | copy-start | bytes 73732
  300.3 13.6 %copy-start.106 = (f32[512]{0:T(512)}, f32[512]{0:T(512)S(1)}, u32[]{:S(2)}) copy-start(f32[512]{0:T(512)S(1)} %multiply_reduce_fusion.9) | copy-start | bytes 6148
  317.1 8.0 %collective-permute-start.9 = (bf16[512,384]{1,0:T(8,128)(2,1)S(1)}, bf16[512,384]{1,0:T(8,128)(2,1)S(1)}, u32[]{:S(2)}, u32[]{:S(2)}) collective-permute-start(bf16[512,384]{1,0:T(8,128)(2,1)S(1)} %constant_dynamic-slice_fusion.4), channel_id=1, source_target_pairs={{0,4},{4,0},{1,5},{5,1},{2,6},{6,2},{3,7},{7,3},{8,12},{12,8},{9,1... | collective-permute-start | bytes 1179656 | tf_op jit(solution)/shard_map/ppermute | solution.py:81
  332.6 10.5 %slice-start = ((s8[12582912]{0:T(1024)(128)(4,1)}), s8[4194304]{0:T(1024)(128)(4,1)S(1)}, s32[]{:S(2)}) async-start(s8[12582912]{0:T(1024)(128)(4,1)} %bitcast.291), calls=%async_computation.10 | async-start | bytes 8388608
  332.6 10.5 %slice-start.1 = ((s8[12582912]{0:T(1024)(128)(4,1)}), s8[4194304]{0:T(1024)(128)(4,1)S(1)}, s32[]{:S(2)}) async-start(s8[12582912]{0:T(1024)(128)(4,1)} %bitcast.291), calls=%async_computation.11 | async-start | bytes 8388608
  350.7 10.0 %copy-start.15 = (bf16[6,1024,64]{1,2,0:T(8,128)(2,1)S(1)}, bf16[6,1024,64]{1,2,0:T(8,128)(2,1)}, u32[]{:S(2)}) copy-start(bf16[6,1024,64]{1,2,0:T(8,128)(2,1)} %copy-done.14) | copy-start | bytes 2359300
  350.7 10.0 %copy-start.41 = (f32[6,512,64]{1,2,0:T(8,128)S(1)}, f32[6,512,64]{1,2,0:T(8,128)}, u32[]{:S(2)}) copy-start(f32[6,512,64]{1,2,0:T(8,128)} %convolution_multiply_fusion.1) | copy-start | bytes 2359300
  380.6 16.9 %collective-permute-start.10 = (bf16[512,768]{1,0:T(8,128)(2,1)}, bf16[512,768]{1,0:T(8,128)(2,1)S(1)}, u32[]{:S(2)}, u32[]{:S(2)}) collective-permute-start(bf16[512,768]{1,0:T(8,128)(2,1)} %dynamic-slice_convert_fusion), channel_id=1, source_target_pairs={{0,4},{4,0},{1,5},{5,1},{2,6},{6,2},{3,7},{7,3},{8,12},{12,8},{9,1... | collective-permute-start | bytes 2359304 | tf_op jit(solution)/shard_map/ppermute | solution.py:81
  382.7 14.8 %copy-start.96 = (f32[512]{0:T(512)}, f32[512]{0:T(512)S(1)}, u32[]{:S(2)}) copy-start(f32[512]{0:T(512)S(1)} %get-tuple-element.215) | copy-start | bytes 6148
  383.4 14.2 %copy-start.9 = (bf16[1,512,768]{2,1,0:T(8,128)(2,1)S(1)}, bf16[1,512,768]{2,1,0:T(8,128)(2,1)}, u32[]{:S(2)}) copy-start(bf16[1,512,768]{2,1,0:T(8,128)(2,1)} %param.29) | copy-start | bytes 2359300
  383.4 14.2 %copy-start.19 = (f32[1024,768]{1,0:T(8,128)S(1)}, f32[1024,768]{1,0:T(8,128)}, u32[]{:S(2)}) copy-start(f32[1024,768]{1,0:T(8,128)} %copy-done.18) | copy-start | bytes 9437188
  404.6 4.3 collective-permute-start.11
  412.2 17.9 %collective-permute-start.12 = (bf16[4,2,24,1280]{3,2,1,0:T(8,128)(2,1)}, bf16[4,2,24,1280]{3,2,1,0:T(8,128)(2,1)}, u32[]{:S(2)}, u32[]{:S(2)}) collective-permute-start(bf16[4,2,24,1280]{3,2,1,0:T(8,128)(2,1)} %dynamic-slice_bitcast_fusion.2), channel_id=1, source_target_pairs={{0,2},{1,3},{2,0},{3,1},{4,6},{5,7},{6,4},{7,5},{8,10},{9,11},{10,... | collective-permute-start | bytes 1474568 | tf_op jit(solution)/shard_map/ppermute | solution.py:115
  421.6 27.1 %copy-start.69 = (f32[1,512,12]{1,0,2:T(1,128)S(1)}, f32[1,512,12]{1,0,2:T(1,128)}, u32[]{:S(2)}) copy-start(f32[1,512,12]{1,0,2:T(1,128)} %param.31) | copy-start | bytes 73732
  421.6 27.1 %copy-start.102 = (f32[512]{0:T(512)S(1)}, f32[512]{0:T(512)}, u32[]{:S(2)}) copy-start(f32[512]{0:T(512)} %copy-done.100) | copy-start | bytes 6148
  421.6 27.1 %copy-start.105 = (f32[512]{0:T(512)S(1)}, f32[512]{0:T(512)}, u32[]{:S(2)}) copy-start(f32[512]{0:T(512)} %copy-done.103) | copy-start | bytes 6148
  421.6 27.1 %copy-start.108 = (f32[512]{0:T(512)S(1)}, f32[512]{0:T(512)}, u32[]{:S(2)}) copy-start(f32[512]{0:T(512)} %copy-done.106) | copy-start | bytes 6148
  432.0 5.3 collective-permute-start.15
  432.5 13.6 %collective-permute-start.14 = (bf16[2,24,1280]{2,1,0:T(8,128)(2,1)S(1)}, bf16[2,24,1280]{2,1,0:T(8,128)(2,1)S(1)}, u32[]{:S(2)}, u32[]{:S(2)}) collective-permute-start(bf16[2,24,1280]{2,1,0:T(8,128)(2,1)S(1)} %get-tuple-element.191), channel_id=1, source_target_pairs={{0,16},{8,24},{16,0},{24,8},{1,17},{9,25},{17,1},{25,9},{2,18},{10... | collective-permute-start | bytes 368648 | tf_op jit(solution)/shard_map/ppermute | solution.py:115
  433.3 12.8 %collective-permute-start.13 = (bf16[2,24,1280]{2,1,0:T(8,128)(2,1)S(1)}, bf16[2,24,1280]{2,1,0:T(8,128)(2,1)S(1)}, u32[]{:S(2)}, u32[]{:S(2)}) collective-permute-start(bf16[2,24,1280]{2,1,0:T(8,128)(2,1)S(1)} %get-tuple-element.189), channel_id=1, source_target_pairs={{0,8},{8,16},{16,24},{24,0},{1,9},{9,17},{17,25},{25,1},{2,10},{10... | collective-permute-start | bytes 368648 | tf_op jit(solution)/shard_map/ppermute | solution.py:115
  447.1 5.4 collective-permute-start.16
  455.7 89.4 %copy-start.42 = (f32[4,24,768]{2,1,0:T(8,128)S(1)}, f32[4,24,768]{2,1,0:T(8,128)}, u32[]{:S(2)}) copy-start(f32[4,24,768]{2,1,0:T(8,128)} %param.34) | copy-start | bytes 884740
  462.2 85.1 %collective-permute-start.17 = (bf16[3,96,2048]{2,1,0:T(8,128)(2,1)}, bf16[3,96,2048]{2,1,0:T(8,128)(2,1)}, u32[]{:S(2)}, u32[]{:S(2)}) collective-permute-start(bf16[3,96,2048]{2,1,0:T(8,128)(2,1)} %dynamic-slice_bitcast_fusion), channel_id=1, source_target_pairs={{0,4},{4,0},{1,5},{5,1},{2,6},{6,2},{3,7},{7,3},{8,12},{12,8},{9,1... | collective-permute-start | bytes 3538952 | tf_op jit(solution)/shard_map/ppermute | solution.py:81
  549.1 11.8 %copy-start.121 = (f32[144]{0:T(256)S(1)}, f32[144]{0:T(256)}, u32[]{:S(2)}) copy-start(f32[144]{0:T(256)} %reshape.495) | copy-start | bytes 1732
  549.1 24.2 %copy-start.114 = (f32[512]{0:T(512)S(1)}, f32[512]{0:T(512)}, u32[]{:S(2)}) copy-start(f32[512]{0:T(512)} %get-tuple-element.112) | copy-start | bytes 6148
  549.1 27.9 %copy-start.34 = (bf16[512,768]{1,0:T(8,128)(2,1)S(1)}, bf16[512,768]{1,0:T(8,128)(2,1)}, u32[]{:S(2)}) copy-start(bf16[512,768]{1,0:T(8,128)(2,1)} %copy-done.33) | copy-start | bytes 2359300
  549.1 27.9 %copy-start.97 = (f32[512]{0:T(512)S(1)}, f32[512]{0:T(512)}, u32[]{:S(2)}) copy-start(f32[512]{0:T(512)} %copy-done.96) | copy-start | bytes 6148
  549.1 27.9 %copy-start.99 = (f32[512]{0:T(512)S(1)}, f32[512]{0:T(512)}, u32[]{:S(2)}) copy-start(f32[512]{0:T(512)} %get-tuple-element.214) | copy-start | bytes 6148
  563.6 1.2 collective-permute-start.18
  564.8 3.6 collective-permute-start.19
  568.3 3.6 collective-permute-start.20
  571.9 3.6 collective-permute-start.21
  575.5 4.6 collective-permute-start.22
  577.0 9.8 %copy-start.65 = (f32[16,24]{1,0:T(8,128)S(1)}, f32[16,24]{1,0:T(8,128)}, u32[]{:S(2)}) copy-start(f32[16,24]{1,0:T(8,128)} %param.35) | copy-start | bytes 4612
  577.0 9.8 %copy-start.81 = (f32[16,24]{1,0:T(8,128)S(1)}, f32[16,24]{1,0:T(8,128)}, u32[]{:S(2)}) copy-start(f32[16,24]{1,0:T(8,128)} %get-tuple-element.151) | copy-start | bytes 4612
  577.0 9.7 %copy-start.82 = (f32[16,24]{1,0:T(8,128)S(1)}, f32[16,24]{1,0:T(8,128)}, u32[]{:S(2)}) copy-start(f32[16,24]{1,0:T(8,128)} %get-tuple-element.152) | copy-start | bytes 4612
  581.0 16.2 %copy-start.83 = (f32[12,12]{1,0:T(8,128)}, f32[12,12]{1,0:T(8,128)S(1)}, u32[]{:S(2)}) copy-start(f32[12,12]{1,0:T(8,128)S(1)} %get-tuple-element.147) | copy-start | bytes 1732
  581.0 16.2 %copy-start.84 = (f32[12,12]{1,0:T(8,128)}, f32[12,12]{1,0:T(8,128)S(1)}, u32[]{:S(2)}) copy-start(f32[12,12]{1,0:T(8,128)S(1)} %get-tuple-element.148) | copy-start | bytes 1732
  582.6 14.6 %copy-start.129 = (f32[2,33]{1,0:T(2,128)}, f32[2,33]{1,0:T(2,128)S(1)}, u32[]{:S(2)}) copy-start(f32[2,33]{1,0:T(2,128)S(1)} %maximum_sqrt_fusion) | copy-start | bytes 796
  (123 other events, 547.7 us)
Sparse Core Ops, SparseCore 0:
  60.4 168.2 all-gather.1
  276.3 159.8 reduce-scatter.4
  442.2 102.9 reduce-scatter.2

commit v2 on v1

v2 whole, which is shorter than its diff:
```python
import jax
import jax.numpy as jnp
from jax import lax
from jax.experimental import pallas as pl
from jax.experimental.pallas import tpu as pltpu
from jax.sharding import PartitionSpec as P

HEADS = 12
HDIM = 64
NFFN = 8
TOP = 2
STEP = 4
NEXP = 12

beta_one = 0.9
beta_two = 0.999
adam_eps = 1e-06
weight_decay = 0.01
learn_rate = 0.25
norm_eps = 1e-06
rope_base = 10000.0

bf16 = jnp.bfloat16
f32 = jnp.float32


def exact_dot(left, right):
    return jnp.dot(left, right, precision=lax.Precision.HIGHEST, preferred_element_type=f32)


def dot_nn(left, right):
    return lax.dot_general(left, right, (((1,), (0,)), ((), ())), preferred_element_type=f32)


def dot_nt(left, right):
    return lax.dot_general(left, right, (((1,), (1,)), ((), ())), preferred_element_type=f32)


def dot_tn(left, right):
    return lax.dot_general(left, right, (((0,), (0,)), ((), ())), preferred_element_type=f32)


def rotary_tables(length):
    freqs = rope_base ** (-jnp.arange(0, HDIM, 2).astype(f32) / HDIM)
    angles = jnp.arange(length).astype(f32)[:, None] * freqs[None, :]
    cosine, sine = jnp.cos(angles), jnp.sin(angles)
    return (
        jnp.concatenate([cosine] * 4, axis=-1),
        jnp.concatenate([-sine, sine, -sine, sine], axis=-1),
    )


def softmax_rows(logits):
    row_top = jnp.max(logits, axis=-1, keepdims=True)
    expd_values = jnp.exp(logits - row_top)
    return expd_values / jnp.sum(expd_values, axis=-1, keepdims=True)


def moments(weight, first, second, grad):
    first_new = beta_one * first + (1.0 - beta_one) * grad
    second_new = beta_two * second + (1.0 - beta_two) * grad * grad
    step_value = (
        first_new
        / (1.0 - beta_one**STEP)
        / (jnp.sqrt(second_new / (1.0 - beta_two**STEP)) + adam_eps)
        + weight_decay * weight
    )
    return (first_new, second_new, step_value)


DP = ("dp_far", "dp_near")
SHARD = ("x", "core")


def after(value, *others):
    return lax.optimization_barrier((value,) + others)[0]


def swap(value, axis_name):
    return lax.ppermute(value, axis_name, [(0, 1), (1, 0)])


def swap_seq(value):
    return swap(value, "seq")


def in_order(own, other, which, axis):
    low = jnp.where(which == 0, own, other)
    high = jnp.where(which == 0, other, own)
    return jnp.concatenate([low, high], axis=axis)


def gather_steps(value, axis_name, place, count):
    out = jnp.zeros((count,) + value.shape, value.dtype)
    out = lax.dynamic_update_index_in_dim(out, value, place, 0)
    for step in range(1, count):
        got = lax.ppermute(value, axis_name, [(i, (i + step) % count) for i in range(count)])
        out = lax.dynamic_update_index_in_dim(out, got, (place - step) % count, 0)
    return out


def scatter_steps(value, axis_name, place, count):
    total = lax.dynamic_index_in_dim(value, place, 0, keepdims=False).astype(f32)
    for step in range(1, count):
        block = lax.dynamic_index_in_dim(value, (place + step) % count, 0, keepdims=False)
        got = lax.ppermute(block, axis_name, [(i, (i + step) % count) for i in range(count)])
        total = total + got.astype(f32)
    return total


def keep_and_send(value, place, axis):
    return (
        lax.dynamic_index_in_dim(value, place, axis, keepdims=False),
        lax.dynamic_index_in_dim(value, 1 - place, axis, keepdims=False),
    )


def sum_everywhere(value, sizes):
    for axis_name in ("core", "x", "seq", "dp_near", "dp_far"):
        bit = 1
        while bit < sizes[axis_name]:
            value = value + lax.ppermute(
                value, axis_name, [(i, i ^ bit) for i in range(sizes[axis_name])]
            )
            bit *= 2
    return value


QUERY_ROWS = 256
FF_COLUMNS = 512

def turn(value):
    lane = lax.broadcasted_iota(jnp.int32, value.shape, 1) % HDIM
    return jnp.where(lane < HDIM // 2, pltpu.roll(value, 96, 1), pltpu.roll(value, 32, 1))

def attention_forward_kernel(x_ref, gain_ref, wq_ref, wk_ref, wv_ref, cos_ref, sin_ref, h_ref, q_ref, k_ref, v_ref, o_ref, lse_ref):
    length = x_ref.shape[0]

    @pl.when(pl.program_id(0) == 0)
    def _():
        for start in range(0, length, QUERY_ROWS):
            rows = pl.ds(start, QUERY_ROWS)
            x = x_ref[rows, :].astype(f32)
            rho = lax.rsqrt(jnp.mean(x * x, axis=-1, keepdims=True) + norm_eps)
            h_ref[rows, :] = (x * rho * gain_ref[...]).astype(bf16)

    for start in range(0, length, QUERY_ROWS):
        rows = pl.ds(start, QUERY_ROWS)
        h = h_ref[rows, :]
        cos, sin = cos_ref[rows, :], sin_ref[rows, :]
        q = dot_nn(h, wq_ref[...])
        k = dot_nn(h, wk_ref[...])
        q_ref[rows, :] = (q * cos + turn(q) * sin).astype(bf16)
        k_ref[rows, :] = (k * cos + turn(k) * sin).astype(bf16)
        v_ref[rows, :] = dot_nn(h, wv_ref[...]).astype(bf16)

    ahead = lax.broadcasted_iota(jnp.int32, (QUERY_ROWS, QUERY_ROWS), 1) > lax.broadcasted_iota(jnp.int32, (QUERY_ROWS, QUERY_ROWS), 0)
    for start in range(0, length, QUERY_ROWS):
        end = start + QUERY_ROWS
        outs = []
        for head in range(2):
            lanes = slice(head * HDIM, (head + 1) * HDIM)
            q = q_ref[start:end, lanes]
            s = dot_nt(q, k_ref[:end, lanes]) * (HDIM**-0.5)
            last = jnp.where(ahead, -1e30, s[:, start:])
            s = jnp.concatenate([s[:, :start], last], axis=1) if start else last
            top = jnp.max(s, axis=-1, keepdims=True)
            p = jnp.exp(s - top)
            total = jnp.sum(p, axis=-1, keepdims=True)
            p = (p * (1.0 / total)).astype(bf16)
            outs.append(dot_nn(p, v_ref[:end, lanes]))
            lse = jnp.broadcast_to(top + jnp.log(total), (QUERY_ROWS, 128))
            lse_ref[0, head : head + 1, start:end] = lse.T[0:1, :]
        o_ref[start:end, :] = jnp.concatenate(outs, axis=1).astype(bf16)

def attention_forward(x, gain, weight, cos, sin):
    length, width = x.shape
    half = weight.shape[1] // 3
    pairs = half // 128
    full = lambda shape: pl.BlockSpec(shape, lambda p: (0,) * len(shape))
    col = lambda base: pl.BlockSpec((width, 128), lambda p, base=base: (0, base + p))
    out_col = pl.BlockSpec((length, 128), lambda p: (0, p))
    return pl.pallas_call(
        attention_forward_kernel,
        grid=(pairs,),
        in_specs=[full((length, width)), full((1, width)), col(0), col(pairs), col(2 * pairs), full((length, 128)), full((length, 128))],
        out_specs=[full((length, width)), out_col, out_col, out_col, out_col, pl.BlockSpec((1, 2, length), lambda p: (p, 0, 0))],
        out_shape=[jax.ShapeDtypeStruct((length, width), bf16)] + [jax.ShapeDtypeStruct((length, half), bf16)] * 4 + [jax.ShapeDtypeStruct((pairs, 2, length), f32)],
        compiler_params=pltpu.CompilerParams(vmem_limit_bytes=40 * 2**20),
        cost_estimate=pl.CostEstimate(flops=6 * length * width * half + 4 * length * length * half, bytes_accessed=8 * length * width, transcendentals=length * length * half // HDIM),
    )(x, gain, weight, weight, weight, cos, sin)

def attention_backward_kernel(h_ref, q_ref, k_ref, v_ref, do_ref, lse_ref, wq_ref, wk_ref, wv_ref, cos_ref, sin_ref, dw_ref, dh_ref, dq_scr, dk_scr, dv_scr):
    length = h_ref.shape[0]
    step = pl.program_id(0)
    behind = lax.broadcasted_iota(jnp.int32, (QUERY_ROWS, QUERY_ROWS), 0) > lax.broadcasted_iota(jnp.int32, (QUERY_ROWS, QUERY_ROWS), 1)
    dk_scr[...] = jnp.zeros_like(dk_scr)
    dv_scr[...] = jnp.zeros_like(dv_scr)
    for start in range(0, length, QUERY_ROWS):
        end = start + QUERY_ROWS
        for head in range(2):
            lanes = slice(head * HDIM, (head + 1) * HDIM)
            q, do = q_ref[start:end, lanes], do_ref[start:end, lanes]
            k, v = k_ref[:end, lanes], v_ref[:end, lanes]
            s = dot_nt(k, q) * (HDIM**-0.5) - lse_ref[0, head : head + 1, start:end]
            last = jnp.where(behind, -1e30, s[start:])
            s = jnp.concatenate([s[:start], last], axis=0) if start else last
            p = jnp.exp(s)
            dp = dot_nt(v, do)
            delta = jnp.sum(p * dp, axis=0, keepdims=True)
            ds = (p * (dp - delta)).astype(bf16)
            dq_scr[start:end, lanes] = dot_tn(ds, k) * (HDIM**-0.5)
            dk_scr[:end, lanes] += dot_nn(ds, q)
            dv_scr[:end, lanes] += dot_nn(p.astype(bf16), do)
    cos, sin = cos_ref[...], sin_ref[...]

    dq = dq_scr[...].astype(bf16).astype(f32)
    dk = (dk_scr[...] * (HDIM**-0.5)).astype(bf16).astype(f32)
    dqp = (dq * cos + turn(dq * sin)).astype(bf16)
    dkp = (dk * cos + turn(dk * sin)).astype(bf16)
    dvb = dv_scr[...].astype(bf16)
    d = jnp.concatenate([dqp, dkp, dvb], axis=1)
    w = jnp.concatenate([wq_ref[...], wk_ref[...], wv_ref[...]], axis=1)
    dw_ref[...] = dot_tn(h_ref[...], d).astype(bf16)
    dh = dot_nt(d, w)

    @pl.when(step == 0)
    def _():
        dh_ref[...] = dh

    @pl.when(step > 0)
    def _():
        dh_ref[...] += dh

def attention_backward(h, q, k, v, do, lse, weight, cos, sin):
    length, width = h.shape
    half = weight.shape[1] // 3
    pairs = half // 128
    full = lambda shape: pl.BlockSpec(shape, lambda p: (0,) * len(shape))
    col = lambda base: pl.BlockSpec((width, 128), lambda p, base=base: (0, base + p))
    out_col = pl.BlockSpec((length, 128), lambda p: (0, p))
    return pl.pallas_call(
        attention_backward_kernel,
        grid=(pairs,),
        in_specs=[full((length, width)), out_col, out_col, out_col, out_col, pl.BlockSpec((1, 2, length), lambda p: (p, 0, 0)), col(0), col(pairs), col(2 * pairs), full((length, 128)), full((length, 128))],
        out_specs=[pl.BlockSpec((width, 384), lambda p: (0, p)), full((length, width))],
        out_shape=[jax.ShapeDtypeStruct((width, 3 * half), bf16), jax.ShapeDtypeStruct((length, width), f32)],
        scratch_shapes=[pltpu.VMEM((length, 128), f32)] * 3,
        compiler_params=pltpu.CompilerParams(vmem_limit_bytes=48 * 2**20),
        cost_estimate=pl.CostEstimate(flops=12 * length * width * half + 10 * length * length * half, bytes_accessed=12 * length * width, transcendentals=length * length * half // HDIM),
    )(h, q, k, v, do, lse, weight, weight, weight, cos, sin)


def three_parts(value):
    high = value.astype(bf16)
    rest = value - high.astype(f32)
    middle = rest.astype(bf16)
    low = (rest - middle.astype(f32)).astype(bf16)
    lane = lax.broadcasted_iota(jnp.int32, (value.shape[0], 128), 1)
    zero = jnp.zeros((), bf16)
    return jnp.where(lane == 0, high, jnp.where(lane == 1, middle, jnp.where(lane == 2, low, zero)))

def three_parts_rounded(value):
    high = lax.reduce_precision(value, 8, 7)
    middle = lax.reduce_precision(value - high, 8, 7)
    low = lax.reduce_precision(value - high - middle, 8, 7)
    lane = lax.broadcasted_iota(jnp.int32, (value.shape[0], 128), 1)
    return (
        jnp.where(lane == 0, high, 0.0)
        + jnp.where(lane == 1, middle, 0.0)
        + jnp.where(lane == 2, low, 0.0)
    ).astype(bf16)


def expert_kernel(taken_ref, dout_ref, weight_ref, f_ref, dtaken_ref, hidden_ref, dgate_ref, dup_ref, dresult_ref, f_acc, d_acc):
    step, last = pl.program_id(0), pl.num_programs(0) - 1
    width = dout_ref.shape[1]

    @pl.when(step == 0)
    def _():
        parts = taken_ref[:, width:].astype(f32)
        gate = jnp.sum(parts, axis=1, keepdims=True)
        dresult_ref[...] = (gate * dout_ref[...].astype(f32)).astype(bf16)
        f_acc[...] = jnp.zeros_like(f_acc)
        d_acc[...] = jnp.zeros_like(d_acc)

    taken = taken_ref[:, :width]
    a = dot_nn(taken, weight_ref[0])
    b = dot_nn(taken, weight_ref[1])
    sig = jax.nn.sigmoid(a)
    act = a * sig
    hidden = (act * b).astype(bf16)
    hidden_ref[...] = hidden
    f_acc[...] += dot_nt(hidden, weight_ref[2])
    dhidden = dot_nn(dresult_ref[...], weight_ref[2])
    dgate = (dhidden * b * (sig * (1.0 + a - act))).astype(bf16)
    dup = (dhidden * act).astype(bf16)
    dgate_ref[...] = dgate
    dup_ref[...] = dup
    d_acc[...] += dot_nt(dgate, weight_ref[0]) + dot_nt(dup, weight_ref[1])

    @pl.when(step == last)
    def _():
        f = f_acc[...].astype(bf16)
        f_ref[...] = f
        dtaken_ref[:, :width] = d_acc[...].astype(bf16)
        dpicked = jnp.sum(dout_ref[...].astype(f32) * f.astype(f32), axis=1, keepdims=True)
        dtaken_ref[:, width:] = three_parts(dpicked)

def expert_compute(taken, dout, weight):
    rows, width = dout.shape
    hidden = weight.shape[2]
    whole = lambda columns: pl.BlockSpec((rows, columns), lambda i: (0, 0))
    part = pl.BlockSpec((rows, FF_COLUMNS), lambda i: (0, i))
    shape = lambda columns: jax.ShapeDtypeStruct((rows, columns), bf16)
    return pl.pallas_call(
        expert_kernel,
        grid=(hidden // FF_COLUMNS,),
        in_specs=[whole(width + 128), whole(width), pl.BlockSpec((3, width, FF_COLUMNS), lambda i: (0, 0, i))],
        out_specs=[whole(width), whole(width + 128), part, part, part, whole(width)],
        out_shape=[shape(width), shape(width + 128), shape(hidden), shape(hidden), shape(hidden), shape(width)],
        scratch_shapes=[pltpu.VMEM((rows, width), f32)] * 2,
        compiler_params=pltpu.CompilerParams(vmem_limit_bytes=48 * 2**20),
        cost_estimate=pl.CostEstimate(flops=14 * rows * width * hidden, bytes_accessed=6 * width * hidden + 6 * rows * hidden, transcendentals=rows * hidden),
    )(taken, dout, weight)


def make_shards(sizes):
    n_seq, n_x = sizes["seq"], sizes["x"]
    n_dp = sizes["dp_far"] * sizes["dp_near"]

    def shards(
        tokens,
        cotangent,
        previous_logits,
        routes,
        priority,
        attention_master,
        vector_master,
        expert_master,
        mixing_master,
        attention_first,
        vector_first,
        expert_first,
        mixing_first,
        attention_second,
        vector_second,
        expert_second,
        mixing_second,
    ):
        z, y, s = lax.axis_index(DP), lax.axis_index("seq"), lax.axis_index(SHARD)
        far, near = lax.axis_index("dp_far"), lax.axis_index("dp_near")
        x_place, core = lax.axis_index("x"), lax.axis_index("core")
        row_count, model_width = tokens.shape[1], tokens.shape[2]
        half_width = model_width // 2
        local_experts = expert_master.shape[0]
        spread = local_experts == 2 and n_x == 2 and sizes["dp_far"] == 2
        ep_axes = ("dp_near", "seq", "x") if spread else SHARD
        own_rows = attention_master.shape[1]

        def cross(same_y, other_y):
            got = lax.ppermute(same_y, ("dp_near", "core"), [(1, 2), (2, 1)])
            moves = [
                (4 * n + 2 * q + c, 4 * c + 2 * (1 - q) + n)
                for n in range(2)
                for q in range(2)
                for c in range(2)
            ]
            return (
                jnp.where(near == core, same_y, got),
                lax.ppermute(other_y, ("dp_near", "seq", "core"), moves),
            )

        attention_low = attention_master.astype(bf16)
        vector_low = vector_master.astype(bf16).T
        vector_pad = 128 - vector_low.shape[1]

        def weight_pack(which):
            columns = lax.dynamic_slice_in_dim(attention_low[:3], which * half_width, half_width, 2)
            return jnp.concatenate(
                [columns[0], columns[1], columns[2], attention_low[3], jnp.pad(vector_low, ((0, 0), (0, vector_pad)))],
                axis=1,
            )

        packed = in_order(weight_pack(y)[None], swap_seq(weight_pack(1 - y))[None], y, 0)
        packed_z = gather_steps(packed, DP, z, n_dp)

        expert_low = after(expert_master, packed).astype(bf16)
        if spread:
            rows_low = in_order(*cross(*keep_and_send(expert_low, y, 0)), y, 1)
            rows_low = after(rows_low, packed_z)
            expert_use = lax.all_gather(rows_low, ("dp_far", "core"), axis=1, tiled=True)
        else:
            rows_low = expert_low[0]
            expert_use = lax.all_gather(rows_low, DP + ("seq",), axis=1, tiled=True)

        packed = gather_steps(packed_z, "x", x_place, n_x)
        packed = in_order(packed[None], swap(packed, "core")[None], core, 0)
        packed = packed.transpose(2, 3, 1, 0, 4, 5).reshape(model_width, -1)
        qkv_weight = packed[:, : 3 * half_width]
        out_weight = packed[:, 3 * half_width : 3 * half_width + model_width]
        vector_all = packed[:, 3 * half_width + model_width :][:, : 4 + NEXP].T

        route_rows = routes[0]
        order = priority[0, 0]
        capacity = 9 * row_count * TOP // (8 * NEXP)
        expert_ids = jnp.arange(NEXP)[None, :]
        hit_each = [route_rows[:, j : j + 1] == expert_ids for j in range(TOP)]
        hits = (hit_each[0] | hit_each[1]).astype(bf16)
        before = (order[None, :] < order[:, None]).astype(bf16)
        counts = dot_nn(before, hits)
        kept, dispatch = [], []
        block_ids = jnp.arange(NFFN * capacity)[None, :]
        for j in range(TOP):
            slot = jnp.sum(jnp.where(hit_each[j], counts, 0.0), axis=1, keepdims=True).astype(
                jnp.int32
            )
            route = route_rows[:, j : j + 1]
            keep = (route < NFFN) & (slot < capacity)
            block = ((route // 2) % 2) * 4 + (route % 2) * 2 + route // 4 if spread else route
            kept.append(keep)
            dispatch.append(
                ((block_ids == block * capacity + slot) & keep).astype(bf16)
            )
        dispatch_both = dispatch[0] + dispatch[1]

        tokens_all = in_order(tokens[0], swap_seq(after(tokens[0], rows_low)), y, 0)
        gain_one = vector_all[0].astype(f32)[None, :]
        gain_two = vector_all[1].astype(f32)[None, :]
        cosine, sine = rotary_tables(tokens_all.shape[0])
        normed, query, key, value, mixed, log_sums = attention_forward(
            tokens_all, gain_one, qkv_weight, cosine, sine
        )

        upstream = cotangent[0].astype(f32)
        dout_rows = dot_tn(dispatch_both, after(cotangent[0], tokens_all)).astype(bf16)
        dout_rows = lax.all_to_all(
            dout_rows.reshape(NFFN, capacity, model_width), ep_axes, 0, 0, tiled=True
        ).reshape(NFFN * capacity, model_width)
        mixed, dout_rows = lax.optimization_barrier((mixed, dout_rows))

        mixed_keep = lax.dynamic_slice_in_dim(mixed, y * row_count, row_count, 0)
        mixed_send = lax.dynamic_slice_in_dim(mixed, (1 - y) * row_count, row_count, 0)
        mixed_tokens = in_order(mixed_keep, swap_seq(mixed_send), y, 1)

        inputs = tokens[0].astype(f32)
        resid = inputs + dot_nn(mixed_tokens, out_weight)
        rho_two = lax.rsqrt(jnp.mean(resid * resid, axis=-1, keepdims=True) + norm_eps)
        normed_two = resid * rho_two * gain_two
        expert_in = normed_two.astype(bf16)
        router = vector_all[4:]
        previous = previous_logits[0]
        logits = dot_nt(expert_in, router) + exact_dot(previous, mixing_master)
        gates = softmax_rows(logits)
        picked = [
            jnp.sum(jnp.where(hit_each[j], gates, 0.0), axis=1, keepdims=True) for j in range(TOP)
        ]

        consts = vector_all[2:4].astype(f32)
        dlocal = [
            jnp.sum(upstream * normed_two, axis=-1, keepdims=True),
            jnp.sum(upstream * consts[0:1], axis=-1, keepdims=True),
            jnp.sum(upstream * consts[1:2], axis=-1, keepdims=True),
        ]

        def to_experts(rows):
            rows = rows.reshape(NFFN, capacity, rows.shape[1])
            return lax.all_to_all(rows, ep_axes, 0, 0, tiled=True).reshape(NFFN * capacity, -1)

        gate_parts = [three_parts_rounded(picked[j]) for j in range(TOP)]
        taken = dot_tn(
            jnp.concatenate(dispatch, axis=0),
            jnp.concatenate(
                [jnp.concatenate([expert_in, gate_parts[j]], axis=1) for j in range(TOP)], axis=0
            ),
        ).astype(bf16)
        taken = to_experts(taken)
        result, dtaken, hidden, dgate_low, dup_low, dresult = expert_compute(
            taken, dout_rows, expert_use
        )
        dtaken = to_experts(dtaken)
        result = to_experts(after(result, dtaken))
        taken = taken[:, :model_width]

        def sum_rows(grad):
            if not spread:
                return lax.psum_scatter(grad, DP + ("seq",), scatter_dimension=0, tiled=True)[None]
            grad = lax.psum_scatter(grad, ("dp_far", "core"), scatter_dimension=0, tiled=True)
            grad = grad.reshape(2, -1, grad.shape[1])
            same_y, other_y = cross(*keep_and_send(grad, y, 0))
            return in_order(same_y[None], other_y[None], y, 0)

        hidden_width = hidden.shape[1]
        ddown = sum_rows(dot_tn(dresult, hidden).astype(bf16))
        dgate_up = sum_rows(dot_tn(taken, jnp.concatenate([dgate_low, dup_low], axis=1)).astype(bf16))
        expert_sum = jnp.stack(
            [dgate_up[..., :hidden_width], dgate_up[..., hidden_width:], ddown], axis=1
        ).astype(f32)

        dgates = jnp.zeros_like(gates)
        dnormed_two = dot_nn(dispatch_both, dtaken[:, :model_width])
        value_weight = [0.0, 0.0, 0.0]
        for j in range(TOP):
            route = route_rows[:, j : j + 1]
            local = [jnp.where(route == NFFN + 1 + i, 1.0, 0.0) for i in range(3)]
            parts = dot_nn(dispatch[j], dtaken[:, model_width:])
            dpicked = jnp.sum(parts, axis=1, keepdims=True)
            for i in range(3):
                dpicked = dpicked + jnp.where(route == NFFN + 1 + i, dlocal[i], 0.0)
                value_weight[i] = value_weight[i] + local[i] * picked[j]
            dgates = dgates + jnp.where(hit_each[j], dpicked, 0.0)
        dnormed_two = dnormed_two + value_weight[0] * upstream
        dconst_one = jnp.sum(value_weight[1] * upstream, axis=0, keepdims=True)
        dconst_two = jnp.sum(value_weight[2] * upstream, axis=0, keepdims=True)
        mixture = (
            picked[0] * dot_nn(dispatch[0], result)
            + picked[1] * dot_nn(dispatch[1], result)
            + value_weight[0] * normed_two
            + value_weight[1] * consts[0:1]
            + value_weight[2] * consts[1:2]
        )
        block_output = (resid + mixture).astype(bf16)
        dlogits = gates * (dgates - jnp.sum(gates * dgates, axis=-1, keepdims=True))
        dnormed_two = dnormed_two + exact_dot(dlogits, router.astype(f32))
        drouter = exact_dot(dlogits.T, expert_in.astype(f32))
        dmixing = exact_dot(previous.T, dlogits)
        scaled_two = dnormed_two * gain_two
        dresid = upstream + (
            rho_two * scaled_two
            - resid * (rho_two * rho_two * rho_two) * jnp.mean(resid * scaled_two, -1, keepdims=True)
        )
        dgain_two = jnp.sum(dnormed_two * resid * rho_two, axis=0, keepdims=True)
        dbranch_low = dresid.astype(bf16)
        dweight_out = dot_tn(mixed_tokens, dbranch_low)

        group, place = n_seq * n_x, y * n_x + x_place

        def core_sum(grad):
            grad = grad.astype(bf16).reshape(n_dp, n_seq, n_x, 2, own_rows, -1)
            keep, send = keep_and_send(grad.transpose(3, 1, 2, 0, 4, 5), core, 0)
            return (keep.astype(f32) + swap(send, "core").astype(f32)).astype(bf16)

        def plane_sum(grad):
            grad = grad.reshape((group,) + grad.shape[2:])
            totals = [lax.dynamic_index_in_dim(grad, place, 0, keepdims=False).astype(f32), 0.0]
            for step in range(1, group):
                block = lax.dynamic_index_in_dim(grad, place ^ step, 0, keepdims=False)
                got = lax.ppermute(block, ("seq", "x"), [(i, i ^ step) for i in range(group)])
                totals[step // n_x] = totals[step // n_x] + got.astype(f32)
            return totals

        def dp_sum(grad):
            return scatter_steps(grad.astype(bf16), DP, z, n_dp)

        dout_part = core_sum(dweight_out)
        dmixed = dot_nt(dbranch_low, out_weight).astype(bf16)
        dmixed_keep = lax.dynamic_slice_in_dim(dmixed, y * half_width, half_width, 1)
        dmixed_send = lax.dynamic_slice_in_dim(dmixed, (1 - y) * half_width, half_width, 1)
        dmixed_heads = in_order(dmixed_keep, swap_seq(dmixed_send), y, 0)
        dmixed_heads = after(dmixed_heads, dout_part)
        dweight_qkv, dnormed_all = attention_backward(
            normed, query, key, value, dmixed_heads, log_sums, qkv_weight, cosine, sine
        )
        dout_sum = dp_sum(sum(plane_sum(dout_part)))
        dnormed_keep = lax.dynamic_slice_in_dim(dnormed_all, y * row_count, row_count, 0)
        dnormed_send = lax.dynamic_slice_in_dim(dnormed_all, (1 - y) * row_count, row_count, 0)
        dnormed = dnormed_keep + swap_seq(dnormed_send.astype(bf16)).astype(f32)
        rho_one = lax.rsqrt(jnp.mean(inputs * inputs, axis=-1, keepdims=True) + norm_eps)
        scaled_one = dnormed * gain_one
        input_gradient = dresid + (
            rho_one * scaled_one
            - inputs * (rho_one * rho_one * rho_one) * jnp.mean(inputs * scaled_one, -1, keepdims=True)
        )
        dgain_one = jnp.sum(dnormed * inputs * rho_one, axis=0, keepdims=True)

        dvector = jnp.concatenate([dgain_one, dgain_two, dconst_one, dconst_two, drouter], axis=0)
        qkv_part = core_sum(dweight_qkv)
        vector_part = core_sum(jnp.pad(dvector.T, ((0, 0), (0, vector_pad))))
        this_y, other_y = plane_sum(jnp.concatenate([qkv_part, vector_part], axis=-1))
        columns = 3 * half_width
        dpack = dp_sum(
            jnp.concatenate(
                [
                    this_y[..., :columns],
                    other_y[..., :columns],
                    this_y[..., columns:] + other_y[..., columns:],
                ],
                axis=-1,
            )
        )
        head_pairs = half_width // 128

        def by_matrix(part):
            part = part.reshape(own_rows, head_pairs, 3, 128)
            return part.transpose(2, 0, 1, 3).reshape(3, own_rows, half_width)

        qkv_sum = in_order(
            by_matrix(dpack[:, :columns]), by_matrix(dpack[:, columns : 2 * columns]), y, 2
        )
        attention_sum = jnp.concatenate([qkv_sum, dout_sum[None]], axis=0)
        vector_sum = dpack[:, 2 * columns :][:, : 4 + NEXP].T

        attention_m, attention_s, attention_u = moments(
            attention_master, attention_first, attention_second, attention_sum
        )
        vector_m, vector_s, vector_u = moments(
            vector_master, vector_first, vector_second, vector_sum
        )
        expert_m, expert_s, expert_u = moments(
            expert_master, expert_first, expert_second, expert_sum
        )

        def squares(attention_x, vector_x, expert_x):
            vector_parts = jnp.sum(vector_x * vector_x, axis=1)
            expert_parts = lax.dynamic_update_slice_in_dim(
                jnp.zeros((NFFN * 3,), f32),
                jnp.sum(expert_x * expert_x, axis=(2, 3)).reshape(-1),
                s * local_experts * 3,
                0,
            )
            return jnp.concatenate(
                [
                    jnp.sum(attention_x * attention_x, axis=(1, 2)),
                    vector_parts[0:2],
                    jnp.sum(vector_parts[2:4])[None],
                    jnp.sum(vector_parts[4:])[None],
                    expert_parts,
                ]
            )

        count = 8 + 3 * NFFN
        small = jnp.concatenate(
            [
                squares(attention_master, vector_master, expert_master),
                squares(attention_u, vector_u, expert_u),
                dmixing.reshape(-1),
            ]
        )
        used = small.shape[0]
        small = jnp.pad(small, (0, -used % 128)).reshape(-1, 128)
        small = sum_everywhere(small, sizes).reshape(-1)
        summed_squares = small[: 2 * count].reshape(2, count)
        mixing_grad = small[2 * count : used].reshape(NEXP, NEXP)
        mixing_m, mixing_s, mixing_u = moments(
            mixing_master, mixing_first, mixing_second, mixing_grad
        )
        mixing_squares = jnp.stack(
            [jnp.sum(mixing_master * mixing_master), jnp.sum(mixing_u * mixing_u)]
        )
        tensor_norms = jnp.sqrt(jnp.concatenate([summed_squares, mixing_squares[:, None]], axis=1))
        ratios = learn_rate * (tensor_norms[0] / (tensor_norms[1] + norm_eps))
        vector_ratio = jnp.concatenate(
            [
                ratios[4:6],
                jnp.broadcast_to(ratios[6:7], (2,)),
                jnp.broadcast_to(ratios[7:8], (NEXP,)),
            ]
        )[:, None]
        expert_ratio = lax.dynamic_slice_in_dim(
            ratios[8:count].reshape(NFFN, 3), s * local_experts, local_experts, 0
        )[:, :, None, None]
        return (
            block_output[None],
            input_gradient[None],
            attention_master - ratios[0:4][:, None, None] * attention_u,
            vector_master - vector_ratio * vector_u,
            expert_master - expert_ratio * expert_u,
            mixing_master - ratios[count] * mixing_u,
            attention_m,
            vector_m,
            expert_m,
            mixing_m,
            attention_s,
            vector_s,
            expert_s,
            mixing_s,
            tensor_norms,
        )

    return shards


def solution(mesh):
    n_dp, n_seq, n_shard = (mesh.shape[name] for name in ("dp", "seq", "shard"))
    finer = jax.sharding.Mesh(
        mesh.devices.reshape(n_dp // 2, 2, n_seq, n_shard // 2, 2), DP + ("seq",) + SHARD
    )
    tokens_spec = P(DP + SHARD, "seq", None)
    attention_spec = P(None, DP + ("seq",) + SHARD, None)
    vector_spec = P(None, DP + ("seq",) + SHARD)
    expert_spec = P(SHARD, None, DP + ("seq",), None)
    weights = (attention_spec, vector_spec, expert_spec, P())
    return jax.shard_map(
        make_shards(dict(finer.shape)),
        mesh=finer,
        in_specs=(tokens_spec,) * 5 + weights * 3,
        out_specs=(tokens_spec,) * 2 + weights * 3 + (P(),),
        check_vma=False,
    )
```

time: 615 us -> 473 us (0.77)
  waiting for transfers between devices: 250 us -> 119 us
  matrix products: 134 us -> 42.2 us
  Pallas kernels: 0 us -> 71.9 us
  blocking collectives: 0 us -> 50.7 us
  other arithmetic: 101 us -> 64 us
  local copies, waits for them, and re-layouts: 47.9 us -> 39.8 us
  starting transfers between devices: 55.4 us -> 62.7 us
    reduce_scatter x2, waiting for transfers between devices: 78 us -> 0.01 us  [sum_rows(): lax.psum_scatter(grad, ('dp_far', 'core'), scatter_dimension=0, tiled=True)]
    pallas_call x0 -> x3, Pallas kernels: none -> 71.9 us  [the longest x1 29.3 us: attention_backward(): pl.pallas_call(attention_backward_kernel, grid=(pairs,), in_specs=[full((...]
    all_gather x1, waiting for transfers between devices: 65.3 us -> 0.01 us  [shards(): lax.all_gather(rows_low, ('dp_far', 'core'), axis=1, tiled=True)]
    all_to_all x0 -> x1, blocking collectives: none -> 50.7 us  [to_experts(): lax.all_to_all(rows, ep_axes, 0, 0, tiled=True).reshape(NFFN * capacity, -1)]
    dot_general x12 -> x0, matrix products: 44.6 us -> none  [the longest x2 14.4 us: attention_backward(): jnp.einsum('hqd,hkd->hqk', dout[:, start:end], value[:, :end], preferred_...]
    ppermute x18 -> x31, waiting for transfers between devices: 78.4 us -> 107 us  [the longest x3 41.2 us: cross(): lax.ppermute(other_y, ('dp_near', 'seq', 'core'), moves)]
    dot_general x9 -> x7, matrix products: 36.4 us -> 14.3 us  [dot_nn(): lax.dot_general(left, right, (((1,), (0,)), ((), ())), preferred_element_...]
    dot_general x6 -> x2, matrix products: 20.2 us -> 3.04 us  [dot_nt(): lax.dot_general(left, right, (((1,), (1,)), ((), ())), preferred_element_...]
  transfers between devices with their start and end apart: 31 -> 42, of which waited for: 20 -> 19; matrix products, arithmetic and copies ran while one was open for 36% -> 23% of each run, Pallas kernels for 0% -> 10%
where the time goes in v2:
time: 473 us; the launch traced here: 466 us
  waiting for transfers between devices  119 us (25%)
  Pallas kernels  71.9 us (15%)
  other arithmetic  64 us (14%)
  starting transfers between devices  62.7 us (13%)
  blocking collectives  50.7 us (11%)
  matrix products  42.2 us (9%)
  local copies, waits for them, and re-layouts  39.8 us (8%)
  between operations  15.4 us (3%)
    all_to_all x1, blocking collectives, to_experts(): lax.all_to_all(rows, ep_axes, 0, 0, tiled=True).reshape(NFFN * capacity, -1)  50.7 us
    ppermute x3, waiting for transfers between devices, cross(): lax.ppermute(other_y, ('dp_near', 'seq', 'core'), moves)  41.2 us
    pallas_call x1, Pallas kernels, attention_backward(): pl.pallas_call(attention_backward_kernel, grid=(pairs,), in_specs=[full((...  29.3 us
    ppermute x9, waiting for transfers between devices, swap(): return lax.ppermute(value, axis_name, [(0, 1), (1, 0)])  25.5 us
    pallas_call x1, Pallas kernels, expert_compute(): pl.pallas_call(expert_kernel, grid=(hidden // FF_COLUMNS,), in_specs=[who...  23.5 us
    dot_general x5, matrix products, dot_tn(): lax.dot_general(left, right, (((0,), (0,)), ((), ())), preferred_element_...  22.4 us
    pallas_call x1, Pallas kernels, attention_forward(): pl.pallas_call(attention_forward_kernel, grid=(pairs,), in_specs=[full((l...  19.1 us
    ppermute x4, waiting for transfers between devices, gather_steps(): lax.ppermute(value, axis_name, [(i, (i + step) % count) for i in range(co...  18.2 us
  transfers between devices with their start and end apart: 42, of which 19 were waited for; matrix products, arithmetic and copies ran while one was open for 23% of the time, Pallas kernels for 10%

profile of v2, /device:TPU:0, one launch (start us, length us, event | category | flops | bytes accessed | tf_op | source)
XLA Modules:
  0.0 465.6 jit_solution(917964223906674713)
XLA Ops:
  9.1 3.0 collective-permute-start
  12.2 2.8 collective-permute-done
  15.0 1.9 collective-permute-start.3
  17.0 2.6 collective-permute-start.4
  20.9 2.7 convert_element_type.274
  23.8 1.6 collective-permute-start.2
  26.2 5.3 %collective-permute-done.4 = bf16[2,24,2048]{2,1,0:T(8,128)(2,1)S(1)} collective-permute-done((bf16[2,24,2048]{2,1,0:T(8,128)(2,1)S(1)}, bf16[2,24,2048]{2,1,0:T(8,128)(2,1)S(1)}, u32[]{:S(2)}, u32[]{:S(2)}) %collective-permute-start.4) | collective-permute-done | bytes 196640 | tf_op jit(solution)/shard_map/ppermute | solution.py:97
  31.6 21.1 %collective-permute-done.2 = bf16[3,96,2048]{2,1,0:T(8,128)(2,1)S(1)} collective-permute-done((bf16[3,96,2048]{2,1,0:T(8,128)(2,1)S(1)}, bf16[3,96,2048]{2,1,0:T(8,128)(2,1)S(1)}, u32[]{:S(2)}, u32[]{:S(2)}) %collective-permute-start.2) | collective-permute-done | bytes 1179680 | tf_op jit(solution)/shard_map/ppermute | solution.py:371
  52.9 1.6 pad_maximum_fusion.1
  59.8 12.9 %collective-permute-done.7 = bf16[4,2,24,2048]{3,2,1,0:T(8,128)(2,1)S(1)} collective-permute-done((bf16[4,2,24,2048]{3,2,1,0:T(8,128)(2,1)S(1)}, bf16[4,2,24,2048]{3,2,1,0:T(8,128)(2,1)S(1)}, u32[]{:S(2)}, u32[]{:S(2)}) %collective-permute-start.7) | collective-permute-done | bytes 786464 | tf_op jit(solution)/shard_map/ppermute | solution.py:97
  72.7 3.2 collective-permute-start.8
  77.5 2.2 convolution_convert_fusion.3
  79.7 4.3 all-to-all-start
  84.0 1.9 fusion.93
  85.9 1.8 pad_maximum_fusion.8
  87.8 1.6 select_bitcast_fusion.1
  96.0 19.1 %shard_map.280 = (bf16[1024,768]{1,0:T(8,128)(2,1)S(1)}, bf16[1024,384]{1,0:T(8,128)(2,1)S(1)}, bf16[1024,384]{1,0:T(8,128)(2,1)S(1)}, bf16[1024,384]{1,0:T(8,12...) custom-call(bf16[1024,768]{1,0:T(8,128)(2,1)S(1)} %pad_maximum_fusion.3.x_ref, ...), custom_call_target="tpu_custom_call" | custom-call | flops 3422552064 | bytes 6291456 | tf_op jit(solution)/shard_map/pallas_call | solution.py:183
  121.1 1.9 collective-permute-start.9
  124.0 7.4 %collective-permute-done.9 = bf16[512,384]{1,0:T(8,128)(2,1)S(1)} collective-permute-done((bf16[512,384]{1,0:T(8,128)(2,1)S(1)}, bf16[512,384]{1,0:T(8,128)(2,1)S(1)}, u32[]{:S(2)}, u32[]{:S(2)}) %collective-permute-start.9) | collective-permute-done | bytes 393248 | tf_op jit(solution)/shard_map/ppermute | solution.py:80
  132.4 2.2 multiply_reduce_fusion.4
  136.9 1.8 fusion.14
  138.8 50.7 %all_to_all.20 = bf16[8,96,896]{2,1,0:T(8,128)(2,1)} all-to-all(bf16[8,96,896]{2,1,0:T(8,128)(2,1)S(1)} %bitcast.291), channel_id=1, replica_groups=mesh['dp_far'=2,'dp_near'=2,'seq'=2,'x'=2,'core'=2] {'dp_near','seq','x'}, dimensions={0} | all-to-all | bytes 2752512 | tf_op jit(solution)/shard_map/all_to_all | solution.py:468
  189.5 23.5 %shard_map.281 = (bf16[768,768]{1,0:T(8,128)(2,1)}, bf16[768,896]{1,0:T(8,128)(2,1)}, bf16[768,2048]{1,0:T(8,128)(2,1)}, bf16[768,2048]{1,0:T(8,128)(2,1)}, bf16...) custom-call(bf16[768,896]{1,0:T(8,128)(2,1)} %bitcast.289, bf16[768,768]{1,0:T(8,128)(2,1)} %bitcast.37.dout_ref, ...), custom_call_target="tpu_custom_call" | custom-call | flops 16911433728 | bytes 18874368 | tf_op jit(solution)/shard_map/pallas_call | solution.py:316
  213.0 5.9 %convolution_convert_fusion.1 = bf16[768,2048]{1,0:T(8,128)(2,1)} fusion(bf16[768,768]{1,0:T(8,128)(2,1)S(1)} %get-tuple-element.57, bf16[768,2048]{1,0:T(8,128)(2,1)} %get-tuple-element.58), kind=kOutput, calls=%fused_computation.19 | convolution fusion | flops 2417491968 | bytes 7471104 | tf_op jit(solution)/shard_map/dot_general | solution.py:40
  218.9 4.3 all-to-all-start.2
  224.0 11.6 %convolution_convert_fusion = bf16[768,4096]{1,0:T(8,128)(2,1)} fusion(bf16[768,2048]{1,0:T(8,128)(2,1)} %get-tuple-element.56, bf16[768,2048]{1,0:T(8,128)(2,1)} %get-tuple-element.55, bf16[768,896]{1,0:T(8,128)(2,1)} %bitcast.290), kind=kOutput, calls=%fused_computation.1 | convolution fusion | flops 4847566848 | bytes 13762560 | tf_op jit(solution)/shard_map/dot_general | solution.py:40
  236.0 2.1 fusion.31
  238.1 6.6 %all-to-all-done.2 = bf16[8,96,896]{2,1,0:T(8,128)(2,1)} async-done(((bf16[8,96,896]{2,1,0:T(8,128)(2,1)}), bf16[8,96,896]{2,1,0:T(8,128)(2,1)}, u32[]{:S(2)}, u32[]{:S(2)}) %all-to-all-start.2) | async-done | bytes 1376288 | tf_op jit(solution)/shard_map/all_to_all | solution.py:468
  244.7 1.6 fusion.62
  246.3 1.6 fusion.59
  248.0 2.5 fusion.56
  250.6 1.7 multiply_reduce_fusion.2
  252.7 2.7 convolution_convert_fusion.4
  259.8 7.9 %all-to-all-start.3 = ((bf16[8,96,768]{2,1,0:T(8,128)(2,1)}), bf16[8,96,768]{2,1,0:T(8,128)(2,1)}, u32[]{:S(2)}, u32[]{:S(2)}) async-start(bf16[8,96,768]{2,1,0:T(8,128)(2,1)} %bitcast.42), calls=%async_computation.3 | async-start | bytes 2359296 | tf_op jit(solution)/shard_map/all_to_all | solution.py:468
  269.3 2.2 fusion.58
  271.5 29.3 %shard_map.282 = (bf16[768,1152]{1,0:T(8,128)(2,1)}, f32[1024,768]{1,0:T(8,128)}) custom-call(bf16[1024,768]{1,0:T(8,128)(2,1)S(1)} %copy-done.8, bf16[1024,384]{1,0:T(8,128)(2,1)S(1)} %copy-done.10, bf16[1024,384]{1,0:T(8,128)(2,1)S(1)} %copy-done.12, bf16[1024,384]{1,0:T(8,128)(2,1)S(1)} %copy-done.14, bf16[1024,384]{1,0:T(8,128)(2,1)S(1)} %pad_maximum_fusion.7.do_ref, ...), custom_call_target="tpu_custom_call" | custom-call | flops 7650410496 | bytes 9437184 | tf_op jit(solution)/shard_map/pallas_call | solution.py:242
  300.8 2.4 dynamic-slice_convert_fusion
  303.2 2.0 collective-permute-start.12
  305.2 2.1 dynamic-slice_bitcast_fusion.2
  308.3 1.9 collective-permute-start.23
  311.8 15.2 %collective-permute-done.12 = bf16[512,768]{1,0:T(8,128)(2,1)S(1)} collective-permute-done((bf16[512,768]{1,0:T(8,128)(2,1)}, bf16[512,768]{1,0:T(8,128)(2,1)S(1)}, u32[]{:S(2)}, u32[]{:S(2)}) %collective-permute-start.12) | collective-permute-done | bytes 786464 | tf_op jit(solution)/shard_map/ppermute | solution.py:80
  327.0 2.4 fusion.24
  329.9 1.6 fusion.13
  331.9 3.0 collective-permute-start.17
  336.0 3.1 collective-permute-start.25
  339.3 2.3 collective-permute-done.17
  341.5 2.2 collective-permute-start.15
  343.7 3.0 collective-permute-done.16
  346.8 2.8 collective-permute-done.15
  350.3 2.7 collective-permute-start.19
  353.4 3.2 collective-permute-done.20
  357.7 10.7 %collective-permute-done.19 = bf16[24,2432]{1,0:T(8,128)(2,1)S(1)} collective-permute-done((bf16[24,2432]{1,0:T(8,128)(2,1)S(1)}, bf16[24,2432]{1,0:T(8,128)(2,1)S(1)}, u32[]{:S(2)}, u32[]{:S(2)}) %collective-permute-start.19) | collective-permute-done | bytes 116768 | tf_op jit(solution)/shard_map/ppermute | solution.py:106
  370.6 1.8 fusion.54
  377.3 2.1 multiply_reduce_fusion.5
  379.4 2.0 dynamic-slice_bitcast_fusion.7
  387.8 5.1 %collective-permute-done.30 = bf16[96,2048]{1,0:T(8,128)(2,1)S(1)} collective-permute-done((bf16[96,2048]{1,0:T(8,128)(2,1)}, bf16[96,2048]{1,0:T(8,128)(2,1)S(1)}, u32[]{:S(2)}, u32[]{:S(2)}) %collective-permute-start.30) | collective-permute-done | bytes 393248 | tf_op jit(solution)/shard_map/ppermute | solution.py:371
  394.8 14.9 %collective-permute-done.28 = bf16[96,4096]{1,0:T(8,128)(2,1)S(1)} collective-permute-done((bf16[96,4096]{1,0:T(8,128)(2,1)S(1)}, bf16[96,4096]{1,0:T(8,128)(2,1)S(1)}, u32[]{:S(2)}, u32[]{:S(2)}) %collective-permute-start.28) | collective-permute-done | bytes 786464 | tf_op jit(solution)/shard_map/ppermute | solution.py:371
  410.1 10.6 %multiply_reduce_fusion = (f32[2,3]{1,0:T(2,128)S(1)}, f32[2,3]{1,0:T(2,128)S(1)}, f32[2,3,96,2048]{3,2,1,0:T(8,128)}, f32[2,3,96,2048]{3,2,1,0:T(8,128)}) fusion(f32[2,3,96,2048]{3,2,1,0:T(8,128)S(1)} %bitcast.273, bf16[2,1,96,2048]{3,2,1,0:T(8,128)(2,1)S(1)} %maximum_bitcast_fusion, bf16[2,1,96,2048]{3,2,1,0:T(8,128)(2,1)S(1)} %get-tuple-element.133, ...), kind=kLoop, calls=%fused_computation.9 | loop fusion | flops 23592948 | bytes 25952304 | tf_op jit(solution)/shard_map/reduce_sum | solution.py:617
  421.3 2.7 concatenate.99
  426.4 2.3 collective-permute-done.32
  430.1 3.3 fusion.21
  433.5 2.3 fusion.39
  437.2 3.7 fusion.50
  447.9 9.8 %multiply_subtract_fusion = f32[2,3,96,2048]{3,2,1,0:T(8,128)} fusion(f32[2,3,96,2048]{3,2,1,0:T(8,128)} %param.24, f32[2,3]{1,0:T(2,128)S(1)} %constant_dynamic-slice_fusion, f32[2,3,96,2048]{3,2,1,0:T(8,128)} %get-tuple-element.119, f32[2,3,96,2048]{3,2,1,0:T(8,128)} %get-tuple-element.118), kind=kLoop, calls=%fused_computation.8 | loop fusion | flops 9437184 | bytes 18874392 | tf_op jit(solution)/shard_map/sub | solution.py:667
  (321 shorter events, 71.8 us)
Async XLA Ops:
  7.2 182.3 %all-gather.2.cloned.1.call-start = ((), (), s32[]{:S(2)}) async-start(), calls=%async_computation.6 | async-start | bytes 11796480 | tf_op jit(solution)/shard_map/all_gather | solution.py:392
  9.1 5.8 %collective-permute-start = (bf16[24,2048]{1,0:T(8,128)(2,1)S(1)}, bf16[24,2048]{1,0:T(8,128)(2,1)S(1)}, u32[]{:S(2)}, u32[]{:S(2)}) collective-permute-start(bf16[24,2048]{1,0:T(8,128)(2,1)S(1)} %get-tuple-element.175), channel_id=1, source_target_pairs={{0,4},{4,0},{1,5},{5,1},{2,6},{6,2},{3,7},{7,3},{8,12},{12,8},{9,1... | collective-permute-start | bytes 294920 | tf_op jit(solution)/shard_map/ppermute | solution.py:80
  15.0 11.2 %collective-permute-start.3 = (bf16[2,24,2048]{2,1,0:T(8,128)(2,1)S(1)}, bf16[2,24,2048]{2,1,0:T(8,128)(2,1)S(1)}, u32[]{:S(2)}, u32[]{:S(2)}) collective-permute-start(bf16[2,24,2048]{2,1,0:T(8,128)(2,1)S(1)} %pad_maximum_fusion.14), channel_id=1, source_target_pairs={{0,8},{8,16},{16,24},{24,0},{1,9},{9,17},{17,25},{25,1},{2,10},{10... | collective-permute-start | bytes 589832 | tf_op jit(solution)/shard_map/ppermute | solution.py:97
  17.0 14.6 %collective-permute-start.4 = (bf16[2,24,2048]{2,1,0:T(8,128)(2,1)S(1)}, bf16[2,24,2048]{2,1,0:T(8,128)(2,1)S(1)}, u32[]{:S(2)}, u32[]{:S(2)}) collective-permute-start(bf16[2,24,2048]{2,1,0:T(8,128)(2,1)S(1)} %pad_maximum_fusion.14), channel_id=1, source_target_pairs={{0,16},{8,24},{16,0},{24,8},{1,17},{9,25},{17,1},{25,9},{2,18},{10... | collective-permute-start | bytes 589832 | tf_op jit(solution)/shard_map/ppermute | solution.py:97
  19.6 12.0 %collective-permute-start.5 = (bf16[2,24,2048]{2,1,0:T(8,128)(2,1)S(1)}, bf16[2,24,2048]{2,1,0:T(8,128)(2,1)S(1)}, u32[]{:S(2)}, u32[]{:S(2)}) collective-permute-start(bf16[2,24,2048]{2,1,0:T(8,128)(2,1)S(1)} %pad_maximum_fusion.14), channel_id=1, source_target_pairs={{0,24},{8,0},{16,8},{24,16},{1,25},{9,1},{17,9},{25,17},{2,26},{10... | collective-permute-start | bytes 589832 | tf_op jit(solution)/shard_map/ppermute | solution.py:97
  23.8 28.9 %collective-permute-start.2 = (bf16[3,96,2048]{2,1,0:T(8,128)(2,1)S(1)}, bf16[3,96,2048]{2,1,0:T(8,128)(2,1)S(1)}, u32[]{:S(2)}, u32[]{:S(2)}) collective-permute-start(bf16[3,96,2048]{2,1,0:T(8,128)(2,1)S(1)} %get-tuple-element.131), channel_id=1, source_target_pairs={{0,4},{1,12},{4,0},{5,8},{8,5},{9,13},{12,1},{13,9},{2,6},{3,14},{... | collective-permute-start | bytes 3538952 | tf_op jit(solution)/shard_map/ppermute | solution.py:371
  25.4 27.3 %collective-permute-start.1 = (bf16[3,96,2048]{2,1,0:T(8,128)(2,1)S(1)}, bf16[3,96,2048]{2,1,0:T(8,128)(2,1)S(1)}, u32[]{:S(2)}, u32[]{:S(2)}) collective-permute-start(bf16[3,96,2048]{2,1,0:T(8,128)(2,1)S(1)} %get-tuple-element.130), channel_id=1, source_target_pairs={{1,8},{8,1},{3,10},{10,3},{5,12},{12,5},{7,14},{14,7},{17,24},{24,... | collective-permute-start | bytes 3538952 | tf_op jit(solution)/shard_map/ppermute | solution.py:362
  55.2 17.5 %collective-permute-start.7 = (bf16[4,2,24,2048]{3,2,1,0:T(8,128)(2,1)S(1)}, bf16[4,2,24,2048]{3,2,1,0:T(8,128)(2,1)S(1)}, u32[]{:S(2)}, u32[]{:S(2)}) collective-permute-start(bf16[4,2,24,2048]{3,2,1,0:T(8,128)(2,1)S(1)} %bitcast_dynamic-update-slice_fusion.2), channel_id=1, source_target_pairs={{0,2},{2,0},{1,3},{3,1},{4,6},{6,4},{5,7},{7,5},{8,10},{10,8},{9,1... | collective-permute-start | bytes 2359304 | tf_op jit(solution)/shard_map/ppermute | solution.py:97
  58.3 18.0 %collective-permute-start.6 = (bf16[512,768]{1,0:T(8,128)(2,1)S(1)}, bf16[512,768]{1,0:T(8,128)(2,1)S(1)}, u32[]{:S(2)}, u32[]{:S(2)}) collective-permute-start(bf16[512,768]{1,0:T(8,128)(2,1)S(1)} %bitcast.274), channel_id=1, source_target_pairs={{0,4},{4,0},{1,5},{5,1},{2,6},{6,2},{3,7},{7,3},{8,12},{12,8},{9,1... | collective-permute-start | bytes 2359304 | tf_op jit(solution)/shard_map/ppermute | solution.py:80
  72.7 15.0 %collective-permute-start.8 = (bf16[2,4,2,24,2048]{4,3,0,2,1:T(8,128)(2,1)S(1)}, bf16[2,4,2,24,2048]{4,3,0,2,1:T(8,128)(2,1)}, u32[]{:S(2)}, u32[]{:S(2)}) collective-permute-start(bf16[2,4,2,24,2048]{4,3,0,2,1:T(8,128)(2,1)S(1)} %bitcast_dynamic-update-slice_fusion.1), channel_id=1, source_target_pairs={{0,1},{1,0},{2,3},{3,2},{4,5},{5,4},{6,7},{7,6},{8,9},{9,8},{10,11... | collective-permute-start | bytes 4718600 | tf_op jit(solution)/shard_map/ppermute | solution.py:80
  79.7 40.3 %all-to-all-start = ((bf16[8,96,768]{2,1,0:T(8,128)(2,1)}), bf16[8,96,768]{2,1,0:T(8,128)(2,1)}, u32[]{:S(2)}, u32[]{:S(2)}) async-start(bf16[8,96,768]{2,1,0:T(8,128)(2,1)} %bitcast.292), calls=%async_computation | async-start | bytes 2359296 | tf_op jit(solution)/shard_map/all_to_all | solution.py:437
  84.0 295.4 %reduce-scatter.5.cloned.1.call-start = ((), (), s32[]{:S(2)}) async-start(), calls=%async_computation.8 | async-start | bytes 3932160 | tf_op jit(solution)/shard_map/reduce_scatter | solution.py:488
  89.9 25.3 %copy-start = (bf16[768,1152]{1,0:T(8,128)(2,1)}, bf16[768,1152]{1,0:T(8,128)(2,1)S(1)}, u32[]{:S(2)}) copy-start(bf16[768,1152]{1,0:T(8,128)(2,1)S(1)} %slice.223.wq_ref.wk_ref.wv_ref) | copy-start | bytes 5308420
  120.0 11.4 %copy-start.2 = (bf16[1024,384]{1,0:T(8,128)(2,1)S(1)}, bf16[1024,384]{1,0:T(8,128)(2,1)}, u32[]{:S(2)}) copy-start(bf16[1024,384]{1,0:T(8,128)(2,1)} %copy-done.1) | copy-start | bytes 2359300
  121.1 10.3 %collective-permute-start.9 = (bf16[512,384]{1,0:T(8,128)(2,1)S(1)}, bf16[512,384]{1,0:T(8,128)(2,1)S(1)}, u32[]{:S(2)}, u32[]{:S(2)}) collective-permute-start(bf16[512,384]{1,0:T(8,128)(2,1)S(1)} %constant_dynamic-slice_fusion.3), channel_id=1, source_target_pairs={{0,4},{4,0},{1,5},{5,1},{2,6},{6,2},{3,7},{7,3},{8,12},{12,8},{9,1... | collective-permute-start | bytes 1179656 | tf_op jit(solution)/shard_map/ppermute | solution.py:80
  123.0 9.3 %copy-start.18 = (bf16[1,512,768]{2,1,0:T(8,128)(2,1)S(1)}, bf16[1,512,768]{2,1,0:T(8,128)(2,1)}, u32[]{:S(2)}) copy-start(bf16[1,512,768]{2,1,0:T(8,128)(2,1)} %param.17) | copy-start | bytes 2359300
  134.5 117.7 %copy-start.15 = (f32[512,768]{1,0:T(8,128)}, f32[512,768]{1,0:T(8,128)S(1)}, u32[]{:S(2)}) copy-start(f32[512,768]{1,0:T(8,128)S(1)} %get-tuple-element.203) | copy-start | bytes 4718596
  218.9 25.8 %all-to-all-start.2 = ((bf16[8,96,896]{2,1,0:T(8,128)(2,1)}), bf16[8,96,896]{2,1,0:T(8,128)(2,1)}, u32[]{:S(2)}, u32[]{:S(2)}) async-start(bf16[8,96,896]{2,1,0:T(8,128)(2,1)} %bitcast.40), calls=%async_computation.2 | async-start | bytes 2752512 | tf_op jit(solution)/shard_map/all_to_all | solution.py:468
  223.3 160.7 %reduce-scatter.3.cloned.1.call-start = ((), (), s32[]{:S(2)}) async-start(), calls=%async_computation.7 | async-start | bytes 7864320 | tf_op jit(solution)/shard_map/reduce_scatter | solution.py:488
  252.7 4.9 %copy-start.27 = (f32[512,768]{1,0:T(8,128)}, f32[512,768]{1,0:T(8,128)S(1)}, u32[]{:S(2)}) copy-start(f32[512,768]{1,0:T(8,128)S(1)} %convert_add_fusion) | copy-start | bytes 4718596
  252.7 4.8 %copy-start.39 = (bf16[512,384]{1,0:T(8,128)(2,1)S(1)}, bf16[512,384]{1,0:T(8,128)(2,1)}, u32[]{:S(2)}) copy-start(bf16[512,384]{1,0:T(8,128)(2,1)} %copy-done.38) | copy-start | bytes 1179652
  252.7 4.8 %copy-start.41 = (bf16[512,384]{1,0:T(8,128)(2,1)S(1)}, bf16[512,384]{1,0:T(8,128)(2,1)}, u32[]{:S(2)}) copy-start(bf16[512,384]{1,0:T(8,128)(2,1)} %copy-done.40) | copy-start | bytes 1179652
  256.4 11.4 %collective-permute-start.10 = (bf16[512,384]{1,0:T(8,128)(2,1)}, bf16[512,384]{1,0:T(8,128)(2,1)}, u32[]{:S(2)}, u32[]{:S(2)}) collective-permute-start(bf16[512,384]{1,0:T(8,128)(2,1)} %constant_dynamic-slice_fusion.2), channel_id=1, source_target_pairs={{0,4},{4,0},{1,5},{5,1},{2,6},{6,2},{3,7},{7,3},{8,12},{12,8},{9,1... | collective-permute-start | bytes 1179656 | tf_op jit(solution)/shard_map/ppermute | solution.py:80
  259.3 10.0 %collective-permute-start.11 = (bf16[2,2,4,24,768]{4,3,1,0,2:T(8,128)(2,1)}, bf16[2,2,4,24,768]{4,3,1,0,2:T(8,128)(2,1)}, u32[]{:S(2)}, u32[]{:S(2)}) collective-permute-start(bf16[2,2,4,24,768]{4,3,1,0,2:T(8,128)(2,1)} %dynamic-slice_bitcast_fusion.5), channel_id=1, source_target_pairs={{0,1},{1,0},{2,3},{3,2},{4,5},{5,4},{6,7},{7,6},{8,9},{9,8},{10,11... | collective-permute-start | bytes 1769480 | tf_op jit(solution)/shard_map/ppermute | solution.py:80
  259.8 11.7 %copy-start.10 = (bf16[1024,384]{1,0:T(8,128)(2,1)S(1)}, bf16[1024,384]{1,0:T(8,128)(2,1)}, u32[]{:S(2)}) copy-start(bf16[1024,384]{1,0:T(8,128)(2,1)} %copy-done.9) | copy-start | bytes 2359300
  259.8 11.7 %copy-start.12 = (bf16[1024,384]{1,0:T(8,128)(2,1)S(1)}, bf16[1024,384]{1,0:T(8,128)(2,1)}, u32[]{:S(2)}) copy-start(bf16[1024,384]{1,0:T(8,128)(2,1)} %copy-done.11) | copy-start | bytes 2359300
  259.8 11.7 %copy-start.14 = (bf16[1024,384]{1,0:T(8,128)(2,1)S(1)}, bf16[1024,384]{1,0:T(8,128)(2,1)}, u32[]{:S(2)}) copy-start(bf16[1024,384]{1,0:T(8,128)(2,1)} %copy-done.13) | copy-start | bytes 2359300
  259.8 173.7 %all-to-all-start.3 = ((bf16[8,96,768]{2,1,0:T(8,128)(2,1)}), bf16[8,96,768]{2,1,0:T(8,128)(2,1)}, u32[]{:S(2)}, u32[]{:S(2)}) async-start(bf16[8,96,768]{2,1,0:T(8,128)(2,1)} %bitcast.42), calls=%async_computation.3 | async-start | bytes 2359296 | tf_op jit(solution)/shard_map/all_to_all | solution.py:468
  300.8 6.9 %copy-start.26 = (bf16[512,768]{1,0:T(8,128)(2,1)S(1)}, bf16[512,768]{1,0:T(8,128)(2,1)}, u32[]{:S(2)}) copy-start(bf16[512,768]{1,0:T(8,128)(2,1)} %copy-done.25) | copy-start | bytes 2359300
  303.2 4.9 %copy-start.31 = (bf16[2,2,4,24,768]{4,3,1,0,2:T(8,128)(2,1)S(1)}, bf16[2,2,4,24,768]{4,3,1,0,2:T(8,128)(2,1)}, u32[]{:S(2)}) copy-start(bf16[2,2,4,24,768]{4,3,1,0,2:T(8,128)(2,1)} %fusion.58) | copy-start | bytes 1769476
  303.2 23.8 %collective-permute-start.12 = (bf16[512,768]{1,0:T(8,128)(2,1)}, bf16[512,768]{1,0:T(8,128)(2,1)S(1)}, u32[]{:S(2)}, u32[]{:S(2)}) collective-permute-start(bf16[512,768]{1,0:T(8,128)(2,1)} %dynamic-slice_convert_fusion), channel_id=1, source_target_pairs={{0,4},{4,0},{1,5},{5,1},{2,6},{6,2},{3,7},{7,3},{8,12},{12,8},{9,1... | collective-permute-start | bytes 2359304 | tf_op jit(solution)/shard_map/ppermute | solution.py:80
  307.4 22.6 %collective-permute-start.13 = (bf16[2,2,4,24,1152]{4,3,1,0,2:T(8,128)(2,1)}, bf16[2,2,4,24,1152]{4,3,1,0,2:T(8,128)(2,1)}, u32[]{:S(2)}, u32[]{:S(2)}) collective-permute-start(bf16[2,2,4,24,1152]{4,3,1,0,2:T(8,128)(2,1)} %dynamic-slice_bitcast_fusion.2), channel_id=1, source_target_pairs={{0,1},{1,0},{2,3},{3,2},{4,5},{5,4},{6,7},{7,6},{8,9},{9,8},{10,11... | collective-permute-start | bytes 2654216 | tf_op jit(solution)/shard_map/ppermute | solution.py:80
  308.3 27.5 %collective-permute-start.23 = (bf16[4,24,768]{2,1,0:T(8,128)(2,1)S(1)}, bf16[4,24,768]{2,1,0:T(8,128)(2,1)S(1)}, u32[]{:S(2)}, u32[]{:S(2)}) collective-permute-start(bf16[4,24,768]{2,1,0:T(8,128)(2,1)S(1)} %get-tuple-element.152), channel_id=1, source_target_pairs={{0,6},{2,4},{4,2},{6,0},{1,7},{3,5},{5,3},{7,1},{8,14},{10,12},{12... | collective-permute-start | bytes 442376 | tf_op jit(solution)/shard_map/ppermute | solution.py:548
  310.2 25.6 %collective-permute-start.22 = (bf16[4,24,768]{2,1,0:T(8,128)(2,1)S(1)}, bf16[4,24,768]{2,1,0:T(8,128)(2,1)S(1)}, u32[]{:S(2)}, u32[]{:S(2)}) collective-permute-start(bf16[4,24,768]{2,1,0:T(8,128)(2,1)S(1)} %get-tuple-element.153), channel_id=1, source_target_pairs={{0,4},{2,6},{4,0},{6,2},{1,5},{3,7},{5,1},{7,3},{8,12},{10,14},{12... | collective-permute-start | bytes 442376 | tf_op jit(solution)/shard_map/ppermute | solution.py:548
  311.3 24.6 %collective-permute-start.21 = (bf16[4,24,768]{2,1,0:T(8,128)(2,1)S(1)}, bf16[4,24,768]{2,1,0:T(8,128)(2,1)S(1)}, u32[]{:S(2)}, u32[]{:S(2)}) collective-permute-start(bf16[4,24,768]{2,1,0:T(8,128)(2,1)S(1)} %get-tuple-element.151), channel_id=1, source_target_pairs={{0,2},{2,0},{4,6},{6,4},{1,3},{3,1},{5,7},{7,5},{8,10},{10,8},{12,... | collective-permute-start | bytes 442376 | tf_op jit(solution)/shard_map/ppermute | solution.py:548
  329.8 1.7 collective-permute-start.14
  331.9 9.7 %collective-permute-start.17 = (bf16[4,24,1280]{2,1,0:T(8,128)(2,1)S(1)}, bf16[4,24,1280]{2,1,0:T(8,128)(2,1)S(1)}, u32[]{:S(2)}, u32[]{:S(2)}) collective-permute-start(bf16[4,24,1280]{2,1,0:T(8,128)(2,1)S(1)} %get-tuple-element.147), channel_id=1, source_target_pairs={{0,6},{2,4},{4,2},{6,0},{1,7},{3,5},{5,3},{7,1},{8,14},{10,12},{12... | collective-permute-start | bytes 737288 | tf_op jit(solution)/shard_map/ppermute | solution.py:548
  334.8 11.9 %collective-permute-start.16 = (bf16[4,24,1280]{2,1,0:T(8,128)(2,1)S(1)}, bf16[4,24,1280]{2,1,0:T(8,128)(2,1)S(1)}, u32[]{:S(2)}, u32[]{:S(2)}) collective-permute-start(bf16[4,24,1280]{2,1,0:T(8,128)(2,1)S(1)} %get-tuple-element.148), channel_id=1, source_target_pairs={{0,4},{2,6},{4,0},{6,2},{1,5},{3,7},{5,1},{7,3},{8,12},{10,14},{12... | collective-permute-start | bytes 737288 | tf_op jit(solution)/shard_map/ppermute | solution.py:548
  335.9 17.1 %collective-permute-start.26 = (bf16[24,768]{1,0:T(8,128)(2,1)S(1)}, bf16[24,768]{1,0:T(8,128)(2,1)S(1)}, u32[]{:S(2)}, u32[]{:S(2)}) collective-permute-start(bf16[24,768]{1,0:T(8,128)(2,1)S(1)} %get-tuple-element.161), channel_id=1, source_target_pairs={{0,24},{8,0},{16,8},{24,16},{1,25},{9,1},{17,9},{25,17},{2,26},{10... | collective-permute-start | bytes 110600 | tf_op jit(solution)/shard_map/ppermute | solution.py:106
  336.0 17.0 %collective-permute-start.25 = (bf16[24,768]{1,0:T(8,128)(2,1)S(1)}, bf16[24,768]{1,0:T(8,128)(2,1)S(1)}, u32[]{:S(2)}, u32[]{:S(2)}) collective-permute-start(bf16[24,768]{1,0:T(8,128)(2,1)S(1)} %get-tuple-element.162), channel_id=1, source_target_pairs={{0,16},{8,24},{16,0},{24,8},{1,17},{9,25},{17,1},{25,9},{2,18},{10... | collective-permute-start | bytes 110600 | tf_op jit(solution)/shard_map/ppermute | solution.py:106
  339.1 13.9 %collective-permute-start.24 = (bf16[24,768]{1,0:T(8,128)(2,1)S(1)}, bf16[24,768]{1,0:T(8,128)(2,1)S(1)}, u32[]{:S(2)}, u32[]{:S(2)}) collective-permute-start(bf16[24,768]{1,0:T(8,128)(2,1)S(1)} %get-tuple-element.160), channel_id=1, source_target_pairs={{0,8},{8,16},{16,24},{24,0},{1,9},{9,17},{17,25},{25,1},{2,10},{10... | collective-permute-start | bytes 110600 | tf_op jit(solution)/shard_map/ppermute | solution.py:106
  341.5 8.0 %collective-permute-start.15 = (bf16[4,24,1280]{2,1,0:T(8,128)(2,1)S(1)}, bf16[4,24,1280]{2,1,0:T(8,128)(2,1)S(1)}, u32[]{:S(2)}, u32[]{:S(2)}) collective-permute-start(bf16[4,24,1280]{2,1,0:T(8,128)(2,1)S(1)} %get-tuple-element.146), channel_id=1, source_target_pairs={{0,2},{2,0},{4,6},{6,4},{1,3},{3,1},{5,7},{7,5},{8,10},{10,8},{12,... | collective-permute-start | bytes 737288 | tf_op jit(solution)/shard_map/ppermute | solution.py:548
  349.8 6.9 %collective-permute-start.20 = (bf16[24,2432]{1,0:T(8,128)(2,1)S(1)}, bf16[24,2432]{1,0:T(8,128)(2,1)S(1)}, u32[]{:S(2)}, u32[]{:S(2)}) collective-permute-start(bf16[24,2432]{1,0:T(8,128)(2,1)S(1)} %get-tuple-element.155), channel_id=1, source_target_pairs={{0,24},{8,0},{16,8},{24,16},{1,25},{9,1},{17,9},{25,17},{2,26},{10... | collective-permute-start | bytes 350216 | tf_op jit(solution)/shard_map/ppermute | solution.py:106
  350.3 18.1 %collective-permute-start.19 = (bf16[24,2432]{1,0:T(8,128)(2,1)S(1)}, bf16[24,2432]{1,0:T(8,128)(2,1)S(1)}, u32[]{:S(2)}, u32[]{:S(2)}) collective-permute-start(bf16[24,2432]{1,0:T(8,128)(2,1)S(1)} %get-tuple-element.156), channel_id=1, source_target_pairs={{0,16},{8,24},{16,0},{24,8},{1,17},{9,25},{17,1},{25,9},{2,18},{10... | collective-permute-start | bytes 350216 | tf_op jit(solution)/shard_map/ppermute | solution.py:106
  353.0 16.5 %collective-permute-start.18 = (bf16[24,2432]{1,0:T(8,128)(2,1)S(1)}, bf16[24,2432]{1,0:T(8,128)(2,1)S(1)}, u32[]{:S(2)}, u32[]{:S(2)}) collective-permute-start(bf16[24,2432]{1,0:T(8,128)(2,1)S(1)} %get-tuple-element.157), channel_id=1, source_target_pairs={{0,8},{8,16},{16,24},{24,0},{1,9},{9,17},{17,25},{25,1},{2,10},{10... | collective-permute-start | bytes 350216 | tf_op jit(solution)/shard_map/ppermute | solution.py:106
  375.2 72.0 %copy-start.46 = (f32[16,24]{1,0:T(8,128)}, f32[16,24]{1,0:T(8,128)S(1)}, u32[]{:S(2)}) copy-start(f32[16,24]{1,0:T(8,128)S(1)} %get-tuple-element.120) | copy-start | bytes 4612
  375.2 72.0 %copy-start.47 = (f32[16,24]{1,0:T(8,128)}, f32[16,24]{1,0:T(8,128)S(1)}, u32[]{:S(2)}) copy-start(f32[16,24]{1,0:T(8,128)S(1)} %get-tuple-element.121) | copy-start | bytes 4612
  379.4 30.7 %slice-start = ((s8[4718592]{0:T(1024)(128)(4,1)}), s8[524288]{0:T(1024)(128)(4,1)S(1)}, s32[]{:S(2)}) async-start(s8[4718592]{0:T(1024)(128)(4,1)} %bitcast.272), calls=%async_computation.9 | async-start | bytes 1048576
  381.4 11.5 %collective-permute-start.30 = (bf16[96,2048]{1,0:T(8,128)(2,1)}, bf16[96,2048]{1,0:T(8,128)(2,1)S(1)}, u32[]{:S(2)}, u32[]{:S(2)}) collective-permute-start(bf16[96,2048]{1,0:T(8,128)(2,1)} %get-tuple-element.150), channel_id=1, source_target_pairs={{0,4},{1,12},{4,0},{5,8},{8,5},{9,13},{12,1},{13,9},{2,6},{3,14},{... | collective-permute-start | bytes 1179656 | tf_op jit(solution)/shard_map/ppermute | solution.py:371
  382.5 11.2 %collective-permute-start.29 = (bf16[96,2048]{1,0:T(8,128)(2,1)S(1)}, bf16[96,2048]{1,0:T(8,128)(2,1)}, u32[]{:S(2)}, u32[]{:S(2)}) collective-permute-start(bf16[96,2048]{1,0:T(8,128)(2,1)S(1)} %get-tuple-element.149), channel_id=1, source_target_pairs={{1,8},{8,1},{3,10},{10,3},{5,12},{12,5},{7,14},{14,7},{17,24},{24,... | collective-permute-start | bytes 1179656 | tf_op jit(solution)/shard_map/ppermute | solution.py:362
  385.4 24.3 %collective-permute-start.28 = (bf16[96,4096]{1,0:T(8,128)(2,1)S(1)}, bf16[96,4096]{1,0:T(8,128)(2,1)S(1)}, u32[]{:S(2)}, u32[]{:S(2)}) collective-permute-start(bf16[96,4096]{1,0:T(8,128)(2,1)S(1)} %get-tuple-element.135), channel_id=1, source_target_pairs={{0,4},{1,12},{4,0},{5,8},{8,5},{9,13},{12,1},{13,9},{2,6},{3,14},{... | collective-permute-start | bytes 2359304 | tf_op jit(solution)/shard_map/ppermute | solution.py:371
  386.4 23.4 %collective-permute-start.27 = (bf16[96,4096]{1,0:T(8,128)(2,1)S(1)}, bf16[96,4096]{1,0:T(8,128)(2,1)S(1)}, u32[]{:S(2)}, u32[]{:S(2)}) collective-permute-start(bf16[96,4096]{1,0:T(8,128)(2,1)S(1)} %get-tuple-element.134), channel_id=1, source_target_pairs={{1,8},{8,1},{3,10},{10,3},{5,12},{12,5},{7,14},{14,7},{17,24},{24,... | collective-permute-start | bytes 2359304 | tf_op jit(solution)/shard_map/ppermute | solution.py:362
  394.8 15.3 %slice-start.1 = ((s8[4718592]{0:T(1024)(128)(4,1)}), s8[4194304]{0:T(1024)(128)(4,1)S(1)}, s32[]{:S(2)}) async-start(s8[4718592]{0:T(1024)(128)(4,1)} %bitcast.272), calls=%async_computation.10 | async-start | bytes 8388608
  410.1 20.1 %copy-start.28 = (f32[512,768]{1,0:T(8,128)S(1)}, f32[512,768]{1,0:T(8,128)}, u32[]{:S(2)}) copy-start(f32[512,768]{1,0:T(8,128)} %copy-done.27) | copy-start | bytes 4718596
  424.0 1.2 collective-permute-start.31
  425.2 3.6 collective-permute-start.32
  428.7 4.7 %collective-permute-start.33 = (f32[2,128]{1,0:T(2,128)S(1)}, f32[2,128]{1,0:T(2,128)S(1)}, u32[]{:S(2)}, u32[]{:S(2)}) collective-permute-start(f32[2,128]{1,0:T(2,128)S(1)} %fusion.170), channel_id=1, source_target_pairs={{0,4},{4,0},{1,5},{5,1},{2,6},{6,2},{3,7},{7,3},{8,12},{12,8},{9,1... | collective-permute-start | bytes 3080 | tf_op jit(solution)/shard_map/ppermute | solution.py:122
  433.5 3.6 collective-permute-start.34
  437.0 7.9 %copy-start.34 = (f32[4,24,768]{2,1,0:T(8,128)S(1)}, f32[4,24,768]{2,1,0:T(8,128)}, u32[]{:S(2)}) copy-start(f32[4,24,768]{2,1,0:T(8,128)} %get-tuple-element.122) | copy-start | bytes 884740
  437.1 7.9 %copy-start.35 = (f32[4,24,768]{2,1,0:T(8,128)S(1)}, f32[4,24,768]{2,1,0:T(8,128)}, u32[]{:S(2)}) copy-start(f32[4,24,768]{2,1,0:T(8,128)} %get-tuple-element.123) | copy-start | bytes 884740
  437.1 4.5 collective-permute-start.35
  442.5 15.2 %copy-start.48 = (f32[12,12]{1,0:T(8,128)}, f32[12,12]{1,0:T(8,128)S(1)}, u32[]{:S(2)}) copy-start(f32[12,12]{1,0:T(8,128)S(1)} %get-tuple-element.116) | copy-start | bytes 1732
  442.5 15.2 %copy-start.49 = (f32[12,12]{1,0:T(8,128)}, f32[12,12]{1,0:T(8,128)S(1)}, u32[]{:S(2)}) copy-start(f32[12,12]{1,0:T(8,128)S(1)} %get-tuple-element.117) | copy-start | bytes 1732
  444.0 13.6 %copy-start.54 = (f32[2,33]{1,0:T(2,128)}, f32[2,33]{1,0:T(2,128)S(1)}, u32[]{:S(2)}) copy-start(f32[2,33]{1,0:T(2,128)S(1)} %maximum_sqrt_fusion) | copy-start | bytes 796
  (36 other events, 68.3 us)
Sparse Core Ops, SparseCore 0:
  54.6 120.2 all-gather.1
  219.1 53.1 reduce-scatter.4
  274.9 105.2 reduce-scatter.2

commit v3 on v2

--- a/solution.py
+++ b/solution.py
@@ -1,7 +1,9 @@
 import jax
 import jax.numpy as jnp
+import numpy as np
 from jax import lax
 from jax.experimental import pallas as pl
+from jax.experimental.layout import Layout, with_layout_constraint
 from jax.experimental.pallas import tpu as pltpu
 from jax.sharding import PartitionSpec as P
 
@@ -41,12 +43,13 @@
 
 
 def rotary_tables(length):
-    freqs = rope_base ** (-jnp.arange(0, HDIM, 2).astype(f32) / HDIM)
-    angles = jnp.arange(length).astype(f32)[:, None] * freqs[None, :]
-    cosine, sine = jnp.cos(angles), jnp.sin(angles)
+    freqs = np.float32(rope_base) ** (-np.arange(0, HDIM, 2).astype(np.float32) / np.float32(HDIM))
+    angles = np.arange(length).astype(np.float32)[:, None] * freqs[None, :]
+    cosine = np.cos(angles.astype(np.float64)).astype(np.float32)
+    sine = np.sin(angles.astype(np.float64)).astype(np.float32)
     return (
-        jnp.concatenate([cosine] * 4, axis=-1),
-        jnp.concatenate([-sine, sine, -sine, sine], axis=-1),
+        jnp.asarray(np.concatenate([cosine] * 4, axis=-1)),
+        jnp.asarray(np.concatenate([-sine, sine, -sine, sine], axis=-1)),
     )
 
 
@@ -99,12 +102,14 @@
     return out
 
 
-def scatter_steps(value, axis_name, place, count):
+def scatter_steps(value, axis_name, place, count, wait_for=()):
     total = lax.dynamic_index_in_dim(value, place, 0, keepdims=False).astype(f32)
+    got = []
     for step in range(1, count):
         block = lax.dynamic_index_in_dim(value, (place + step) % count, 0, keepdims=False)
-        got = lax.ppermute(block, axis_name, [(i, (i + step) % count) for i in range(count)])
-        total = total + got.astype(f32)
+        got.append(lax.ppermute(block, axis_name, [(i, (i + step) % count) for i in range(count)]))
+    for part in after(got, wait_for):
+        total = total + part.astype(f32)
     return total
 
 
@@ -116,13 +121,22 @@
 
 
 def sum_everywhere(value, sizes):
-    for axis_name in ("core", "x", "seq", "dp_near", "dp_far"):
-        bit = 1
-        while bit < sizes[axis_name]:
-            value = value + lax.ppermute(
-                value, axis_name, [(i, i ^ bit) for i in range(sizes[axis_name])]
-            )
-            bit *= 2
+    for axis_names in (("core",), ("seq", "x"), DP):
+        count = 1
+        for name in axis_names:
+            count *= sizes[name]
+        rounds = [[1 << bit] for bit in range(count.bit_length() - 1)]
+        if count <= 4:
+            rounds = [range(1, count)]
+        for steps in rounds:
+            got = [
+                lax.ppermute(value, axis_names, [(i, i ^ step) for i in range(count)])
+                for step in steps
+            ]
+            if len(got) == 3:
+                value = (value + got[0]) + (got[1] + got[2])
+            else:
+                value = value + got[0]
     return value
 
 
@@ -190,7 +204,7 @@
         cost_estimate=pl.CostEstimate(flops=6 * length * width * half + 4 * length * length * half, bytes_accessed=8 * length * width, transcendentals=length * length * half // HDIM),
     )(x, gain, weight, weight, weight, cos, sin)
 
-def attention_backward_kernel(h_ref, q_ref, k_ref, v_ref, do_ref, lse_ref, wq_ref, wk_ref, wv_ref, cos_ref, sin_ref, dw_ref, dh_ref, dq_scr, dk_scr, dv_scr):
+def attention_backward_kernel(h_ref, x_ref, vector_ref, q_ref, k_ref, v_ref, do_ref, lse_ref, wq_ref, wk_ref, wv_ref, cos_ref, sin_ref, dw_ref, dh_ref, dq_scr, dk_scr, dv_scr):
     length = h_ref.shape[0]
     step = pl.program_id(0)
     behind = lax.broadcasted_iota(jnp.int32, (QUERY_ROWS, QUERY_ROWS), 0) > lax.broadcasted_iota(jnp.int32, (QUERY_ROWS, QUERY_ROWS), 1)
@@ -221,7 +235,9 @@
     dvb = dv_scr[...].astype(bf16)
     d = jnp.concatenate([dqp, dkp, dvb], axis=1)
     w = jnp.concatenate([wq_ref[...], wk_ref[...], wv_ref[...]], axis=1)
-    dw_ref[...] = dot_tn(h_ref[...], d).astype(bf16)
+    columns = d.shape[1]
+    place = pl.ds(pl.multiple_of(step * columns, 128), columns)
+    dw_ref[:, place] = dot_tn(h_ref[...], d).astype(bf16)
     dh = dot_nt(d, w)
 
     @pl.when(step == 0)
@@ -232,7 +248,20 @@
     def _():
         dh_ref[...] += dh
 
-def attention_backward(h, q, k, v, do, lse, weight, cos, sin):
+    @pl.when(step == pl.num_programs(0) - 1)
+    def _():
+        dgain = jnp.zeros((1, x_ref.shape[1]), f32)
+        for start in range(0, length, QUERY_ROWS):
+            rows = pl.ds(start, QUERY_ROWS)
+            x = x_ref[rows, :].astype(f32)
+            rho = lax.rsqrt(jnp.mean(x * x, axis=-1, keepdims=True) + norm_eps)
+            dgain += jnp.sum(dh_ref[rows, :] * (x * rho), axis=0, keepdims=True)
+        turned = jnp.broadcast_to(dgain, (128, x_ref.shape[1])).T
+        lane = lax.broadcasted_iota(jnp.int32, turned.shape, 1)
+        vectors = jnp.where(lane == 0, turned, vector_ref[...])
+        dw_ref[:, dw_ref.shape[1] - 128 :] = vectors.astype(bf16)
+
+def attention_backward(h, x, vectors, q, k, v, do, lse, weight, cos, sin):
     length, width = h.shape
     half = weight.shape[1] // 3
     pairs = half // 128
@@ -242,62 +271,84 @@
     return pl.pallas_call(
         attention_backward_kernel,
         grid=(pairs,),
-        in_specs=[full((length, width)), out_col, out_col, out_col, out_col, pl.BlockSpec((1, 2, length), lambda p: (p, 0, 0)), col(0), col(pairs), col(2 * pairs), full((length, 128)), full((length, 128))],
-        out_specs=[pl.BlockSpec((width, 384), lambda p: (0, p)), full((length, width))],
-        out_shape=[jax.ShapeDtypeStruct((width, 3 * half), bf16), jax.ShapeDtypeStruct((length, width), f32)],
+        in_specs=[full((length, width)), full((length, width)), full((width, 128)), out_col, out_col, out_col, out_col, pl.BlockSpec((1, 2, length), lambda p: (p, 0, 0)), col(0), col(pairs), col(2 * pairs), full((length, 128)), full((length, 128))],
+        out_specs=[full((width, 3 * half + 128)), full((length, width))],
+        out_shape=[jax.ShapeDtypeStruct((width, 3 * half + 128), bf16), jax.ShapeDtypeStruct((length, width), f32)],
         scratch_shapes=[pltpu.VMEM((length, 128), f32)] * 3,
         compiler_params=pltpu.CompilerParams(vmem_limit_bytes=48 * 2**20),
         cost_estimate=pl.CostEstimate(flops=12 * length * width * half + 10 * length * length * half, bytes_accessed=12 * length * width, transcendentals=length * length * half // HDIM),
-    )(h, q, k, v, do, lse, weight, weight, weight, cos, sin)
-
-
-def three_parts(value):
-    high = value.astype(bf16)
-    rest = value - high.astype(f32)
-    middle = rest.astype(bf16)
-    low = (rest - middle.astype(f32)).astype(bf16)
-    lane = lax.broadcasted_iota(jnp.int32, (value.shape[0], 128), 1)
-    zero = jnp.zeros((), bf16)
-    return jnp.where(lane == 0, high, jnp.where(lane == 1, middle, jnp.where(lane == 2, low, zero)))
-
-def three_parts_rounded(value):
+    )(h, x, vectors, q, k, v, do, lse, weight, weight, weight, cos, sin)
+
+
+def gate_columns(value, which):
     high = lax.reduce_precision(value, 8, 7)
     middle = lax.reduce_precision(value - high, 8, 7)
     low = lax.reduce_precision(value - high - middle, 8, 7)
     lane = lax.broadcasted_iota(jnp.int32, (value.shape[0], 128), 1)
-    return (
-        jnp.where(lane == 0, high, 0.0)
-        + jnp.where(lane == 1, middle, 0.0)
-        + jnp.where(lane == 2, low, 0.0)
-    ).astype(bf16)
-
-
-def expert_kernel(taken_ref, dout_ref, weight_ref, f_ref, dtaken_ref, hidden_ref, dgate_ref, dup_ref, dresult_ref, f_acc, d_acc):
+    columns = jnp.where(lane == 3, 1.0 * which, 0.0)
+    for part, place in ((high, 0), (middle, 1), (low, 2)):
+        columns = jnp.where(lane == place + 4 * which, part, columns)
+    return columns.astype(bf16)
+
+
+def expert_kernel(
+    flipped_ref,
+    taken_ref,
+    dout_ref,
+    same_ref,
+    other_ref,
+    f_ref,
+    dtaken_ref,
+    right_ref,
+    dresult_ref,
+    weight_ref,
+    f_acc,
+    d_acc,
+):
     step, last = pl.program_id(0), pl.num_programs(0) - 1
     width = dout_ref.shape[1]
 
     @pl.when(step == 0)
     def _():
-        parts = taken_ref[:, width:].astype(f32)
-        gate = jnp.sum(parts, axis=1, keepdims=True)
+        lanes = taken_ref[:, width:].astype(f32)
+        lane = lax.broadcasted_iota(jnp.int32, lanes.shape, 1)
+        gate = jnp.sum(jnp.where(lane == 3, 0.0, lanes), axis=1, keepdims=True)
         dresult_ref[...] = (gate * dout_ref[...].astype(f32)).astype(bf16)
-        f_acc[...] = jnp.zeros_like(f_acc)
-        d_acc[...] = jnp.zeros_like(d_acc)
-
+
+    eighth = width // 8
+    shift = flipped_ref[0] * eighth
+    for matrix in range(3):
+        for pair in range(4):
+            rows = slice(pair * eighth, (pair + 1) * eighth)
+            base = 2 * pair * eighth
+            place = pl.ds(pl.multiple_of(base + shift, 32), eighth)
+            weight_ref[matrix, place, :] = same_ref[matrix, rows, :]
+            place = pl.ds(pl.multiple_of(base + eighth - shift, 32), eighth)
+            weight_ref[matrix, place, :] = other_ref[matrix, rows, :]
     taken = taken_ref[:, :width]
     a = dot_nn(taken, weight_ref[0])
     b = dot_nn(taken, weight_ref[1])
     sig = jax.nn.sigmoid(a)
     act = a * sig
     hidden = (act * b).astype(bf16)
-    hidden_ref[...] = hidden
-    f_acc[...] += dot_nt(hidden, weight_ref[2])
+    right_ref[2] = hidden
     dhidden = dot_nn(dresult_ref[...], weight_ref[2])
     dgate = (dhidden * b * (sig * (1.0 + a - act))).astype(bf16)
     dup = (dhidden * act).astype(bf16)
-    dgate_ref[...] = dgate
-    dup_ref[...] = dup
-    d_acc[...] += dot_nt(dgate, weight_ref[0]) + dot_nt(dup, weight_ref[1])
+    right_ref[0] = dgate
+    right_ref[1] = dup
+    f = dot_nt(hidden, weight_ref[2])
+    d = dot_nt(dgate, weight_ref[0]) + dot_nt(dup, weight_ref[1])
+
+    @pl.when(step == 0)
+    def _():
+        f_acc[...] = f
+        d_acc[...] = d
+
+    @pl.when(step > 0)
+    def _():
+        f_acc[...] += f
+        d_acc[...] += d
 
     @pl.when(step == last)
     def _():
@@ -305,24 +356,93 @@
         f_ref[...] = f
         dtaken_ref[:, :width] = d_acc[...].astype(bf16)
         dpicked = jnp.sum(dout_ref[...].astype(f32) * f.astype(f32), axis=1, keepdims=True)
-        dtaken_ref[:, width:] = three_parts(dpicked)
-
-def expert_compute(taken, dout, weight):
+        high = dpicked.astype(bf16).astype(f32)
+        middle = (dpicked - high).astype(bf16).astype(f32)
+        low = (dpicked - high - middle).astype(bf16).astype(f32)
+        lanes = taken_ref[:, width:].astype(f32)
+        lane = lax.broadcasted_iota(jnp.int32, lanes.shape, 1)
+        second = jnp.sum(jnp.where(lane == 3, lanes, 0.0), axis=1, keepdims=True)
+        mine = jnp.where(lane < 3, 1.0 - second, jnp.where((lane > 3) & (lane < 7), second, 0.0))
+        part = jnp.where(lane % 4 == 0, high, jnp.where(lane % 4 == 1, middle, low))
+        dtaken_ref[:, width:] = (mine * part).astype(bf16)
+
+
+def expert_compute(flipped, taken, dout, same, other):
     rows, width = dout.shape
-    hidden = weight.shape[2]
+    hidden = same.shape[2]
+    half = pl.BlockSpec((3, width // 2, FF_COLUMNS), lambda i: (0, 0, i))
     whole = lambda columns: pl.BlockSpec((rows, columns), lambda i: (0, 0))
-    part = pl.BlockSpec((rows, FF_COLUMNS), lambda i: (0, i))
     shape = lambda columns: jax.ShapeDtypeStruct((rows, columns), bf16)
     return pl.pallas_call(
         expert_kernel,
         grid=(hidden // FF_COLUMNS,),
-        in_specs=[whole(width + 128), whole(width), pl.BlockSpec((3, width, FF_COLUMNS), lambda i: (0, 0, i))],
-        out_specs=[whole(width), whole(width + 128), part, part, part, whole(width)],
-        out_shape=[shape(width), shape(width + 128), shape(hidden), shape(hidden), shape(hidden), shape(width)],
-        scratch_shapes=[pltpu.VMEM((rows, width), f32)] * 2,
+        in_specs=[
+            pl.BlockSpec(memory_space=pltpu.SMEM),
+            whole(width + 128),
+            whole(width),
+            half,
+            half,
+        ],
+        out_specs=[
+            whole(width),
+            whole(width + 128),
+            pl.BlockSpec((3, rows, FF_COLUMNS), lambda i: (0, 0, i)),
+            whole(width),
+        ],
+        out_shape=[
+            shape(width),
+            shape(width + 128),
+            jax.ShapeDtypeStruct((3, rows, hidden), bf16),
+            shape(width),
+        ],
+        scratch_shapes=[pltpu.VMEM((3, width, FF_COLUMNS), bf16)] + [pltpu.VMEM((rows, width), f32)] * 2,
         compiler_params=pltpu.CompilerParams(vmem_limit_bytes=48 * 2**20),
-        cost_estimate=pl.CostEstimate(flops=14 * rows * width * hidden, bytes_accessed=6 * width * hidden + 6 * rows * hidden, transcendentals=rows * hidden),
-    )(taken, dout, weight)
+        cost_estimate=pl.CostEstimate(
+            flops=14 * rows * width * hidden,
+            bytes_accessed=6 * width * hidden + 6 * rows * hidden,
+            transcendentals=rows * hidden,
+        ),
+    )(flipped, taken, dout, same, other)
+
+
+def gradient_kernel(taken_ref, dresult_ref, right_ref, out_ref, turned):
+    step, first_down = pl.program_id(0), 2 * pl.num_programs(0) // 3
+    width = dresult_ref.shape[1]
+
+    @pl.when(step == 0)
+    def _():
+        turned[...] = taken_ref[:, :width].T
+
+    @pl.when(step == first_down)
+    def _():
+        turned[...] = dresult_ref[...].T
+
+    out_ref[...] = dot_nn(turned[...], right_ref[0]).astype(bf16)
+
+
+def weight_gradients(taken, dresult, right):
+    rows, width = dresult.shape
+    columns = right.shape[2]
+    tile = min(columns, 2 * FF_COLUMNS)
+    steps = columns // tile
+    return pl.pallas_call(
+        gradient_kernel,
+        grid=(3 * steps,),
+        in_specs=[
+            pl.BlockSpec((rows, taken.shape[1]), lambda i: (0, 0)),
+            pl.BlockSpec((rows, width), lambda i: (0, 0)),
+            pl.BlockSpec((1, rows, tile), lambda i: (i // steps, 0, i % steps)),
+        ],
+        out_specs=pl.BlockSpec((width, tile), lambda i: (0, i)),
+        out_shape=jax.ShapeDtypeStruct((width, 3 * columns), bf16),
+        scratch_shapes=[pltpu.VMEM((width, rows), bf16)],
+        compiler_params=pltpu.CompilerParams(vmem_limit_bytes=58 * 2**20),
+        cost_estimate=pl.CostEstimate(
+            flops=6 * rows * width * columns,
+            bytes_accessed=6 * (rows + width) * columns,
+            transcendentals=0,
+        ),
+    )(taken, dresult, right)
 
 
 def make_shards(sizes):
@@ -356,6 +476,7 @@
         local_experts = expert_master.shape[0]
         spread = local_experts == 2 and n_x == 2 and sizes["dp_far"] == 2
         ep_axes = ("dp_near", "seq", "x") if spread else SHARD
+        ep_place = lax.axis_index(ep_axes)
         own_rows = attention_master.shape[1]
 
         def cross(same_y, other_y):
@@ -383,18 +504,27 @@
             )
 
         packed = in_order(weight_pack(y)[None], swap_seq(weight_pack(1 - y))[None], y, 0)
+
         packed_z = gather_steps(packed, DP, z, n_dp)
-
+        packed_x = gather_steps(packed_z, "x", x_place, n_x)
         expert_low = after(expert_master, packed).astype(bf16)
         if spread:
-            rows_low = in_order(*cross(*keep_and_send(expert_low, y, 0)), y, 1)
-            rows_low = after(rows_low, packed_z)
-            expert_use = lax.all_gather(rows_low, ("dp_far", "core"), axis=1, tiled=True)
+            same_y, other_y = cross(*keep_and_send(expert_low, y, 0))
+            expert_same = lax.all_gather(
+                after(same_y, packed_z), ("dp_far", "core"), axis=1, tiled=True
+            )
+            expert_other = lax.all_gather(
+                after(other_y, packed_z), ("dp_far", "core"), axis=1, tiled=True
+            )
+            flipped = y
         else:
-            rows_low = expert_low[0]
-            expert_use = lax.all_gather(rows_low, DP + ("seq",), axis=1, tiled=True)
-
-        packed = gather_steps(packed_z, "x", x_place, n_x)
+            expert_use = lax.all_gather(expert_low[0], DP + ("seq",), axis=1, tiled=True)
+            expert_use = expert_use.reshape(3, 4, 2, model_width // 8, -1)
+            expert_same = expert_use[:, :, 0].reshape(3, model_width // 2, -1)
+            expert_other = expert_use[:, :, 1].reshape(3, model_width // 2, -1)
+            flipped = jnp.zeros_like(y)
+
+        packed = packed_x
         packed = in_order(packed[None], swap(packed, "core")[None], core, 0)
         packed = packed.transpose(2, 3, 1, 0, 4, 5).reshape(model_width, -1)
         qkv_weight = packed[:, : 3 * half_width]
@@ -418,13 +548,14 @@
             route = route_rows[:, j : j + 1]
             keep = (route < NFFN) & (slot < capacity)
             block = ((route // 2) % 2) * 4 + (route % 2) * 2 + route // 4 if spread else route
+            block = block ^ ep_place
             kept.append(keep)
             dispatch.append(
                 ((block_ids == block * capacity + slot) & keep).astype(bf16)
             )
         dispatch_both = dispatch[0] + dispatch[1]
 
-        tokens_all = in_order(tokens[0], swap_seq(after(tokens[0], rows_low)), y, 0)
+        tokens_all = in_order(tokens[0], swap_seq(tokens[0]), y, 0)
         gain_one = vector_all[0].astype(f32)[None, :]
         gain_two = vector_all[1].astype(f32)[None, :]
         cosine, sine = rotary_tables(tokens_all.shape[0])
@@ -433,10 +564,18 @@
         )
 
         upstream = cotangent[0].astype(f32)
-        dout_rows = dot_tn(dispatch_both, after(cotangent[0], tokens_all)).astype(bf16)
-        dout_rows = lax.all_to_all(
-            dout_rows.reshape(NFFN, capacity, model_width), ep_axes, 0, 0, tiled=True
-        ).reshape(NFFN * capacity, model_width)
+        def exchange(rows):
+            blocks = rows.reshape(NFFN, capacity, rows.shape[1])
+            return [blocks[0]] + [
+                lax.ppermute(blocks[k], ep_axes, [(i, i ^ k) for i in range(NFFN)])
+                for k in range(1, NFFN)
+            ]
+
+        def exchanged(rows):
+            return jnp.concatenate(exchange(rows), axis=0)
+
+        dout_rows = dot_tn(dispatch_both, cotangent[0]).astype(bf16)
+        dout_rows = exchange(after(dout_rows, tokens_all))
         mixed, dout_rows = lax.optimization_barrier((mixed, dout_rows))
 
         mixed_keep = lax.dynamic_slice_in_dim(mixed, y * row_count, row_count, 0)
@@ -463,47 +602,52 @@
             jnp.sum(upstream * consts[1:2], axis=-1, keepdims=True),
         ]
 
-        def to_experts(rows):
-            rows = rows.reshape(NFFN, capacity, rows.shape[1])
-            return lax.all_to_all(rows, ep_axes, 0, 0, tiled=True).reshape(NFFN * capacity, -1)
-
-        gate_parts = [three_parts_rounded(picked[j]) for j in range(TOP)]
         taken = dot_tn(
             jnp.concatenate(dispatch, axis=0),
             jnp.concatenate(
-                [jnp.concatenate([expert_in, gate_parts[j]], axis=1) for j in range(TOP)], axis=0
+                [
+                    jnp.concatenate([expert_in, gate_columns(picked[j], j)], axis=1)
+                    for j in range(TOP)
+                ],
+                axis=0,
             ),
         ).astype(bf16)
-        taken = to_experts(taken)
-        result, dtaken, hidden, dgate_low, dup_low, dresult = expert_compute(
-            taken, dout_rows, expert_use
-        )
-        dtaken = to_experts(dtaken)
-        result = to_experts(after(result, dtaken))
-        taken = taken[:, :model_width]
+        taken = exchanged(taken)
+        dout_rows = jnp.concatenate(dout_rows, axis=0)
+        result, dtaken, right, dresult = expert_compute(
+            flipped[None].astype(jnp.int32), taken, dout_rows, expert_same, expert_other
+        )
+        dtaken = exchange(dtaken)
+        dtaken = jnp.concatenate(dtaken, axis=0)
 
         def sum_rows(grad):
+            axes = ("dp_far", "core") if spread else DP + ("seq",)
+            return lax.psum_scatter(grad, axes, scatter_dimension=0, tiled=True)
+
+        def to_owners(same_y, other_y):
             if not spread:
-                return lax.psum_scatter(grad, DP + ("seq",), scatter_dimension=0, tiled=True)[None]
-            grad = lax.psum_scatter(grad, ("dp_far", "core"), scatter_dimension=0, tiled=True)
-            grad = grad.reshape(2, -1, grad.shape[1])
-            same_y, other_y = cross(*keep_and_send(grad, y, 0))
+                return same_y[None]
+            same_y, other_y = cross(same_y, other_y)
             return in_order(same_y[None], other_y[None], y, 0)
 
-        hidden_width = hidden.shape[1]
-        ddown = sum_rows(dot_tn(dresult, hidden).astype(bf16))
-        dgate_up = sum_rows(dot_tn(taken, jnp.concatenate([dgate_low, dup_low], axis=1)).astype(bf16))
-        expert_sum = jnp.stack(
-            [dgate_up[..., :hidden_width], dgate_up[..., hidden_width:], ddown], axis=1
-        ).astype(f32)
+        hidden_width = right.shape[2]
+        dexpert = weight_gradients(taken, dresult, right)
+        result = exchange(after(result, dtaken))
+        dexpert = sum_rows(dexpert)
+        if spread:
+            row_parts = keep_and_send(dexpert.reshape(2, -1, dexpert.shape[1]), y, 0)
+        else:
+            row_parts = (dexpert, dexpert)
+
 
         dgates = jnp.zeros_like(gates)
-        dnormed_two = dot_nn(dispatch_both, dtaken[:, :model_width])
+        returned = dot_nn(dispatch_both, dtaken)
+        dnormed_two = returned[:, :model_width]
         value_weight = [0.0, 0.0, 0.0]
         for j in range(TOP):
             route = route_rows[:, j : j + 1]
             local = [jnp.where(route == NFFN + 1 + i, 1.0, 0.0) for i in range(3)]
-            parts = dot_nn(dispatch[j], dtaken[:, model_width:])
+            parts = returned[:, model_width + 4 * j : model_width + 4 * j + 3]
             dpicked = jnp.sum(parts, axis=1, keepdims=True)
             for i in range(3):
                 dpicked = dpicked + jnp.where(route == NFFN + 1 + i, dlocal[i], 0.0)
@@ -512,14 +656,6 @@
         dnormed_two = dnormed_two + value_weight[0] * upstream
         dconst_one = jnp.sum(value_weight[1] * upstream, axis=0, keepdims=True)
         dconst_two = jnp.sum(value_weight[2] * upstream, axis=0, keepdims=True)
-        mixture = (
-            picked[0] * dot_nn(dispatch[0], result)
-            + picked[1] * dot_nn(dispatch[1], result)
-            + value_weight[0] * normed_two
-            + value_weight[1] * consts[0:1]
-            + value_weight[2] * consts[1:2]
-        )
-        block_output = (resid + mixture).astype(bf16)
         dlogits = gates * (dgates - jnp.sum(gates * dgates, axis=-1, keepdims=True))
         dnormed_two = dnormed_two + exact_dot(dlogits, router.astype(f32))
         drouter = exact_dot(dlogits.T, expert_in.astype(f32))
@@ -549,21 +685,42 @@
                 totals[step // n_x] = totals[step // n_x] + got.astype(f32)
             return totals
 
-        def dp_sum(grad):
-            return scatter_steps(grad.astype(bf16), DP, z, n_dp)
-
-        dout_part = core_sum(dweight_out)
+        def dp_sum(grad, wait_for):
+            return scatter_steps(grad.astype(bf16), DP, z, n_dp, wait_for)
+
         dmixed = dot_nt(dbranch_low, out_weight).astype(bf16)
         dmixed_keep = lax.dynamic_slice_in_dim(dmixed, y * half_width, half_width, 1)
         dmixed_send = lax.dynamic_slice_in_dim(dmixed, (1 - y) * half_width, half_width, 1)
         dmixed_heads = in_order(dmixed_keep, swap_seq(dmixed_send), y, 0)
-        dmixed_heads = after(dmixed_heads, dout_part)
-        dweight_qkv, dnormed_all = attention_backward(
-            normed, query, key, value, dmixed_heads, log_sums, qkv_weight, cosine, sine
-        )
-        dout_sum = dp_sum(sum(plane_sum(dout_part)))
+        dout_part = core_sum(dweight_out)
+        vectors = jnp.concatenate(
+            [jnp.zeros_like(dgain_two), dgain_two, dconst_one, dconst_two, drouter], axis=0
+        )
+        vectors = jnp.pad(vectors.T, ((0, 0), (0, vector_pad)))
+        dpack, dnormed_all = attention_backward(
+            normed, tokens_all, vectors, query, key, value, dmixed_heads, log_sums, qkv_weight, cosine, sine
+        )
+        dpack, result = after((dpack, result), dnormed_all)
+        dpack = after(dpack, result)
+        this_y, other_y = plane_sum(jnp.concatenate([core_sum(dpack), dout_part], axis=-1))
+        columns = 3 * half_width
+        dpack = dp_sum(
+            (
+                jnp.concatenate(
+                    [
+                        this_y[..., :columns],
+                        other_y[..., :columns],
+                        this_y[..., columns:] + other_y[..., columns:],
+                    ],
+                    axis=-1,
+                ).astype(bf16)
+            ),
+            row_parts,
+        )
         dnormed_keep = lax.dynamic_slice_in_dim(dnormed_all, y * row_count, row_count, 0)
-        dnormed_send = lax.dynamic_slice_in_dim(dnormed_all, (1 - y) * row_count, row_count, 0)
+        dnormed_send = lax.dynamic_slice_in_dim(
+            dnormed_all, (1 - y) * row_count, row_count, 0
+        )
         dnormed = dnormed_keep + swap_seq(dnormed_send.astype(bf16)).astype(f32)
         rho_one = lax.rsqrt(jnp.mean(inputs * inputs, axis=-1, keepdims=True) + norm_eps)
         scaled_one = dnormed * gain_one
@@ -571,34 +728,39 @@
             rho_one * scaled_one
             - inputs * (rho_one * rho_one * rho_one) * jnp.mean(inputs * scaled_one, -1, keepdims=True)
         )
-        dgain_one = jnp.sum(dnormed * inputs * rho_one, axis=0, keepdims=True)
-
-        dvector = jnp.concatenate([dgain_one, dgain_two, dconst_one, dconst_two, drouter], axis=0)
-        qkv_part = core_sum(dweight_qkv)
-        vector_part = core_sum(jnp.pad(dvector.T, ((0, 0), (0, vector_pad))))
-        this_y, other_y = plane_sum(jnp.concatenate([qkv_part, vector_part], axis=-1))
-        columns = 3 * half_width
-        dpack = dp_sum(
-            jnp.concatenate(
+        dpack = after(dpack, dexpert)
+        result = jnp.concatenate(result, axis=0)
+        mixture = (
+            picked[0] * dot_nn(dispatch[0], result)
+            + picked[1] * dot_nn(dispatch[1], result)
+            + value_weight[0] * normed_two
+            + value_weight[1] * consts[0:1]
+            + value_weight[2] * consts[1:2]
+        )
+        block_output = (resid + mixture).astype(bf16)
+        dpack = with_layout_constraint(dpack, Layout((0, 1)))
+        head_pairs = half_width // 128
+
+        def by_matrix(part):
+            return jnp.stack(
                 [
-                    this_y[..., :columns],
-                    other_y[..., :columns],
-                    this_y[..., columns:] + other_y[..., columns:],
-                ],
-                axis=-1,
+                    jnp.concatenate(
+                        [
+                            part[:, 384 * pair + 128 * which : 384 * pair + 128 * which + 128]
+                            for pair in range(head_pairs)
+                        ],
+                        axis=1,
+                    )
+                    for which in range(3)
+                ]
             )
-        )
-        head_pairs = half_width // 128
-
-        def by_matrix(part):
-            part = part.reshape(own_rows, head_pairs, 3, 128)
-            return part.transpose(2, 0, 1, 3).reshape(3, own_rows, half_width)
 
         qkv_sum = in_order(
             by_matrix(dpack[:, :columns]), by_matrix(dpack[:, columns : 2 * columns]), y, 2
         )
+        vector_sum = dpack[:, 2 * columns :][:, : 4 + NEXP].T
+        dout_sum = dpack[:, 2 * columns + 128 :]
         attention_sum = jnp.concatenate([qkv_sum, dout_sum[None]], axis=0)
-        vector_sum = dpack[:, 2 * columns :][:, : 4 + NEXP].T
 
         attention_m, attention_s, attention_u = moments(
             attention_master, attention_first, attention_second, attention_sum
@@ -606,9 +768,13 @@
         vector_m, vector_s, vector_u = moments(
             vector_master, vector_first, vector_second, vector_sum
         )
+        dexpert = to_owners(*row_parts)
+        expert_sum = jnp.stack(jnp.split(dexpert, 3, axis=2), axis=1).astype(f32)
         expert_m, expert_s, expert_u = moments(
             expert_master, expert_first, expert_second, expert_sum
         )
+
+        expert_u = lax.optimization_barrier(expert_u)
 
         def squares(attention_x, vector_x, expert_x):
             vector_parts = jnp.sum(vector_x * vector_x, axis=1)

time: 473 us -> 456 us (0.964)
  blocking collectives: 50.7 us -> 0 us
  starting transfers between devices: 62.7 us -> 91.7 us
  matrix products: 42.2 us -> 19.4 us
  local copies, waits for them, and re-layouts: 39.8 us -> 58 us
  Pallas kernels: 71.9 us -> 87.2 us
  other arithmetic: 64 us -> 56 us
    all_to_all x1 -> x0, blocking collectives: 50.7 us -> none  [to_experts(): lax.all_to_all(rows, ep_axes, 0, 0, tiled=True).reshape(NFFN * capacity, -1)]
    ppermute x5 -> x35, starting transfers between devices: 2.92 us -> 47.8 us  [the longest x28 38.2 us: exchange(): lax.ppermute(blocks[k], ep_axes, [(i, i ^ k) for i in range(NFFN)])]
    ppermute x5 -> x35, waiting for transfers between devices: 5.32 us -> 42.3 us  [the longest x28 39.2 us: exchange(): lax.ppermute(blocks[k], ep_axes, [(i, i ^ k) for i in range(NFFN)])]
    dot_general x5 -> x3, matrix products: 22.4 us -> 5.87 us  [dot_tn(): lax.dot_general(left, right, (((0,), (0,)), ((), ())), preferred_element_...]
    all_to_all x3 -> x0, starting transfers between devices: 16.5 us -> none  [the longest x2 12.3 us: to_experts(): lax.all_to_all(rows, ep_axes, 0, 0, tiled=True).reshape(NFFN * capacity, -1)]
    pallas_call x1 -> x2, Pallas kernels: 23.5 us -> 37 us  [the longest x1 22.9 us: expert_compute(): pl.pallas_call(expert_kernel, grid=(hidden // FF_COLUMNS,), in_specs=[pl....]
    unnamed x124 -> x256, local copies, waits for them, and re-layouts: 14.8 us -> 28.1 us
    ppermute x6 -> x3, waiting for transfers between devices: 13.9 us -> 4.46 us  [scatter_steps(): lax.ppermute(block, axis_name, [(i, (i + step) % count) for i in range(co...]
  transfers between devices with their start and end apart: 42 -> 60, of which waited for: 19 -> 24; matrix products, arithmetic and copies ran while one was open for 23% -> 20% of each run, Pallas kernels for 10% -> 11%
where the time goes in v3:
time: 456 us; the launch traced here: 449 us
  waiting for transfers between devices  121 us (27%)
  starting transfers between devices  91.7 us (20%)
  Pallas kernels  87.2 us (19%)
  local copies, waits for them, and re-layouts  58 us (13%)
  other arithmetic  56 us (12%)
  matrix products  19.4 us (4%)
  between operations  16 us (4%)
    ppermute x28, waiting for transfers between devices, exchange(): lax.ppermute(blocks[k], ep_axes, [(i, i ^ k) for i in range(NFFN)])  39.2 us
    ppermute x28, starting transfers between devices, exchange(): lax.ppermute(blocks[k], ep_axes, [(i, i ^ k) for i in range(NFFN)])  38.2 us
    ppermute x2, waiting for transfers between devices, cross(): lax.ppermute(other_y, ('dp_near', 'seq', 'core'), moves)  32.2 us
    pallas_call x1, Pallas kernels, attention_backward(): pl.pallas_call(attention_backward_kernel, grid=(pairs,), in_specs=[full((...  31.4 us
    unnamed x256, local copies, waits for them, and re-layouts  28.1 us
    pallas_call x1, Pallas kernels, expert_compute(): pl.pallas_call(expert_kernel, grid=(hidden // FF_COLUMNS,), in_specs=[pl....  22.9 us
    ppermute x8, waiting for transfers between devices, swap(): return lax.ppermute(value, axis_name, [(0, 1), (1, 0)])  20.8 us
    pallas_call x1, Pallas kernels, attention_forward(): pl.pallas_call(attention_forward_kernel, grid=(pairs,), in_specs=[full((l...  18.8 us
  transfers between devices with their start and end apart: 60, of which 24 were waited for; matrix products, arithmetic and copies ran while one was open for 20% of the time, Pallas kernels for 11%

profile of v3, /device:TPU:0, one launch (start us, length us, event | category | flops | bytes accessed | tf_op | source)
XLA Modules:
  0.0 449.3 jit_solution(15136082090203301625)
XLA Ops:
  9.8 3.0 collective-permute-start.1
  12.9 2.8 collective-permute-done.1
  15.7 1.9 collective-permute-start.2
  17.7 2.6 collective-permute-start.3
  21.6 2.7 convert_element_type.189
  28.6 3.6 collective-permute-done.3
  42.4 7.5 %collective-permute-done.5 = bf16[4,2,24,2048]{3,2,1,0:T(8,128)(2,1)S(1)} collective-permute-done((bf16[4,2,24,2048]{3,2,1,0:T(8,128)(2,1)}, bf16[4,2,24,2048]{3,2,1,0:T(8,128)(2,1)S(1)}, u32[]{:S(2)}, u32[]{:S(2)}) %collective-permute-start.5) | collective-permute-done | bytes 786464 | tf_op jit(solution)/shard_map/ppermute | solution.py:100
  50.0 10.4 %collective-permute-start.6 = (bf16[2,4,2,24,2048]{4,3,0,2,1:T(8,128)(2,1)S(1)}, bf16[2,4,2,24,2048]{4,3,0,2,1:T(8,128)(2,1)}, u32[]{:S(2)}, u32[]{:S(2)}) collective-permute-start(bf16[2,4,2,24,2048]{4,3,0,2,1:T(8,128)(2,1)S(1)} %bitcast_dynamic-update-slice_fusion.1), channel_id=1, source_target_pairs={{0,1},{1,0},{2,3},{3,2},{4,5},{5,4},{6,7},{7,6},{8,9},{9,8},{10,11... | collective-permute-start | bytes 4718600 | tf_op jit(solution)/shard_map/ppermute | solution.py:83
  61.1 1.6 fusion.34
  62.6 2.2 convolution_convert_fusion.1
  64.9 2.4 broadcast_select_fusion.3
  67.2 13.6 %collective-permute-done.23 = bf16[3,96,2048]{2,1,0:T(8,128)(2,1)} collective-permute-done((bf16[3,96,2048]{2,1,0:T(8,128)(2,1)}, bf16[3,96,2048]{2,1,0:T(8,128)(2,1)}, u32[]{:S(2)}, u32[]{:S(2)}) %collective-permute-start.23) | collective-permute-done | bytes 1179680 | tf_op jit(solution)/shard_map/ppermute | solution.py:492
  80.9 1.6 pad_maximum_fusion.2.x_ref
  84.9 1.5 collective-permute-start.8
  87.1 4.1 collective-permute-start.10
  91.2 1.6 select_bitcast_fusion.1
  97.6 1.8 collective-permute-start.12
  99.4 2.1 collective-permute-start.13
  103.6 18.8 %shard_map.298 = (bf16[1024,768]{1,0:T(8,128)(2,1)S(1)}, bf16[1024,384]{1,0:T(8,128)(2,1)S(1)}, bf16[1024,384]{1,0:T(8,128)(2,1)S(1)}, bf16[1024,384]{1,0:T(8,12...) custom-call(bf16[1024,768]{1,0:T(8,128)(2,1)S(1)} %pad_maximum_fusion.2.x_ref, ...), custom_call_target="tpu_custom_call" | custom-call | flops 3422552064 | bytes 6291456 | tf_op jit(solution)/shard_map/pallas_call | solution.py:197
  128.6 3.1 collective-permute-done.14
  132.0 2.4 multiply_reduce_fusion.4
  136.8 1.8 fusion.11
  146.1 1.6 collective-permute-done.15
  149.4 2.5 collective-permute-start.21
  153.3 22.3 %collective-permute-done.18 = bf16[96,896]{1,0:T(8,128)(2,1)S(1)} collective-permute-done((bf16[96,896]{1,0:T(8,128)(2,1)S(1)}, bf16[96,896]{1,0:T(8,128)(2,1)S(1)}, u32[]{:S(2)}, u32[]{:S(2)}) %collective-permute-start.18) | collective-permute-done | bytes 172064 | tf_op jit(solution)/shard_map/ppermute | solution.py:570
  176.3 2.7 collective-permute-done.19
  179.7 2.0 collective-permute-done.20
  182.3 1.9 collective-permute-done.21
  186.2 22.9 %shard_map.299 = (bf16[768,768]{1,0:T(8,128)(2,1)S(1)}, bf16[768,896]{1,0:T(8,128)(2,1)S(1)}, bf16[3,768,2048]{2,1,0:T(8,128)(2,1)}, bf16[768,768]{1,0:T(8,128)(2,1)S(1)}) custom-call(s32[1]{0:T(128)} %bitcast.34.flipped_ref, bf16[768,896]{1,0:T(8,128)(2,1)} %constant_dynamic-update-slice_fusion.10.taken_ref, bf16[768,768]{1,0:T(8,128)(2,1)S(1)} %copy-done.3, ...), custom_call_target="tpu_custom_call" | custom-call | flops 16911433728 | bytes 18874368 | tf_op jit(solution)/shard_map/pallas_call | solution.py:376
  210.1 14.1 %shard_map.301 = bf16[768,6144]{1,0:T(8,128)(2,1)} custom-call(bf16[768,896]{1,0:T(8,128)(2,1)} %constant_dynamic-update-slice_fusion.10.taken_ref, bf16[768,768]{1,0:T(8,128)(2,1)} %copy-done.10, bf16[3,768,2048]{2,1,0:T(8,128)(2,1)} %get-tuple-element.90.right_ref), custom_call_target="tpu_custom_call" | custom-call | flops 7247757312 | bytes 18874368 | tf_op jit(solution)/shard_map/pallas_call | solution.py:428
  232.5 2.2 collective-permute-start.26
  234.7 2.1 collective-permute-start.28
  238.1 2.8 collective-permute-start.30
  240.9 3.9 collective-permute-done.26
  244.9 1.6 collective-permute-done.29
  246.6 1.9 collective-permute-done.30
  250.3 1.7 multiply_reduce_fusion.2
  252.4 2.4 convolution_convert_fusion.2
  255.6 1.6 collective-permute-start.31
  258.2 1.8 convolution_convert_fusion
  261.8 1.6 collective-permute-start.33
  263.4 1.6 collective-permute-start.34
  265.1 2.3 constant_dynamic-slice_fusion.2
  271.0 1.8 collective-permute-start.36
  275.3 3.1 collective-permute-start.38
  278.4 31.4 %shard_map.300 = (bf16[768,1280]{1,0:T(8,128)(2,1)}, f32[1024,768]{1,0:T(8,128)}) custom-call(bf16[1024,768]{1,0:T(8,128)(2,1)S(1)} %copy-done.9, bf16[1024,768]{1,0:T(8,128)(2,1)} %copy-done.1, f32[768,128]{1,0:T(8,128)S(1)} %pad.14.vector_ref, bf16[1024,384]{1,0:T(8,128)(2,1)S(1)} %copy-done.12, bf16[1024,384]{1,0:T(8,128)(2,1)S(1)} %copy-done.14, ...), custom_call_target="tpu_custom_call" | custom-call | flops 7650410496 | bytes 9437184 | tf_op jit(solution)/shard_map/pallas_call | solution.py:271
  311.9 1.6 constant_dynamic-slice_fusion.4
  321.0 1.6 collective-permute-start.43
  322.7 2.6 fusion.41
  325.3 14.9 %collective-permute-done.39 = bf16[512,768]{1,0:T(8,128)(2,1)S(1)} collective-permute-done((bf16[512,768]{1,0:T(8,128)(2,1)S(1)}, bf16[512,768]{1,0:T(8,128)(2,1)S(1)}, u32[]{:S(2)}, u32[]{:S(2)}) %collective-permute-start.39) | collective-permute-done | bytes 786464 | tf_op jit(solution)/shard_map/ppermute | solution.py:83
  341.1 7.1 %collective-permute-done.43 = bf16[4,24,2048]{2,1,0:T(8,128)(2,1)S(1)} collective-permute-done((bf16[4,24,2048]{2,1,0:T(8,128)(2,1)S(1)}, bf16[4,24,2048]{2,1,0:T(8,128)(2,1)S(1)}, u32[]{:S(2)}, u32[]{:S(2)}) %collective-permute-start.43) | collective-permute-done | bytes 393248 | tf_op jit(solution)/shard_map/ppermute | solution.py:684
  348.4 2.9 collective-permute-done.42
  353.1 10.9 %collective-permute-start.46 = (bf16[24,3200]{1,0:T(8,128)(2,1)}, bf16[24,3200]{1,0:T(8,128)(2,1)}, u32[]{:S(2)}, u32[]{:S(2)}) collective-permute-start(bf16[24,3200]{1,0:T(8,128)(2,1)} %get-tuple-element.248), channel_id=1, source_target_pairs={{0,16},{8,24},{16,0},{24,8},{1,17},{9,25},{17,1},{25,9},{2,18},{10... | collective-permute-start | bytes 460808 | tf_op jit(solution)/shard_map/ppermute | solution.py:110
  365.0 1.8 dynamic-slice_bitcast_fusion
  368.8 4.3 collective-permute-done.46
  377.1 18.7 %collective-permute-done.49 = bf16[96,6144]{1,0:T(8,128)(2,1)S(1)} collective-permute-done((bf16[96,6144]{1,0:T(8,128)(2,1)S(1)}, bf16[96,6144]{1,0:T(8,128)(2,1)S(1)}, u32[]{:S(2)}, u32[]{:S(2)}) %collective-permute-start.49) | collective-permute-done | bytes 1179680 | tf_op jit(solution)/shard_map/ppermute | solution.py:492
  396.3 8.1 %multiply_add_fusion = (f32[2,3,96,2048]{3,2,1,0:T(8,128)}, f32[2,3,96,2048]{3,2,1,0:T(8,128)}, f32[2,3,96,2048]{3,2,1,0:T(8,128)}, f32[2,3]{1,0:T(2,128)S(1)}) fusion(f32[2,3,96,2048]{3,2,1,0:T(8,128)S(1)} %bitcast.229, bf16[2,1,96,2048]{3,2,1,0:T(8,128)(2,1)S(1)} %get-tuple-element.196, bf16[2,1,96,2048]{3,2,1,0:T(8,128)(2,1)S(1)} %get-tuple-element.197, ...), kind=kLoop, calls=%fused_computation.6 | loop fusion | flops 21233658 | bytes 30670872 | tf_op jit(solution)/shard_map/add | solution.py:66
  404.5 2.9 multiply_reduce_fusion
  407.9 2.6 concatenate.118
  410.5 2.3 collective-permute-start.50
  414.2 1.6 collective-permute-start.53
  420.5 2.2 collective-permute-start.56
  423.2 3.1 fusion.18
  433.0 7.5 %multiply_subtract_fusion = f32[2,3,96,2048]{3,2,1,0:T(8,128)} fusion(f32[2,3,96,2048]{3,2,1,0:T(8,128)} %param.26, f32[2,3,96,2048]{3,2,1,0:T(8,128)} %get-tuple-element.182, f32[2,3]{1,0:T(2,128)S(1)} %constant_dynamic-slice_fusion), kind=kLoop, calls=%fused_computation.4 | loop fusion | flops 2359296 | bytes 14155800 | tf_op jit(solution)/shard_map/sub | solution.py:833
  (482 shorter events, 109.6 us)
Async XLA Ops:
  7.2 177.7 %all-gather.3.cloned.1.call-start = ((), (), s32[]{:S(2)}) async-start(), calls=%async_computation.1 | async-start | bytes 5898240 | tf_op jit(solution)/shard_map/all_gather | solution.py:513
  9.8 5.8 %collective-permute-start.1 = (bf16[24,2048]{1,0:T(8,128)(2,1)S(1)}, bf16[24,2048]{1,0:T(8,128)(2,1)S(1)}, u32[]{:S(2)}, u32[]{:S(2)}) collective-permute-start(bf16[24,2048]{1,0:T(8,128)(2,1)S(1)} %get-tuple-element.286), channel_id=1, source_target_pairs={{0,4},{4,0},{1,5},{5,1},{2,6},{6,2},{3,7},{7,3},{8,12},{12,8},{9,1... | collective-permute-start | bytes 294920 | tf_op jit(solution)/shard_map/ppermute | solution.py:83
  15.7 12.2 %collective-permute-start.2 = (bf16[2,24,2048]{2,1,0:T(8,128)(2,1)S(1)}, bf16[2,24,2048]{2,1,0:T(8,128)(2,1)S(1)}, u32[]{:S(2)}, u32[]{:S(2)}) collective-permute-start(bf16[2,24,2048]{2,1,0:T(8,128)(2,1)S(1)} %pad_maximum_fusion.11), channel_id=1, source_target_pairs={{0,8},{8,16},{16,24},{24,0},{1,9},{9,17},{17,25},{25,1},{2,10},{10... | collective-permute-start | bytes 589832 | tf_op jit(solution)/shard_map/ppermute | solution.py:100
  17.7 14.6 %collective-permute-start.3 = (bf16[2,24,2048]{2,1,0:T(8,128)(2,1)S(1)}, bf16[2,24,2048]{2,1,0:T(8,128)(2,1)S(1)}, u32[]{:S(2)}, u32[]{:S(2)}) collective-permute-start(bf16[2,24,2048]{2,1,0:T(8,128)(2,1)S(1)} %pad_maximum_fusion.11), channel_id=1, source_target_pairs={{0,16},{8,24},{16,0},{24,8},{1,17},{9,25},{17,1},{25,9},{2,18},{10... | collective-permute-start | bytes 589832 | tf_op jit(solution)/shard_map/ppermute | solution.py:100
  20.2 12.7 %collective-permute-start.4 = (bf16[2,24,2048]{2,1,0:T(8,128)(2,1)S(1)}, bf16[2,24,2048]{2,1,0:T(8,128)(2,1)S(1)}, u32[]{:S(2)}, u32[]{:S(2)}) collective-permute-start(bf16[2,24,2048]{2,1,0:T(8,128)(2,1)S(1)} %pad_maximum_fusion.11), channel_id=1, source_target_pairs={{0,24},{8,0},{16,8},{24,16},{1,25},{9,1},{17,9},{25,17},{2,26},{10... | collective-permute-start | bytes 589832 | tf_op jit(solution)/shard_map/ppermute | solution.py:100
  25.5 8.1 %collective-permute-start.22 = (bf16[3,96,2048]{2,1,0:T(8,128)(2,1)S(1)}, bf16[3,96,2048]{2,1,0:T(8,128)(2,1)S(1)}, u32[]{:S(2)}, u32[]{:S(2)}) collective-permute-start(bf16[3,96,2048]{2,1,0:T(8,128)(2,1)S(1)} %get-tuple-element.201), channel_id=1, source_target_pairs={{1,8},{8,1},{3,10},{10,3},{5,12},{12,5},{7,14},{14,7},{17,24},{24,... | collective-permute-start | bytes 3538952 | tf_op jit(solution)/shard_map/ppermute | solution.py:483
  34.9 150.1 %all-gather.5.cloned.1.call-start = ((), (), s32[]{:S(2)}) async-start(), calls=%async_computation.2 | async-start | bytes 5898240 | tf_op jit(solution)/shard_map/all_gather | solution.py:516
  34.9 29.9 %collective-permute-start = (bf16[512,768]{1,0:T(8,128)(2,1)S(1)}, bf16[512,768]{1,0:T(8,128)(2,1)}, u32[]{:S(2)}, u32[]{:S(2)}) collective-permute-start(bf16[512,768]{1,0:T(8,128)(2,1)S(1)} %bitcast.234), channel_id=1, source_target_pairs={{0,4},{4,0},{1,5},{5,1},{2,6},{6,2},{3,7},{7,3},{8,12},{12,8},{9,1... | collective-permute-start | bytes 2359304 | tf_op jit(solution)/shard_map/ppermute | solution.py:83
  37.7 12.2 %collective-permute-start.5 = (bf16[4,2,24,2048]{3,2,1,0:T(8,128)(2,1)}, bf16[4,2,24,2048]{3,2,1,0:T(8,128)(2,1)S(1)}, u32[]{:S(2)}, u32[]{:S(2)}) collective-permute-start(bf16[4,2,24,2048]{3,2,1,0:T(8,128)(2,1)} %bitcast_dynamic-update-slice_fusion.2), channel_id=1, source_target_pairs={{0,2},{2,0},{1,3},{3,1},{4,6},{6,4},{5,7},{7,5},{8,10},{10,8},{9,1... | collective-permute-start | bytes 2359304 | tf_op jit(solution)/shard_map/ppermute | solution.py:100
  40.4 40.4 %collective-permute-start.23 = (bf16[3,96,2048]{2,1,0:T(8,128)(2,1)}, bf16[3,96,2048]{2,1,0:T(8,128)(2,1)}, u32[]{:S(2)}, u32[]{:S(2)}) collective-permute-start(bf16[3,96,2048]{2,1,0:T(8,128)(2,1)} %get-tuple-element.200), channel_id=1, source_target_pairs={{0,4},{1,12},{4,0},{5,8},{8,5},{9,13},{12,1},{13,9},{2,6},{3,14},{... | collective-permute-start | bytes 3538952 | tf_op jit(solution)/shard_map/ppermute | solution.py:492
  50.0 41.3 %collective-permute-start.6 = (bf16[2,4,2,24,2048]{4,3,0,2,1:T(8,128)(2,1)S(1)}, bf16[2,4,2,24,2048]{4,3,0,2,1:T(8,128)(2,1)}, u32[]{:S(2)}, u32[]{:S(2)}) collective-permute-start(bf16[2,4,2,24,2048]{4,3,0,2,1:T(8,128)(2,1)S(1)} %bitcast_dynamic-update-slice_fusion.1), channel_id=1, source_target_pairs={{0,1},{1,0},{2,3},{3,2},{4,5},{5,4},{6,7},{7,6},{8,9},{9,8},{10,11... | collective-permute-start | bytes 4718600 | tf_op jit(solution)/shard_map/ppermute | solution.py:83
  61.1 187.5 %copy-start.74 = (s32[512,1]{0,1:T(1,128)}, s32[512,1]{0,1:T(1,128)S(1)}, u32[]{:S(2)}) copy-start(s32[512,1]{0,1:T(1,128)S(1)} %get-tuple-element.288) | copy-start | bytes 6148
  80.8 284.2 %reduce-scatter.2.cloned.1.call-start = ((), (), s32[]{:S(2)}) async-start(), calls=%async_computation.3 | async-start | bytes 11796480 | tf_op jit(solution)/shard_map/reduce_scatter | solution.py:625
  83.6 13.9 %collective-permute-start.7 = (bf16[96,768]{1,0:T(8,128)(2,1)}, bf16[96,768]{1,0:T(8,128)(2,1)}, u32[]{:S(2)}, u32[]{:S(2)}) collective-permute-start(bf16[96,768]{1,0:T(8,128)(2,1)} %get-tuple-element.245), channel_id=1, source_target_pairs={{0,2},{2,0},{4,6},{6,4},{8,10},{10,8},{12,14},{14,12},{1,3},{3,1},... | collective-permute-start | bytes 442376 | tf_op jit(solution)/shard_map/ppermute | solution.py:570
  84.9 14.5 %collective-permute-start.8 = (bf16[96,768]{1,0:T(8,128)(2,1)}, bf16[96,768]{1,0:T(8,128)(2,1)}, u32[]{:S(2)}, u32[]{:S(2)}) collective-permute-start(bf16[96,768]{1,0:T(8,128)(2,1)} %get-tuple-element.244), channel_id=1, source_target_pairs={{0,4},{2,6},{4,0},{6,2},{8,12},{10,14},{12,8},{14,10},{1,5},{3,7},... | collective-permute-start | bytes 442376 | tf_op jit(solution)/shard_map/ppermute | solution.py:570
  86.4 36.1 %collective-permute-start.9 = (bf16[96,768]{1,0:T(8,128)(2,1)}, bf16[96,768]{1,0:T(8,128)(2,1)}, u32[]{:S(2)}, u32[]{:S(2)}) collective-permute-start(bf16[96,768]{1,0:T(8,128)(2,1)} %get-tuple-element.243), channel_id=1, source_target_pairs={{0,6},{2,4},{4,2},{6,0},{8,14},{10,12},{12,10},{14,8},{1,7},{3,5},... | collective-permute-start | bytes 442376 | tf_op jit(solution)/shard_map/ppermute | solution.py:570
  87.1 35.3 %collective-permute-start.10 = (bf16[96,768]{1,0:T(8,128)(2,1)}, bf16[96,768]{1,0:T(8,128)(2,1)}, u32[]{:S(2)}, u32[]{:S(2)}) collective-permute-start(bf16[96,768]{1,0:T(8,128)(2,1)} %get-tuple-element.242), channel_id=1, source_target_pairs={{0,8},{2,10},{4,12},{6,14},{8,0},{10,2},{12,4},{14,6},{1,9},{3,11}... | collective-permute-start | bytes 442376 | tf_op jit(solution)/shard_map/ppermute | solution.py:570
  91.2 31.2 %collective-permute-start.11 = (bf16[96,768]{1,0:T(8,128)(2,1)}, bf16[96,768]{1,0:T(8,128)(2,1)}, u32[]{:S(2)}, u32[]{:S(2)}) collective-permute-start(bf16[96,768]{1,0:T(8,128)(2,1)} %get-tuple-element.241), channel_id=1, source_target_pairs={{0,10},{2,8},{4,14},{6,12},{8,2},{10,0},{12,6},{14,4},{1,11},{3,9}... | collective-permute-start | bytes 442376 | tf_op jit(solution)/shard_map/ppermute | solution.py:570
  97.6 24.9 %collective-permute-start.12 = (bf16[96,768]{1,0:T(8,128)(2,1)}, bf16[96,768]{1,0:T(8,128)(2,1)S(1)}, u32[]{:S(2)}, u32[]{:S(2)}) collective-permute-start(bf16[96,768]{1,0:T(8,128)(2,1)} %get-tuple-element.240), channel_id=1, source_target_pairs={{0,12},{2,14},{4,8},{6,10},{8,4},{10,6},{12,0},{14,2},{1,13},{3,15... | collective-permute-start | bytes 442376 | tf_op jit(solution)/shard_map/ppermute | solution.py:570
  99.4 23.1 %collective-permute-start.13 = (bf16[96,768]{1,0:T(8,128)(2,1)}, bf16[96,768]{1,0:T(8,128)(2,1)S(1)}, u32[]{:S(2)}, u32[]{:S(2)}) collective-permute-start(bf16[96,768]{1,0:T(8,128)(2,1)} %get-tuple-element.239), channel_id=1, source_target_pairs={{0,14},{2,12},{4,10},{6,8},{8,6},{10,4},{12,2},{14,0},{1,15},{3,13... | collective-permute-start | bytes 442376 | tf_op jit(solution)/shard_map/ppermute | solution.py:570
  122.6 9.2 %collective-permute-start.14 = (bf16[512,384]{1,0:T(8,128)(2,1)S(1)}, bf16[512,384]{1,0:T(8,128)(2,1)S(1)}, u32[]{:S(2)}, u32[]{:S(2)}) collective-permute-start(bf16[512,384]{1,0:T(8,128)(2,1)S(1)} %constant_dynamic-slice_fusion.6), channel_id=1, source_target_pairs={{0,4},{4,0},{1,5},{5,1},{2,6},{6,2},{3,7},{7,3},{8,12},{12,8},{9,1... | collective-permute-start | bytes 1179656 | tf_op jit(solution)/shard_map/ppermute | solution.py:83
  135.9 92.9 %copy-start.62 = (f32[512]{0:T(512)}, f32[512]{0:T(512)S(1)}, u32[]{:S(2)}) copy-start(f32[512]{0:T(512)S(1)} %get-tuple-element.172) | copy-start | bytes 6148
  135.9 92.9 %copy-start.64 = (f32[512]{0:T(512)}, f32[512]{0:T(512)S(1)}, u32[]{:S(2)}) copy-start(f32[512]{0:T(512)S(1)} %get-tuple-element.173) | copy-start | bytes 6148
  139.4 8.3 %collective-permute-start.15 = (bf16[96,896]{1,0:T(8,128)(2,1)S(1)}, bf16[96,896]{1,0:T(8,128)(2,1)S(1)}, u32[]{:S(2)}, u32[]{:S(2)}) collective-permute-start(bf16[96,896]{1,0:T(8,128)(2,1)S(1)} %get-tuple-element.223), channel_id=1, source_target_pairs={{0,2},{2,0},{4,6},{6,4},{8,10},{10,8},{12,14},{14,12},{1,3},{3,1},... | collective-permute-start | bytes 516104 | tf_op jit(solution)/shard_map/ppermute | solution.py:570
  140.1 9.3 %collective-permute-start.16 = (bf16[96,896]{1,0:T(8,128)(2,1)S(1)}, bf16[96,896]{1,0:T(8,128)(2,1)S(1)}, u32[]{:S(2)}, u32[]{:S(2)}) collective-permute-start(bf16[96,896]{1,0:T(8,128)(2,1)S(1)} %get-tuple-element.222), channel_id=1, source_target_pairs={{0,4},{2,6},{4,0},{6,2},{8,12},{10,14},{12,8},{14,10},{1,5},{3,7},... | collective-permute-start | bytes 516104 | tf_op jit(solution)/shard_map/ppermute | solution.py:570
  142.6 10.0 %collective-permute-start.17 = (bf16[96,896]{1,0:T(8,128)(2,1)S(1)}, bf16[96,896]{1,0:T(8,128)(2,1)S(1)}, u32[]{:S(2)}, u32[]{:S(2)}) collective-permute-start(bf16[96,896]{1,0:T(8,128)(2,1)S(1)} %get-tuple-element.221), channel_id=1, source_target_pairs={{0,6},{2,4},{4,2},{6,0},{8,14},{10,12},{12,10},{14,8},{1,7},{3,5},... | collective-permute-start | bytes 516104 | tf_op jit(solution)/shard_map/ppermute | solution.py:570
  144.0 31.6 %collective-permute-start.18 = (bf16[96,896]{1,0:T(8,128)(2,1)S(1)}, bf16[96,896]{1,0:T(8,128)(2,1)S(1)}, u32[]{:S(2)}, u32[]{:S(2)}) collective-permute-start(bf16[96,896]{1,0:T(8,128)(2,1)S(1)} %get-tuple-element.220), channel_id=1, source_target_pairs={{0,8},{2,10},{4,12},{6,14},{8,0},{10,2},{12,4},{14,6},{1,9},{3,11}... | collective-permute-start | bytes 516104 | tf_op jit(solution)/shard_map/ppermute | solution.py:570
  144.7 34.3 %collective-permute-start.19 = (bf16[96,896]{1,0:T(8,128)(2,1)S(1)}, bf16[96,896]{1,0:T(8,128)(2,1)S(1)}, u32[]{:S(2)}, u32[]{:S(2)}) collective-permute-start(bf16[96,896]{1,0:T(8,128)(2,1)S(1)} %get-tuple-element.219), channel_id=1, source_target_pairs={{0,10},{2,8},{4,14},{6,12},{8,2},{10,0},{12,6},{14,4},{1,11},{3,9}... | collective-permute-start | bytes 516104 | tf_op jit(solution)/shard_map/ppermute | solution.py:570
  147.7 33.9 %collective-permute-start.20 = (bf16[96,896]{1,0:T(8,128)(2,1)S(1)}, bf16[96,896]{1,0:T(8,128)(2,1)S(1)}, u32[]{:S(2)}, u32[]{:S(2)}) collective-permute-start(bf16[96,896]{1,0:T(8,128)(2,1)S(1)} %get-tuple-element.218), channel_id=1, source_target_pairs={{0,12},{2,14},{4,8},{6,10},{8,4},{10,6},{12,0},{14,2},{1,13},{3,15... | collective-permute-start | bytes 516104 | tf_op jit(solution)/shard_map/ppermute | solution.py:570
  149.4 34.9 %collective-permute-start.21 = (bf16[96,896]{1,0:T(8,128)(2,1)S(1)}, bf16[96,896]{1,0:T(8,128)(2,1)S(1)}, u32[]{:S(2)}, u32[]{:S(2)}) collective-permute-start(bf16[96,896]{1,0:T(8,128)(2,1)S(1)} %get-tuple-element.217), channel_id=1, source_target_pairs={{0,14},{2,12},{4,10},{6,8},{8,6},{10,4},{12,2},{14,0},{1,15},{3,13... | collective-permute-start | bytes 516104 | tf_op jit(solution)/shard_map/ppermute | solution.py:570
  229.0 9.1 %collective-permute-start.24 = (bf16[96,896]{1,0:T(8,128)(2,1)S(1)}, bf16[96,896]{1,0:T(8,128)(2,1)S(1)}, u32[]{:S(2)}, u32[]{:S(2)}) collective-permute-start(bf16[96,896]{1,0:T(8,128)(2,1)S(1)} %get-tuple-element.215), channel_id=1, source_target_pairs={{0,2},{2,0},{4,6},{6,4},{8,10},{10,8},{12,14},{14,12},{1,3},{3,1},... | collective-permute-start | bytes 516104 | tf_op jit(solution)/shard_map/ppermute | solution.py:570
  229.7 8.4 %collective-permute-start.25 = (bf16[96,896]{1,0:T(8,128)(2,1)S(1)}, bf16[96,896]{1,0:T(8,128)(2,1)S(1)}, u32[]{:S(2)}, u32[]{:S(2)}) collective-permute-start(bf16[96,896]{1,0:T(8,128)(2,1)S(1)} %get-tuple-element.214), channel_id=1, source_target_pairs={{0,4},{2,6},{4,0},{6,2},{8,12},{10,14},{12,8},{14,10},{1,5},{3,7},... | collective-permute-start | bytes 516104 | tf_op jit(solution)/shard_map/ppermute | solution.py:570
  232.5 12.3 %collective-permute-start.26 = (bf16[96,896]{1,0:T(8,128)(2,1)S(1)}, bf16[96,896]{1,0:T(8,128)(2,1)S(1)}, u32[]{:S(2)}, u32[]{:S(2)}) collective-permute-start(bf16[96,896]{1,0:T(8,128)(2,1)S(1)} %get-tuple-element.213), channel_id=1, source_target_pairs={{0,6},{2,4},{4,2},{6,0},{8,14},{10,12},{12,10},{14,8},{1,7},{3,5},... | collective-permute-start | bytes 516104 | tf_op jit(solution)/shard_map/ppermute | solution.py:570
  234.7 10.2 %collective-permute-start.27 = (bf16[96,896]{1,0:T(8,128)(2,1)S(1)}, bf16[96,896]{1,0:T(8,128)(2,1)S(1)}, u32[]{:S(2)}, u32[]{:S(2)}) collective-permute-start(bf16[96,896]{1,0:T(8,128)(2,1)S(1)} %get-tuple-element.212), channel_id=1, source_target_pairs={{0,8},{2,10},{4,12},{6,14},{8,0},{10,2},{12,4},{14,6},{1,9},{3,11}... | collective-permute-start | bytes 516104 | tf_op jit(solution)/shard_map/ppermute | solution.py:570
  234.7 10.2 %collective-permute-start.28 = (bf16[96,896]{1,0:T(8,128)(2,1)S(1)}, bf16[96,896]{1,0:T(8,128)(2,1)S(1)}, u32[]{:S(2)}, u32[]{:S(2)}) collective-permute-start(bf16[96,896]{1,0:T(8,128)(2,1)S(1)} %get-tuple-element.211), channel_id=1, source_target_pairs={{0,10},{2,8},{4,14},{6,12},{8,2},{10,0},{12,6},{14,4},{1,11},{3,9}... | collective-permute-start | bytes 516104 | tf_op jit(solution)/shard_map/ppermute | solution.py:570
  238.1 8.5 %collective-permute-start.29 = (bf16[96,896]{1,0:T(8,128)(2,1)S(1)}, bf16[96,896]{1,0:T(8,128)(2,1)S(1)}, u32[]{:S(2)}, u32[]{:S(2)}) collective-permute-start(bf16[96,896]{1,0:T(8,128)(2,1)S(1)} %get-tuple-element.210), channel_id=1, source_target_pairs={{0,12},{2,14},{4,8},{6,10},{8,4},{10,6},{12,0},{14,2},{1,13},{3,15... | collective-permute-start | bytes 516104 | tf_op jit(solution)/shard_map/ppermute | solution.py:570
  238.1 10.4 %collective-permute-start.30 = (bf16[96,896]{1,0:T(8,128)(2,1)S(1)}, bf16[96,896]{1,0:T(8,128)(2,1)S(1)}, u32[]{:S(2)}, u32[]{:S(2)}) collective-permute-start(bf16[96,896]{1,0:T(8,128)(2,1)S(1)} %get-tuple-element.209), channel_id=1, source_target_pairs={{0,14},{2,12},{4,10},{6,8},{8,6},{10,4},{12,2},{14,0},{1,15},{3,13... | collective-permute-start | bytes 516104 | tf_op jit(solution)/shard_map/ppermute | solution.py:570
  255.6 15.4 %collective-permute-start.31 = (bf16[512,384]{1,0:T(8,128)(2,1)}, bf16[512,384]{1,0:T(8,128)(2,1)}, u32[]{:S(2)}, u32[]{:S(2)}) collective-permute-start(bf16[512,384]{1,0:T(8,128)(2,1)} %constant_dynamic-slice_fusion.5), channel_id=1, source_target_pairs={{0,4},{4,0},{1,5},{5,1},{2,6},{6,2},{3,7},{7,3},{8,12},{12,8},{9,1... | collective-permute-start | bytes 1179656 | tf_op jit(solution)/shard_map/ppermute | solution.py:83
  261.5 12.6 %collective-permute-start.32 = (bf16[96,768]{1,0:T(8,128)(2,1)}, bf16[96,768]{1,0:T(8,128)(2,1)}, u32[]{:S(2)}, u32[]{:S(2)}) collective-permute-start(bf16[96,768]{1,0:T(8,128)(2,1)} %get-tuple-element.233), channel_id=1, source_target_pairs={{0,2},{2,0},{4,6},{6,4},{8,10},{10,8},{12,14},{14,12},{1,3},{3,1},... | collective-permute-start | bytes 442376 | tf_op jit(solution)/shard_map/ppermute | solution.py:570
  261.8 13.5 %collective-permute-start.33 = (bf16[96,768]{1,0:T(8,128)(2,1)}, bf16[96,768]{1,0:T(8,128)(2,1)}, u32[]{:S(2)}, u32[]{:S(2)}) collective-permute-start(bf16[96,768]{1,0:T(8,128)(2,1)} %get-tuple-element.232), channel_id=1, source_target_pairs={{0,4},{2,6},{4,0},{6,2},{8,12},{10,14},{12,8},{14,10},{1,5},{3,7},... | collective-permute-start | bytes 442376 | tf_op jit(solution)/shard_map/ppermute | solution.py:570
  263.4 46.4 %collective-permute-start.34 = (bf16[96,768]{1,0:T(8,128)(2,1)}, bf16[96,768]{1,0:T(8,128)(2,1)}, u32[]{:S(2)}, u32[]{:S(2)}) collective-permute-start(bf16[96,768]{1,0:T(8,128)(2,1)} %get-tuple-element.231), channel_id=1, source_target_pairs={{0,6},{2,4},{4,2},{6,0},{8,14},{10,12},{12,10},{14,8},{1,7},{3,5},... | collective-permute-start | bytes 442376 | tf_op jit(solution)/shard_map/ppermute | solution.py:570
  265.0 44.9 %collective-permute-start.35 = (bf16[96,768]{1,0:T(8,128)(2,1)}, bf16[96,768]{1,0:T(8,128)(2,1)}, u32[]{:S(2)}, u32[]{:S(2)}) collective-permute-start(bf16[96,768]{1,0:T(8,128)(2,1)} %get-tuple-element.230), channel_id=1, source_target_pairs={{0,8},{2,10},{4,12},{6,14},{8,0},{10,2},{12,4},{14,6},{1,9},{3,11}... | collective-permute-start | bytes 442376 | tf_op jit(solution)/shard_map/ppermute | solution.py:570
  271.0 38.9 %collective-permute-start.36 = (bf16[96,768]{1,0:T(8,128)(2,1)}, bf16[96,768]{1,0:T(8,128)(2,1)S(1)}, u32[]{:S(2)}, u32[]{:S(2)}) collective-permute-start(bf16[96,768]{1,0:T(8,128)(2,1)} %get-tuple-element.229), channel_id=1, source_target_pairs={{0,10},{2,8},{4,14},{6,12},{8,2},{10,0},{12,6},{14,4},{1,11},{3,9}... | collective-permute-start | bytes 442376 | tf_op jit(solution)/shard_map/ppermute | solution.py:570
  274.2 35.7 %collective-permute-start.37 = (bf16[96,768]{1,0:T(8,128)(2,1)S(1)}, bf16[96,768]{1,0:T(8,128)(2,1)S(1)}, u32[]{:S(2)}, u32[]{:S(2)}) collective-permute-start(bf16[96,768]{1,0:T(8,128)(2,1)S(1)} %copy-done.48), channel_id=1, source_target_pairs={{0,12},{2,14},{4,8},{6,10},{8,4},{10,6},{12,0},{14,2},{1,13},{3,15... | collective-permute-start | bytes 442376 | tf_op jit(solution)/shard_map/ppermute | solution.py:570
  275.3 34.6 %collective-permute-start.38 = (bf16[96,768]{1,0:T(8,128)(2,1)S(1)}, bf16[96,768]{1,0:T(8,128)(2,1)S(1)}, u32[]{:S(2)}, u32[]{:S(2)}) collective-permute-start(bf16[96,768]{1,0:T(8,128)(2,1)S(1)} %get-tuple-element.227), channel_id=1, source_target_pairs={{0,14},{2,12},{4,10},{6,8},{8,6},{10,4},{12,2},{14,0},{1,15},{3,13... | collective-permute-start | bytes 442376 | tf_op jit(solution)/shard_map/ppermute | solution.py:570
  278.4 31.4 %copy-start.41 = (bf16[4,2,2,1,24,768]{5,4,0,2,1,3:T(8,128)(2,1)S(1)}, bf16[4,2,2,1,24,768]{5,4,0,2,1,3:T(8,128)(2,1)}, u32[]{:S(2)}) copy-start(bf16[4,2,2,1,24,768]{5,4,0,2,1,3:T(8,128)(2,1)} %copy.142) | copy-start | bytes 1769476
  309.8 8.9 %collective-permute-start.41 = (bf16[2,2,4,24,768]{4,3,2,1,0:T(8,128)(2,1)S(1)}, bf16[2,2,4,24,768]{4,3,2,1,0:T(8,128)(2,1)S(1)}, u32[]{:S(2)}, u32[]{:S(2)}) collective-permute-start(bf16[2,2,4,24,768]{4,3,2,1,0:T(8,128)(2,1)S(1)} %bitcast.244), channel_id=1, source_target_pairs={{0,1},{1,0},{2,3},{3,2},{4,5},{5,4},{6,7},{7,6},{8,9},{9,8},{10,11... | collective-permute-start | bytes 1769480 | tf_op jit(solution)/shard_map/ppermute | solution.py:83
  311.4 28.8 %collective-permute-start.39 = (bf16[512,768]{1,0:T(8,128)(2,1)S(1)}, bf16[512,768]{1,0:T(8,128)(2,1)S(1)}, u32[]{:S(2)}, u32[]{:S(2)}) collective-permute-start(bf16[512,768]{1,0:T(8,128)(2,1)S(1)} %dynamic-slice_convert_fusion), channel_id=1, source_target_pairs={{0,4},{4,0},{1,5},{5,1},{2,6},{6,2},{3,7},{7,3},{8,12},{12,8},{9,1... | collective-permute-start | bytes 2359304 | tf_op jit(solution)/shard_map/ppermute | solution.py:83
  313.7 5.3 %collective-permute-start.40 = (bf16[2,2,4,24,1280]{4,3,2,1,0:T(8,128)(2,1)S(1)}, bf16[2,2,4,24,1280]{4,3,2,1,0:T(8,128)(2,1)S(1)}, u32[]{:S(2)}, u32[]{:S(2)}) collective-permute-start(bf16[2,2,4,24,1280]{4,3,2,1,0:T(8,128)(2,1)S(1)} %bitcast.243), channel_id=1, source_target_pairs={{0,1},{1,0},{2,3},{3,2},{4,5},{5,4},{6,7},{7,6},{8,9},{9,8},{10,11... | collective-permute-start | bytes 2949128 | tf_op jit(solution)/shard_map/ppermute | solution.py:83
  319.7 21.5 %collective-permute-start.44 = (bf16[4,24,2048]{2,1,0:T(8,128)(2,1)S(1)}, bf16[4,24,2048]{2,1,0:T(8,128)(2,1)S(1)}, u32[]{:S(2)}, u32[]{:S(2)}) collective-permute-start(bf16[4,24,2048]{2,1,0:T(8,128)(2,1)S(1)} %get-tuple-element.205), channel_id=1, source_target_pairs={{0,6},{2,4},{4,2},{6,0},{1,7},{3,5},{5,3},{7,1},{8,14},{10,12},{12... | collective-permute-start | bytes 1179656 | tf_op jit(solution)/shard_map/ppermute | solution.py:684
  321.0 27.3 %collective-permute-start.43 = (bf16[4,24,2048]{2,1,0:T(8,128)(2,1)S(1)}, bf16[4,24,2048]{2,1,0:T(8,128)(2,1)S(1)}, u32[]{:S(2)}, u32[]{:S(2)}) collective-permute-start(bf16[4,24,2048]{2,1,0:T(8,128)(2,1)S(1)} %get-tuple-element.206), channel_id=1, source_target_pairs={{0,4},{2,6},{4,0},{6,2},{1,5},{3,7},{5,1},{7,3},{8,12},{10,14},{12... | collective-permute-start | bytes 1179656 | tf_op jit(solution)/shard_map/ppermute | solution.py:684
  340.8 10.5 %collective-permute-start.42 = (bf16[4,24,2048]{2,1,0:T(8,128)(2,1)S(1)}, bf16[4,24,2048]{2,1,0:T(8,128)(2,1)S(1)}, u32[]{:S(2)}, u32[]{:S(2)}) collective-permute-start(bf16[4,24,2048]{2,1,0:T(8,128)(2,1)S(1)} %get-tuple-element.204), channel_id=1, source_target_pairs={{0,2},{2,0},{4,6},{6,4},{1,3},{3,1},{5,7},{7,5},{8,10},{10,8},{12,... | collective-permute-start | bytes 1179656 | tf_op jit(solution)/shard_map/ppermute | solution.py:684
  353.1 15.6 %collective-permute-start.45 = (bf16[24,3200]{1,0:T(8,128)(2,1)}, bf16[24,3200]{1,0:T(8,128)(2,1)}, u32[]{:S(2)}, u32[]{:S(2)}) collective-permute-start(bf16[24,3200]{1,0:T(8,128)(2,1)} %get-tuple-element.249), channel_id=1, source_target_pairs={{0,8},{8,16},{16,24},{24,0},{1,9},{9,17},{17,25},{25,1},{2,10},{10... | collective-permute-start | bytes 460808 | tf_op jit(solution)/shard_map/ppermute | solution.py:110
  353.1 20.0 %collective-permute-start.46 = (bf16[24,3200]{1,0:T(8,128)(2,1)}, bf16[24,3200]{1,0:T(8,128)(2,1)}, u32[]{:S(2)}, u32[]{:S(2)}) collective-permute-start(bf16[24,3200]{1,0:T(8,128)(2,1)} %get-tuple-element.248), channel_id=1, source_target_pairs={{0,16},{8,24},{16,0},{24,8},{1,17},{9,25},{17,1},{25,9},{2,18},{10... | collective-permute-start | bytes 460808 | tf_op jit(solution)/shard_map/ppermute | solution.py:110
  364.0 9.1 %collective-permute-start.47 = (bf16[24,3200]{1,0:T(8,128)(2,1)}, bf16[24,3200]{1,0:T(8,128)(2,1)}, u32[]{:S(2)}, u32[]{:S(2)}) collective-permute-start(bf16[24,3200]{1,0:T(8,128)(2,1)} %get-tuple-element.247), channel_id=1, source_target_pairs={{0,24},{8,0},{16,8},{24,16},{1,25},{9,1},{17,9},{25,17},{2,26},{10... | collective-permute-start | bytes 460808 | tf_op jit(solution)/shard_map/ppermute | solution.py:110
  366.9 28.9 %collective-permute-start.49 = (bf16[96,6144]{1,0:T(8,128)(2,1)S(1)}, bf16[96,6144]{1,0:T(8,128)(2,1)S(1)}, u32[]{:S(2)}, u32[]{:S(2)}) collective-permute-start(bf16[96,6144]{1,0:T(8,128)(2,1)S(1)} %get-tuple-element.198), channel_id=1, source_target_pairs={{0,4},{1,12},{4,0},{5,8},{8,5},{9,13},{12,1},{13,9},{2,6},{3,14},{... | collective-permute-start | bytes 3538952 | tf_op jit(solution)/shard_map/ppermute | solution.py:492
  367.9 27.9 %collective-permute-start.48 = (bf16[96,6144]{1,0:T(8,128)(2,1)S(1)}, bf16[96,6144]{1,0:T(8,128)(2,1)S(1)}, u32[]{:S(2)}, u32[]{:S(2)}) collective-permute-start(bf16[96,6144]{1,0:T(8,128)(2,1)S(1)} %get-tuple-element.199), channel_id=1, source_target_pairs={{1,8},{8,1},{3,10},{10,3},{5,12},{12,5},{7,14},{14,7},{17,24},{24,... | collective-permute-start | bytes 3538952 | tf_op jit(solution)/shard_map/ppermute | solution.py:483
  410.5 3.1 collective-permute-start.50
  413.6 3.6 collective-permute-start.52
  414.2 4.5 collective-permute-start.53
  415.8 3.6 collective-permute-start.51
  419.4 8.2 %collective-permute-start.55 = (f32[2,128]{1,0:T(2,128)S(1)}, f32[2,128]{1,0:T(2,128)S(1)}, u32[]{:S(2)}, u32[]{:S(2)}) collective-permute-start(f32[2,128]{1,0:T(2,128)S(1)} %add_add_fusion.1), channel_id=1, source_target_pairs={{0,16},{8,24},{16,0},{24,8},{1,17},{9,25},{17,1},{25,9},{2,18},{10... | collective-permute-start | bytes 3080 | tf_op jit(solution)/shard_map/ppermute | solution.py:133
  420.5 7.1 %collective-permute-start.56 = (f32[2,128]{1,0:T(2,128)S(1)}, f32[2,128]{1,0:T(2,128)S(1)}, u32[]{:S(2)}, u32[]{:S(2)}) collective-permute-start(f32[2,128]{1,0:T(2,128)S(1)} %add_add_fusion.1), channel_id=1, source_target_pairs={{0,24},{8,16},{16,8},{24,0},{1,25},{9,17},{17,9},{25,1},{2,26},{10... | collective-permute-start | bytes 3080 | tf_op jit(solution)/shard_map/ppermute | solution.py:133
  422.7 4.9 %collective-permute-start.54 = (f32[2,128]{1,0:T(2,128)S(1)}, f32[2,128]{1,0:T(2,128)S(1)}, u32[]{:S(2)}, u32[]{:S(2)}) collective-permute-start(f32[2,128]{1,0:T(2,128)S(1)} %add_add_fusion.1), channel_id=1, source_target_pairs={{0,8},{8,0},{16,24},{24,16},{1,9},{9,1},{17,25},{25,17},{2,10},{10... | collective-permute-start | bytes 3080 | tf_op jit(solution)/shard_map/ppermute | solution.py:133
  (104 other events, 682.6 us)
Sparse Core Ops, SparseCore 0:
  35.0 76.7 all-gather.2
  113.4 62.7 all-gather.4
  224.5 133.6 reduce-scatter.1

commit v4 on v3

--- a/solution.py
+++ b/solution.py
@@ -102,13 +102,13 @@
     return out
 
 
-def scatter_steps(value, axis_name, place, count, wait_for=()):
+def scatter_steps(value, axis_name, place, count):
     total = lax.dynamic_index_in_dim(value, place, 0, keepdims=False).astype(f32)
     got = []
     for step in range(1, count):
         block = lax.dynamic_index_in_dim(value, (place + step) % count, 0, keepdims=False)
         got.append(lax.ppermute(block, axis_name, [(i, (i + step) % count) for i in range(count)]))
-    for part in after(got, wait_for):
+    for part in got:
         total = total + part.astype(f32)
     return total
 
@@ -299,11 +299,13 @@
     other_ref,
     f_ref,
     dtaken_ref,
-    right_ref,
-    dresult_ref,
+    gradient_ref,
     weight_ref,
     f_acc,
     d_acc,
+    dresult_ref,
+    taken_turned,
+    dresult_turned,
 ):
     step, last = pl.program_id(0), pl.num_programs(0) - 1
     width = dout_ref.shape[1]
@@ -314,6 +316,8 @@
         lane = lax.broadcasted_iota(jnp.int32, lanes.shape, 1)
         gate = jnp.sum(jnp.where(lane == 3, 0.0, lanes), axis=1, keepdims=True)
         dresult_ref[...] = (gate * dout_ref[...].astype(f32)).astype(bf16)
+        taken_turned[...] = taken_ref[:, :width].T
+        dresult_turned[...] = dresult_ref[...].T
 
     eighth = width // 8
     shift = flipped_ref[0] * eighth
@@ -331,12 +335,12 @@
     sig = jax.nn.sigmoid(a)
     act = a * sig
     hidden = (act * b).astype(bf16)
-    right_ref[2] = hidden
+    gradient_ref[2] = dot_nn(dresult_turned[...], hidden).astype(bf16)
     dhidden = dot_nn(dresult_ref[...], weight_ref[2])
     dgate = (dhidden * b * (sig * (1.0 + a - act))).astype(bf16)
     dup = (dhidden * act).astype(bf16)
-    right_ref[0] = dgate
-    right_ref[1] = dup
+    gradient_ref[0] = dot_nn(taken_turned[...], dgate).astype(bf16)
+    gradient_ref[1] = dot_nn(taken_turned[...], dup).astype(bf16)
     f = dot_nt(hidden, weight_ref[2])
     d = dot_nt(dgate, weight_ref[0]) + dot_nt(dup, weight_ref[1])
 
@@ -386,63 +390,24 @@
         out_specs=[
             whole(width),
             whole(width + 128),
-            pl.BlockSpec((3, rows, FF_COLUMNS), lambda i: (0, 0, i)),
-            whole(width),
+            pl.BlockSpec((3, width, FF_COLUMNS), lambda i: (0, 0, i)),
         ],
         out_shape=[
             shape(width),
             shape(width + 128),
-            jax.ShapeDtypeStruct((3, rows, hidden), bf16),
-            shape(width),
+            jax.ShapeDtypeStruct((3, width, hidden), bf16),
         ],
-        scratch_shapes=[pltpu.VMEM((3, width, FF_COLUMNS), bf16)] + [pltpu.VMEM((rows, width), f32)] * 2,
-        compiler_params=pltpu.CompilerParams(vmem_limit_bytes=48 * 2**20),
+        scratch_shapes=[pltpu.VMEM((3, width, FF_COLUMNS), bf16)]
+        + [pltpu.VMEM((rows, width), f32)] * 2
+        + [pltpu.VMEM((rows, width), bf16)]
+        + [pltpu.VMEM((width, rows), bf16)] * 2,
+        compiler_params=pltpu.CompilerParams(vmem_limit_bytes=58 * 2**20),
         cost_estimate=pl.CostEstimate(
-            flops=14 * rows * width * hidden,
+            flops=20 * rows * width * hidden,
             bytes_accessed=6 * width * hidden + 6 * rows * hidden,
             transcendentals=rows * hidden,
         ),
     )(flipped, taken, dout, same, other)
-
-
-def gradient_kernel(taken_ref, dresult_ref, right_ref, out_ref, turned):
-    step, first_down = pl.program_id(0), 2 * pl.num_programs(0) // 3
-    width = dresult_ref.shape[1]
-
-    @pl.when(step == 0)
-    def _():
-        turned[...] = taken_ref[:, :width].T
-
-    @pl.when(step == first_down)
-    def _():
-        turned[...] = dresult_ref[...].T
-
-    out_ref[...] = dot_nn(turned[...], right_ref[0]).astype(bf16)
-
-
-def weight_gradients(taken, dresult, right):
-    rows, width = dresult.shape
-    columns = right.shape[2]
-    tile = min(columns, 2 * FF_COLUMNS)
-    steps = columns // tile
-    return pl.pallas_call(
-        gradient_kernel,
-        grid=(3 * steps,),
-        in_specs=[
-            pl.BlockSpec((rows, taken.shape[1]), lambda i: (0, 0)),
-            pl.BlockSpec((rows, width), lambda i: (0, 0)),
-            pl.BlockSpec((1, rows, tile), lambda i: (i // steps, 0, i % steps)),
-        ],
-        out_specs=pl.BlockSpec((width, tile), lambda i: (0, i)),
-        out_shape=jax.ShapeDtypeStruct((width, 3 * columns), bf16),
-        scratch_shapes=[pltpu.VMEM((width, rows), bf16)],
-        compiler_params=pltpu.CompilerParams(vmem_limit_bytes=58 * 2**20),
-        cost_estimate=pl.CostEstimate(
-            flops=6 * rows * width * columns,
-            bytes_accessed=6 * (rows + width) * columns,
-            transcendentals=0,
-        ),
-    )(taken, dresult, right)
 
 
 def make_shards(sizes):
@@ -614,7 +579,7 @@
         ).astype(bf16)
         taken = exchanged(taken)
         dout_rows = jnp.concatenate(dout_rows, axis=0)
-        result, dtaken, right, dresult = expert_compute(
+        result, dtaken, dexpert = expert_compute(
             flipped[None].astype(jnp.int32), taken, dout_rows, expert_same, expert_other
         )
         dtaken = exchange(dtaken)
@@ -622,7 +587,7 @@
 
         def sum_rows(grad):
             axes = ("dp_far", "core") if spread else DP + ("seq",)
-            return lax.psum_scatter(grad, axes, scatter_dimension=0, tiled=True)
+            return lax.psum_scatter(grad, axes, scatter_dimension=1, tiled=True)
 
         def to_owners(same_y, other_y):
             if not spread:
@@ -630,12 +595,10 @@
             same_y, other_y = cross(same_y, other_y)
             return in_order(same_y[None], other_y[None], y, 0)
 
-        hidden_width = right.shape[2]
-        dexpert = weight_gradients(taken, dresult, right)
         result = exchange(after(result, dtaken))
         dexpert = sum_rows(dexpert)
         if spread:
-            row_parts = keep_and_send(dexpert.reshape(2, -1, dexpert.shape[1]), y, 0)
+            row_parts = keep_and_send(dexpert.reshape(3, 2, -1, dexpert.shape[2]), y, 1)
         else:
             row_parts = (dexpert, dexpert)
 
@@ -686,7 +649,7 @@
             return totals
 
         def dp_sum(grad, wait_for):
-            return scatter_steps(grad.astype(bf16), DP, z, n_dp, wait_for)
+            return scatter_steps(after(grad.astype(bf16), wait_for), DP, z, n_dp)
 
         dmixed = dot_nt(dbranch_low, out_weight).astype(bf16)
         dmixed_keep = lax.dynamic_slice_in_dim(dmixed, y * half_width, half_width, 1)
@@ -719,7 +682,7 @@
         )
         dnormed_keep = lax.dynamic_slice_in_dim(dnormed_all, y * row_count, row_count, 0)
         dnormed_send = lax.dynamic_slice_in_dim(
-            dnormed_all, (1 - y) * row_count, row_count, 0
+            after(dnormed_all, this_y), (1 - y) * row_count, row_count, 0
         )
         dnormed = dnormed_keep + swap_seq(dnormed_send.astype(bf16)).astype(f32)
         rho_one = lax.rsqrt(jnp.mean(inputs * inputs, axis=-1, keepdims=True) + norm_eps)
@@ -768,8 +731,7 @@
         vector_m, vector_s, vector_u = moments(
             vector_master, vector_first, vector_second, vector_sum
         )
-        dexpert = to_owners(*row_parts)
-        expert_sum = jnp.stack(jnp.split(dexpert, 3, axis=2), axis=1).astype(f32)
+        expert_sum = to_owners(*row_parts).astype(f32)
         expert_m, expert_s, expert_u = moments(
             expert_master, expert_first, expert_second, expert_sum
         )

time: 456 us -> 448 us (0.982)
  waiting for transfers between devices: 121 us -> 127 us
  Pallas kernels: 87.2 us -> 82.2 us
    ppermute x8, waiting for transfers between devices: 20.8 us -> 5.5 us  [swap(): return lax.ppermute(value, axis_name, [(0, 1), (1, 0)])]
    pallas_call x1 -> x0, Pallas kernels: 14.1 us -> none  [weight_gradients(): pl.pallas_call(gradient_kernel, grid=(3 * steps,), in_specs=[pl.BlockSpec...]
    reduce_scatter x1, waiting for transfers between devices: 0.01 us -> 13.9 us  [sum_rows(): return lax.psum_scatter(grad, axes, scatter_dimension=1, tiled=True)]
    ppermute x3, starting transfers between devices: 11.9 us -> 2.08 us  [scatter_steps(): lax.ppermute(block, axis_name, [(i, (i + step) % count) for i in range(co...]
    pallas_call x1, Pallas kernels: 22.9 us -> 32 us  [expert_compute(): pl.pallas_call(expert_kernel, grid=(hidden // FF_COLUMNS,), in_specs=[pl....]
    ppermute x3, waiting for transfers between devices: 9.99 us -> 15.9 us  [plane_sum(): lax.ppermute(block, ('seq', 'x'), [(i, i ^ step) for i in range(group)])]
    ppermute x3, waiting for transfers between devices: 4.46 us -> 9.53 us  [scatter_steps(): lax.ppermute(block, axis_name, [(i, (i + step) % count) for i in range(co...]
    unnamed x256 -> x244, local copies, waits for them, and re-layouts: 28.1 us -> 23.2 us
  transfers between devices with their start and end apart: 60 -> 60, of which waited for: 24 -> 27; matrix products, arithmetic and copies ran while one was open for 20% -> 20% of each run, Pallas kernels for 11% -> 11%
where the time goes in v4:
time: 448 us; the launch traced here: 442 us
  waiting for transfers between devices  127 us (28%)
  starting transfers between devices  87.2 us (19%)
  Pallas kernels  82.2 us (18%)
  other arithmetic  55.1 us (12%)
  local copies, waits for them, and re-layouts  55.1 us (12%)
  matrix products  19.5 us (4%)
  between operations  16 us (4%)
    ppermute x28, waiting for transfers between devices, exchange(): lax.ppermute(blocks[k], ep_axes, [(i, i ^ k) for i in range(NFFN)])  39.2 us
    ppermute x28, starting transfers between devices, exchange(): lax.ppermute(blocks[k], ep_axes, [(i, i ^ k) for i in range(NFFN)])  38.3 us
    pallas_call x1, Pallas kernels, expert_compute(): pl.pallas_call(expert_kernel, grid=(hidden // FF_COLUMNS,), in_specs=[pl....  32 us
    pallas_call x1, Pallas kernels, attention_backward(): pl.pallas_call(attention_backward_kernel, grid=(pairs,), in_specs=[full((...  31.4 us
    ppermute x2, waiting for transfers between devices, cross(): lax.ppermute(other_y, ('dp_near', 'seq', 'core'), moves)  28 us
    unnamed x244, local copies, waits for them, and re-layouts  23.2 us
    pallas_call x1, Pallas kernels, attention_forward(): pl.pallas_call(attention_forward_kernel, grid=(pairs,), in_specs=[full((l...  18.8 us
    ppermute x8, starting transfers between devices, swap(): return lax.ppermute(value, axis_name, [(0, 1), (1, 0)])  18.3 us
  transfers between devices with their start and end apart: 60, of which 27 were waited for; matrix products, arithmetic and copies ran while one was open for 20% of the time, Pallas kernels for 11%

profile of v4, /device:TPU:0, one launch (start us, length us, event | category | flops | bytes accessed | tf_op | source)
XLA Modules:
  0.0 442.3 jit_solution(4143787015477852498)
XLA Ops:
  9.8 3.0 collective-permute-start.1
  12.9 2.8 collective-permute-done.1
  15.7 1.9 collective-permute-start.2
  17.7 2.6 collective-permute-start.3
  21.6 2.7 convert_element_type.189
  28.6 3.6 collective-permute-done.3
  42.4 7.5 %collective-permute-done.5 = bf16[4,2,24,2048]{3,2,1,0:T(8,128)(2,1)S(1)} collective-permute-done((bf16[4,2,24,2048]{3,2,1,0:T(8,128)(2,1)}, bf16[4,2,24,2048]{3,2,1,0:T(8,128)(2,1)S(1)}, u32[]{:S(2)}, u32[]{:S(2)}) %collective-permute-start.5) | collective-permute-done | bytes 786464 | tf_op jit(solution)/shard_map/ppermute | solution.py:100
  49.9 10.4 %collective-permute-start.6 = (bf16[2,4,2,24,2048]{4,3,0,2,1:T(8,128)(2,1)S(1)}, bf16[2,4,2,24,2048]{4,3,0,2,1:T(8,128)(2,1)}, u32[]{:S(2)}, u32[]{:S(2)}) collective-permute-start(bf16[2,4,2,24,2048]{4,3,0,2,1:T(8,128)(2,1)S(1)} %bitcast_dynamic-update-slice_fusion.1), channel_id=1, source_target_pairs={{0,1},{1,0},{2,3},{3,2},{4,5},{5,4},{6,7},{7,6},{8,9},{9,8},{10,11... | collective-permute-start | bytes 4718600 | tf_op jit(solution)/shard_map/ppermute | solution.py:83
  61.0 1.6 fusion.34
  62.5 2.2 convolution_convert_fusion.1
  64.8 2.4 broadcast_select_fusion.3
  67.1 13.6 %collective-permute-done.23 = bf16[3,96,2048]{2,1,0:T(8,128)(2,1)} collective-permute-done((bf16[3,96,2048]{2,1,0:T(8,128)(2,1)}, bf16[3,96,2048]{2,1,0:T(8,128)(2,1)}, u32[]{:S(2)}, u32[]{:S(2)}) %collective-permute-start.23) | collective-permute-done | bytes 1179680 | tf_op jit(solution)/shard_map/ppermute | solution.py:457
  80.9 1.6 pad_maximum_fusion.2.x_ref
  84.9 1.5 collective-permute-start.8
  87.1 4.2 collective-permute-start.10
  91.4 1.6 select_bitcast_fusion.1
  97.7 1.9 collective-permute-start.12
  99.6 2.0 collective-permute-start.13
  103.7 18.8 %shard_map.298 = (bf16[1024,768]{1,0:T(8,128)(2,1)S(1)}, bf16[1024,384]{1,0:T(8,128)(2,1)S(1)}, bf16[1024,384]{1,0:T(8,128)(2,1)S(1)}, bf16[1024,384]{1,0:T(8,12...) custom-call(bf16[1024,768]{1,0:T(8,128)(2,1)S(1)} %pad_maximum_fusion.2.x_ref, ...), custom_call_target="tpu_custom_call" | custom-call | flops 3422552064 | bytes 6291456 | tf_op jit(solution)/shard_map/pallas_call | solution.py:197
  128.8 2.7 collective-permute-done.14
  131.7 2.3 multiply_reduce_fusion.4
  135.8 1.8 fusion.11
  151.8 25.4 %collective-permute-done.19 = bf16[96,896]{1,0:T(8,128)(2,1)S(1)} collective-permute-done((bf16[96,896]{1,0:T(8,128)(2,1)S(1)}, bf16[96,896]{1,0:T(8,128)(2,1)S(1)}, u32[]{:S(2)}, u32[]{:S(2)}) %collective-permute-start.19) | collective-permute-done | bytes 172064 | tf_op jit(solution)/shard_map/ppermute | solution.py:535
  177.8 1.9 collective-permute-done.20
  180.5 1.9 collective-permute-done.21
  183.1 32.0 %shard_map.299 = (bf16[768,768]{1,0:T(8,128)(2,1)}, bf16[768,896]{1,0:T(8,128)(2,1)}, bf16[3,768,2048]{2,1,0:T(8,128)(2,1)}) custom-call(s32[1]{0:T(128)} %bitcast.34.flipped_ref, bf16[768,896]{1,0:T(8,128)(2,1)} %constant_dynamic-update-slice_fusion.10.taken_ref, bf16[768,768]{1,0:T(8,128)(2,1)} %copy-done.59, ...), custom_call_target="tpu_custom_call" | custom-call | flops 24159191040 | bytes 18874368 | tf_op jit(solution)/shard_map/pallas_call | solution.py:380
  219.7 1.6 fusion.130
  224.5 2.5 collective-permute-start.26
  227.0 2.2 collective-permute-start.28
  230.1 2.8 collective-permute-start.30
  233.9 2.9 collective-permute-done.28
  237.5 2.7 collective-permute-done.30
  242.0 1.7 multiply_reduce_fusion.2
  244.2 2.7 convolution_convert_fusion.2
  247.7 1.7 collective-permute-start.31
  250.4 1.8 convolution_convert_fusion
  254.8 2.5 collective-permute-start.34
  257.7 2.3 constant_dynamic-slice_fusion.2
  263.7 1.8 collective-permute-start.36
  267.5 3.2 collective-permute-start.38
  270.7 31.4 %shard_map.300 = (bf16[768,1280]{1,0:T(8,128)(2,1)}, f32[1024,768]{1,0:T(8,128)}) custom-call(bf16[1024,768]{1,0:T(8,128)(2,1)S(1)} %copy-done.7, bf16[1024,768]{1,0:T(8,128)(2,1)} %copy-done.1, f32[768,128]{1,0:T(8,128)S(1)} %pad.14.vector_ref, bf16[1024,384]{1,0:T(8,128)(2,1)S(1)} %copy-done.9, bf16[1024,384]{1,0:T(8,128)(2,1)S(1)} %copy-done.11, ...), custom_call_target="tpu_custom_call" | custom-call | flops 7650410496 | bytes 9437184 | tf_op jit(solution)/shard_map/pallas_call | solution.py:271
  302.2 1.6 constant_dynamic-slice_fusion.4
  311.0 2.6 fusion.41
  314.7 1.7 collective-permute-start.43
  316.4 5.8 %collective-permute-done.41 = bf16[4,24,2048]{2,1,0:T(8,128)(2,1)S(1)} collective-permute-done((bf16[4,24,2048]{2,1,0:T(8,128)(2,1)S(1)}, bf16[4,24,2048]{2,1,0:T(8,128)(2,1)S(1)}, u32[]{:S(2)}, u32[]{:S(2)}) %collective-permute-start.41) | collective-permute-done | bytes 393248 | tf_op jit(solution)/shard_map/ppermute | solution.py:647
  322.4 2.4 dynamic-slice_convert_fusion
  325.0 4.5 %collective-permute-done.44 = bf16[4,24,2048]{2,1,0:T(8,128)(2,1)S(1)} collective-permute-done((bf16[4,24,2048]{2,1,0:T(8,128)(2,1)S(1)}, bf16[4,24,2048]{2,1,0:T(8,128)(2,1)S(1)}, u32[]{:S(2)}, u32[]{:S(2)}) %collective-permute-start.44) | collective-permute-done | bytes 393248 | tf_op jit(solution)/shard_map/ppermute | solution.py:647
  329.6 5.6 %collective-permute-done.43 = bf16[4,24,2048]{2,1,0:T(8,128)(2,1)S(1)} collective-permute-done((bf16[4,24,2048]{2,1,0:T(8,128)(2,1)S(1)}, bf16[4,24,2048]{2,1,0:T(8,128)(2,1)S(1)}, u32[]{:S(2)}, u32[]{:S(2)}) %collective-permute-start.43) | collective-permute-done | bytes 393248 | tf_op jit(solution)/shard_map/ppermute | solution.py:647
  335.4 13.9 %reduce-scatter.2.cloned.1.call-done = bf16[3,192,2048]{2,1,0:T(8,128)(2,1)} async-done(((bf16[3,768,2048]{2,1,0:T(8,128)(2,1)}), bf16[3,192,2048]{2,1,0:T(8,128)(2,1)}) %reduce-scatter.2.cloned.1.call-update) | async-done | bytes 2359312 | tf_op jit(solution)/shard_map/reduce_scatter | solution.py:590
  349.3 1.9 dynamic-slice_bitcast_fusion
  354.0 1.6 collective-permute-start.49
  356.2 1.9 collective-permute-done.47
  358.1 7.7 %collective-permute-done.46 = bf16[24,3200]{1,0:T(8,128)(2,1)S(1)} collective-permute-done((bf16[24,3200]{1,0:T(8,128)(2,1)S(1)}, bf16[24,3200]{1,0:T(8,128)(2,1)S(1)}, u32[]{:S(2)}, u32[]{:S(2)}) %collective-permute-start.46) | collective-permute-done | bytes 153632 | tf_op jit(solution)/shard_map/ppermute | solution.py:110
  368.5 14.4 %collective-permute-done.49 = bf16[3,96,2048]{2,1,0:T(8,128)(2,1)S(1)} collective-permute-done((bf16[3,96,2048]{2,1,0:T(8,128)(2,1)S(1)}, bf16[3,96,2048]{2,1,0:T(8,128)(2,1)S(1)}, u32[]{:S(2)}, u32[]{:S(2)}) %collective-permute-start.49) | collective-permute-done | bytes 1179680 | tf_op jit(solution)/shard_map/ppermute | solution.py:457
  383.1 8.7 %multiply_add_fusion = (f32[2,3,96,2048]{3,2,1,0:T(8,128)}, f32[2,3,96,2048]{3,2,1,0:T(8,128)}, f32[2,3,96,2048]{3,2,1,0:T(8,128)}, f32[2,3]{1,0:T(2,128)S(1)}) fusion(f32[2,3,96,2048]{3,2,1,0:T(8,128)S(1)} %bitcast.223, bf16[1,3,96,2048]{3,2,1,0:T(8,128)(2,1)S(1)} %get-tuple-element.188, bf16[1,3,96,2048]{3,2,1,0:T(8,128)(2,1)S(1)} %get-tuple-element.187, ...), kind=kLoop, calls=%fused_computation.6 | loop fusion | flops 20054010 | bytes 30670872 | tf_op jit(solution)/shard_map/add | solution.py:66
  391.9 3.0 multiply_reduce_fusion
  395.4 2.7 concatenate.118
  398.0 6.1 %collective-permute-start.50 = (f32[2,128]{1,0:T(2,128)S(1)}, f32[2,128]{1,0:T(2,128)S(1)}, u32[]{:S(2)}, u32[]{:S(2)}) collective-permute-start(f32[2,128]{1,0:T(2,128)S(1)} %pad_bitcast_fusion), channel_id=1, source_target_pairs={{0,1},{1,0},{2,3},{3,2},{4,5},{5,4},{6,7},{7,6},{8,9},{9,8},{10,11... | collective-permute-start | bytes 3080 | tf_op jit(solution)/shard_map/ppermute | solution.py:133
  405.0 1.7 collective-permute-start.52
  408.6 2.6 collective-permute-done.53
  411.7 1.5 collective-permute-start.55
  413.3 2.7 collective-permute-start.56
  415.9 3.1 fusion.18
  425.9 7.5 %multiply_subtract_fusion = f32[2,3,96,2048]{3,2,1,0:T(8,128)} fusion(f32[2,3,96,2048]{3,2,1,0:T(8,128)} %param.26, f32[2,3,96,2048]{3,2,1,0:T(8,128)} %get-tuple-element.178, f32[2,3]{1,0:T(2,128)S(1)} %constant_dynamic-slice_fusion), kind=kLoop, calls=%fused_computation.4 | loop fusion | flops 2359296 | bytes 14155800 | tf_op jit(solution)/shard_map/sub | solution.py:795
  (468 shorter events, 103.6 us)
Async XLA Ops:
  7.2 175.9 %all-gather.3.cloned.1.call-start = ((), (), s32[]{:S(2)}) async-start(), calls=%async_computation.1 | async-start | bytes 5898240 | tf_op jit(solution)/shard_map/all_gather | solution.py:478
  9.8 5.8 %collective-permute-start.1 = (bf16[24,2048]{1,0:T(8,128)(2,1)S(1)}, bf16[24,2048]{1,0:T(8,128)(2,1)S(1)}, u32[]{:S(2)}, u32[]{:S(2)}) collective-permute-start(bf16[24,2048]{1,0:T(8,128)(2,1)S(1)} %get-tuple-element.279), channel_id=1, source_target_pairs={{0,4},{4,0},{1,5},{5,1},{2,6},{6,2},{3,7},{7,3},{8,12},{12,8},{9,1... | collective-permute-start | bytes 294920 | tf_op jit(solution)/shard_map/ppermute | solution.py:83
  15.7 12.2 %collective-permute-start.2 = (bf16[2,24,2048]{2,1,0:T(8,128)(2,1)S(1)}, bf16[2,24,2048]{2,1,0:T(8,128)(2,1)S(1)}, u32[]{:S(2)}, u32[]{:S(2)}) collective-permute-start(bf16[2,24,2048]{2,1,0:T(8,128)(2,1)S(1)} %pad_maximum_fusion.10), channel_id=1, source_target_pairs={{0,8},{8,16},{16,24},{24,0},{1,9},{9,17},{17,25},{25,1},{2,10},{10... | collective-permute-start | bytes 589832 | tf_op jit(solution)/shard_map/ppermute | solution.py:100
  17.7 14.6 %collective-permute-start.3 = (bf16[2,24,2048]{2,1,0:T(8,128)(2,1)S(1)}, bf16[2,24,2048]{2,1,0:T(8,128)(2,1)S(1)}, u32[]{:S(2)}, u32[]{:S(2)}) collective-permute-start(bf16[2,24,2048]{2,1,0:T(8,128)(2,1)S(1)} %pad_maximum_fusion.10), channel_id=1, source_target_pairs={{0,16},{8,24},{16,0},{24,8},{1,17},{9,25},{17,1},{25,9},{2,18},{10... | collective-permute-start | bytes 589832 | tf_op jit(solution)/shard_map/ppermute | solution.py:100
  20.2 12.7 %collective-permute-start.4 = (bf16[2,24,2048]{2,1,0:T(8,128)(2,1)S(1)}, bf16[2,24,2048]{2,1,0:T(8,128)(2,1)S(1)}, u32[]{:S(2)}, u32[]{:S(2)}) collective-permute-start(bf16[2,24,2048]{2,1,0:T(8,128)(2,1)S(1)} %pad_maximum_fusion.10), channel_id=1, source_target_pairs={{0,24},{8,0},{16,8},{24,16},{1,25},{9,1},{17,9},{25,17},{2,26},{10... | collective-permute-start | bytes 589832 | tf_op jit(solution)/shard_map/ppermute | solution.py:100
  25.5 8.1 %collective-permute-start.22 = (bf16[3,96,2048]{2,1,0:T(8,128)(2,1)S(1)}, bf16[3,96,2048]{2,1,0:T(8,128)(2,1)S(1)}, u32[]{:S(2)}, u32[]{:S(2)}) collective-permute-start(bf16[3,96,2048]{2,1,0:T(8,128)(2,1)S(1)} %get-tuple-element.194), channel_id=1, source_target_pairs={{1,8},{8,1},{3,10},{10,3},{5,12},{12,5},{7,14},{14,7},{17,24},{24,... | collective-permute-start | bytes 3538952 | tf_op jit(solution)/shard_map/ppermute | solution.py:448
  34.8 148.2 %all-gather.5.cloned.1.call-start = ((), (), s32[]{:S(2)}) async-start(), calls=%async_computation.2 | async-start | bytes 5898240 | tf_op jit(solution)/shard_map/all_gather | solution.py:481
  34.9 29.9 %collective-permute-start = (bf16[512,768]{1,0:T(8,128)(2,1)S(1)}, bf16[512,768]{1,0:T(8,128)(2,1)}, u32[]{:S(2)}, u32[]{:S(2)}) collective-permute-start(bf16[512,768]{1,0:T(8,128)(2,1)S(1)} %bitcast.228), channel_id=1, source_target_pairs={{0,4},{4,0},{1,5},{5,1},{2,6},{6,2},{3,7},{7,3},{8,12},{12,8},{9,1... | collective-permute-start | bytes 2359304 | tf_op jit(solution)/shard_map/ppermute | solution.py:83
  37.7 12.2 %collective-permute-start.5 = (bf16[4,2,24,2048]{3,2,1,0:T(8,128)(2,1)}, bf16[4,2,24,2048]{3,2,1,0:T(8,128)(2,1)S(1)}, u32[]{:S(2)}, u32[]{:S(2)}) collective-permute-start(bf16[4,2,24,2048]{3,2,1,0:T(8,128)(2,1)} %bitcast_dynamic-update-slice_fusion.2), channel_id=1, source_target_pairs={{0,2},{2,0},{1,3},{3,1},{4,6},{6,4},{5,7},{7,5},{8,10},{10,8},{9,1... | collective-permute-start | bytes 2359304 | tf_op jit(solution)/shard_map/ppermute | solution.py:100
  40.4 40.4 %collective-permute-start.23 = (bf16[3,96,2048]{2,1,0:T(8,128)(2,1)}, bf16[3,96,2048]{2,1,0:T(8,128)(2,1)}, u32[]{:S(2)}, u32[]{:S(2)}) collective-permute-start(bf16[3,96,2048]{2,1,0:T(8,128)(2,1)} %get-tuple-element.193), channel_id=1, source_target_pairs={{0,4},{1,12},{4,0},{5,8},{8,5},{9,13},{12,1},{13,9},{2,6},{3,14},{... | collective-permute-start | bytes 3538952 | tf_op jit(solution)/shard_map/ppermute | solution.py:457
  49.9 41.4 %collective-permute-start.6 = (bf16[2,4,2,24,2048]{4,3,0,2,1:T(8,128)(2,1)S(1)}, bf16[2,4,2,24,2048]{4,3,0,2,1:T(8,128)(2,1)}, u32[]{:S(2)}, u32[]{:S(2)}) collective-permute-start(bf16[2,4,2,24,2048]{4,3,0,2,1:T(8,128)(2,1)S(1)} %bitcast_dynamic-update-slice_fusion.1), channel_id=1, source_target_pairs={{0,1},{1,0},{2,3},{3,2},{4,5},{5,4},{6,7},{7,6},{8,9},{9,8},{10,11... | collective-permute-start | bytes 4718600 | tf_op jit(solution)/shard_map/ppermute | solution.py:83
  60.9 179.3 %copy-start.68 = (s32[512,1]{0,1:T(1,128)}, s32[512,1]{0,1:T(1,128)S(1)}, u32[]{:S(2)}) copy-start(s32[512,1]{0,1:T(1,128)S(1)} %get-tuple-element.281) | copy-start | bytes 6148
  80.8 268.5 %reduce-scatter.2.cloned.1.call-start = ((), (), s32[]{:S(2)}) async-start(), calls=%async_computation.3 | async-start | bytes 11796480 | tf_op jit(solution)/shard_map/reduce_scatter | solution.py:590
  83.6 14.1 %collective-permute-start.7 = (bf16[96,768]{1,0:T(8,128)(2,1)}, bf16[96,768]{1,0:T(8,128)(2,1)}, u32[]{:S(2)}, u32[]{:S(2)}) collective-permute-start(bf16[96,768]{1,0:T(8,128)(2,1)} %get-tuple-element.238), channel_id=1, source_target_pairs={{0,2},{2,0},{4,6},{6,4},{8,10},{10,8},{12,14},{14,12},{1,3},{3,1},... | collective-permute-start | bytes 442376 | tf_op jit(solution)/shard_map/ppermute | solution.py:535
  84.9 14.7 %collective-permute-start.8 = (bf16[96,768]{1,0:T(8,128)(2,1)}, bf16[96,768]{1,0:T(8,128)(2,1)}, u32[]{:S(2)}, u32[]{:S(2)}) collective-permute-start(bf16[96,768]{1,0:T(8,128)(2,1)} %get-tuple-element.237), channel_id=1, source_target_pairs={{0,4},{2,6},{4,0},{6,2},{8,12},{10,14},{12,8},{14,10},{1,5},{3,7},... | collective-permute-start | bytes 442376 | tf_op jit(solution)/shard_map/ppermute | solution.py:535
  86.4 36.2 %collective-permute-start.9 = (bf16[96,768]{1,0:T(8,128)(2,1)}, bf16[96,768]{1,0:T(8,128)(2,1)}, u32[]{:S(2)}, u32[]{:S(2)}) collective-permute-start(bf16[96,768]{1,0:T(8,128)(2,1)} %get-tuple-element.236), channel_id=1, source_target_pairs={{0,6},{2,4},{4,2},{6,0},{8,14},{10,12},{12,10},{14,8},{1,7},{3,5},... | collective-permute-start | bytes 442376 | tf_op jit(solution)/shard_map/ppermute | solution.py:535
  87.1 35.4 %collective-permute-start.10 = (bf16[96,768]{1,0:T(8,128)(2,1)}, bf16[96,768]{1,0:T(8,128)(2,1)}, u32[]{:S(2)}, u32[]{:S(2)}) collective-permute-start(bf16[96,768]{1,0:T(8,128)(2,1)} %get-tuple-element.235), channel_id=1, source_target_pairs={{0,8},{2,10},{4,12},{6,14},{8,0},{10,2},{12,4},{14,6},{1,9},{3,11}... | collective-permute-start | bytes 442376 | tf_op jit(solution)/shard_map/ppermute | solution.py:535
  91.4 31.2 %collective-permute-start.11 = (bf16[96,768]{1,0:T(8,128)(2,1)}, bf16[96,768]{1,0:T(8,128)(2,1)}, u32[]{:S(2)}, u32[]{:S(2)}) collective-permute-start(bf16[96,768]{1,0:T(8,128)(2,1)} %get-tuple-element.234), channel_id=1, source_target_pairs={{0,10},{2,8},{4,14},{6,12},{8,2},{10,0},{12,6},{14,4},{1,11},{3,9}... | collective-permute-start | bytes 442376 | tf_op jit(solution)/shard_map/ppermute | solution.py:535
  97.7 24.9 %collective-permute-start.12 = (bf16[96,768]{1,0:T(8,128)(2,1)}, bf16[96,768]{1,0:T(8,128)(2,1)S(1)}, u32[]{:S(2)}, u32[]{:S(2)}) collective-permute-start(bf16[96,768]{1,0:T(8,128)(2,1)} %get-tuple-element.233), channel_id=1, source_target_pairs={{0,12},{2,14},{4,8},{6,10},{8,4},{10,6},{12,0},{14,2},{1,13},{3,15... | collective-permute-start | bytes 442376 | tf_op jit(solution)/shard_map/ppermute | solution.py:535
  99.6 23.0 %collective-permute-start.13 = (bf16[96,768]{1,0:T(8,128)(2,1)}, bf16[96,768]{1,0:T(8,128)(2,1)S(1)}, u32[]{:S(2)}, u32[]{:S(2)}) collective-permute-start(bf16[96,768]{1,0:T(8,128)(2,1)} %get-tuple-element.232), channel_id=1, source_target_pairs={{0,14},{2,12},{4,10},{6,8},{8,6},{10,4},{12,2},{14,0},{1,15},{3,13... | collective-permute-start | bytes 442376 | tf_op jit(solution)/shard_map/ppermute | solution.py:535
  122.7 8.8 %collective-permute-start.14 = (bf16[512,384]{1,0:T(8,128)(2,1)S(1)}, bf16[512,384]{1,0:T(8,128)(2,1)S(1)}, u32[]{:S(2)}, u32[]{:S(2)}) collective-permute-start(bf16[512,384]{1,0:T(8,128)(2,1)S(1)} %constant_dynamic-slice_fusion.6), channel_id=1, source_target_pairs={{0,4},{4,0},{1,5},{5,1},{2,6},{6,2},{3,7},{7,3},{8,12},{12,8},{9,1... | collective-permute-start | bytes 1179656 | tf_op jit(solution)/shard_map/ppermute | solution.py:83
  135.1 84.5 %copy-start.55 = (f32[512]{0:T(512)}, f32[512]{0:T(512)S(1)}, u32[]{:S(2)}) copy-start(f32[512]{0:T(512)S(1)} %get-tuple-element.168) | copy-start | bytes 6148
  135.1 84.5 %copy-start.57 = (f32[512]{0:T(512)}, f32[512]{0:T(512)S(1)}, u32[]{:S(2)}) copy-start(f32[512]{0:T(512)S(1)} %get-tuple-element.169) | copy-start | bytes 6148
  138.5 7.5 %collective-permute-start.15 = (bf16[96,896]{1,0:T(8,128)(2,1)S(1)}, bf16[96,896]{1,0:T(8,128)(2,1)S(1)}, u32[]{:S(2)}, u32[]{:S(2)}) collective-permute-start(bf16[96,896]{1,0:T(8,128)(2,1)S(1)} %get-tuple-element.216), channel_id=1, source_target_pairs={{0,2},{2,0},{4,6},{6,4},{8,10},{10,8},{12,14},{14,12},{1,3},{3,1},... | collective-permute-start | bytes 516104 | tf_op jit(solution)/shard_map/ppermute | solution.py:535
  139.4 8.5 %collective-permute-start.16 = (bf16[96,896]{1,0:T(8,128)(2,1)S(1)}, bf16[96,896]{1,0:T(8,128)(2,1)S(1)}, u32[]{:S(2)}, u32[]{:S(2)}) collective-permute-start(bf16[96,896]{1,0:T(8,128)(2,1)S(1)} %get-tuple-element.215), channel_id=1, source_target_pairs={{0,4},{2,6},{4,0},{6,2},{8,12},{10,14},{12,8},{14,10},{1,5},{3,7},... | collective-permute-start | bytes 516104 | tf_op jit(solution)/shard_map/ppermute | solution.py:535
  140.8 41.5 %copy-start.59 = (bf16[768,768]{1,0:T(8,128)(2,1)}, bf16[768,768]{1,0:T(8,128)(2,1)S(1)}, u32[]{:S(2)}) copy-start(bf16[768,768]{1,0:T(8,128)(2,1)S(1)} %constant_dynamic-update-slice_fusion.17.dout_ref) | copy-start | bytes 3538948
  140.9 9.2 %collective-permute-start.17 = (bf16[96,896]{1,0:T(8,128)(2,1)S(1)}, bf16[96,896]{1,0:T(8,128)(2,1)S(1)}, u32[]{:S(2)}, u32[]{:S(2)}) collective-permute-start(bf16[96,896]{1,0:T(8,128)(2,1)S(1)} %get-tuple-element.214), channel_id=1, source_target_pairs={{0,6},{2,4},{4,2},{6,0},{8,14},{10,12},{12,10},{14,8},{1,7},{3,5},... | collective-permute-start | bytes 516104 | tf_op jit(solution)/shard_map/ppermute | solution.py:535
  142.1 8.9 %collective-permute-start.18 = (bf16[96,896]{1,0:T(8,128)(2,1)S(1)}, bf16[96,896]{1,0:T(8,128)(2,1)S(1)}, u32[]{:S(2)}, u32[]{:S(2)}) collective-permute-start(bf16[96,896]{1,0:T(8,128)(2,1)S(1)} %get-tuple-element.213), channel_id=1, source_target_pairs={{0,8},{2,10},{4,12},{6,14},{8,0},{10,2},{12,4},{14,6},{1,9},{3,11}... | collective-permute-start | bytes 516104 | tf_op jit(solution)/shard_map/ppermute | solution.py:535
  143.2 33.9 %collective-permute-start.19 = (bf16[96,896]{1,0:T(8,128)(2,1)S(1)}, bf16[96,896]{1,0:T(8,128)(2,1)S(1)}, u32[]{:S(2)}, u32[]{:S(2)}) collective-permute-start(bf16[96,896]{1,0:T(8,128)(2,1)S(1)} %get-tuple-element.212), channel_id=1, source_target_pairs={{0,10},{2,8},{4,14},{6,12},{8,2},{10,0},{12,6},{14,4},{1,11},{3,9}... | collective-permute-start | bytes 516104 | tf_op jit(solution)/shard_map/ppermute | solution.py:535
  146.0 33.8 %collective-permute-start.20 = (bf16[96,896]{1,0:T(8,128)(2,1)S(1)}, bf16[96,896]{1,0:T(8,128)(2,1)S(1)}, u32[]{:S(2)}, u32[]{:S(2)}) collective-permute-start(bf16[96,896]{1,0:T(8,128)(2,1)S(1)} %get-tuple-element.211), channel_id=1, source_target_pairs={{0,12},{2,14},{4,8},{6,10},{8,4},{10,6},{12,0},{14,2},{1,13},{3,15... | collective-permute-start | bytes 516104 | tf_op jit(solution)/shard_map/ppermute | solution.py:535
  147.9 34.5 %collective-permute-start.21 = (bf16[96,896]{1,0:T(8,128)(2,1)S(1)}, bf16[96,896]{1,0:T(8,128)(2,1)S(1)}, u32[]{:S(2)}, u32[]{:S(2)}) collective-permute-start(bf16[96,896]{1,0:T(8,128)(2,1)S(1)} %get-tuple-element.210), channel_id=1, source_target_pairs={{0,14},{2,12},{4,10},{6,8},{8,6},{10,4},{12,2},{14,0},{1,15},{3,13... | collective-permute-start | bytes 516104 | tf_op jit(solution)/shard_map/ppermute | solution.py:535
  221.2 8.8 %collective-permute-start.24 = (bf16[96,896]{1,0:T(8,128)(2,1)S(1)}, bf16[96,896]{1,0:T(8,128)(2,1)S(1)}, u32[]{:S(2)}, u32[]{:S(2)}) collective-permute-start(bf16[96,896]{1,0:T(8,128)(2,1)S(1)} %get-tuple-element.208), channel_id=1, source_target_pairs={{0,2},{2,0},{4,6},{6,4},{8,10},{10,8},{12,14},{14,12},{1,3},{3,1},... | collective-permute-start | bytes 516104 | tf_op jit(solution)/shard_map/ppermute | solution.py:535
  222.0 8.1 %collective-permute-start.25 = (bf16[96,896]{1,0:T(8,128)(2,1)S(1)}, bf16[96,896]{1,0:T(8,128)(2,1)S(1)}, u32[]{:S(2)}, u32[]{:S(2)}) collective-permute-start(bf16[96,896]{1,0:T(8,128)(2,1)S(1)} %get-tuple-element.207), channel_id=1, source_target_pairs={{0,4},{2,6},{4,0},{6,2},{8,12},{10,14},{12,8},{14,10},{1,5},{3,7},... | collective-permute-start | bytes 516104 | tf_op jit(solution)/shard_map/ppermute | solution.py:535
  224.5 8.5 %collective-permute-start.26 = (bf16[96,896]{1,0:T(8,128)(2,1)S(1)}, bf16[96,896]{1,0:T(8,128)(2,1)S(1)}, u32[]{:S(2)}, u32[]{:S(2)}) collective-permute-start(bf16[96,896]{1,0:T(8,128)(2,1)S(1)} %get-tuple-element.206), channel_id=1, source_target_pairs={{0,6},{2,4},{4,2},{6,0},{8,14},{10,12},{12,10},{14,8},{1,7},{3,5},... | collective-permute-start | bytes 516104 | tf_op jit(solution)/shard_map/ppermute | solution.py:535
  227.0 6.9 %collective-permute-start.27 = (bf16[96,896]{1,0:T(8,128)(2,1)S(1)}, bf16[96,896]{1,0:T(8,128)(2,1)S(1)}, u32[]{:S(2)}, u32[]{:S(2)}) collective-permute-start(bf16[96,896]{1,0:T(8,128)(2,1)S(1)} %get-tuple-element.205), channel_id=1, source_target_pairs={{0,8},{2,10},{4,12},{6,14},{8,0},{10,2},{12,4},{14,6},{1,9},{3,11}... | collective-permute-start | bytes 516104 | tf_op jit(solution)/shard_map/ppermute | solution.py:535
  227.0 9.8 %collective-permute-start.28 = (bf16[96,896]{1,0:T(8,128)(2,1)S(1)}, bf16[96,896]{1,0:T(8,128)(2,1)S(1)}, u32[]{:S(2)}, u32[]{:S(2)}) collective-permute-start(bf16[96,896]{1,0:T(8,128)(2,1)S(1)} %get-tuple-element.204), channel_id=1, source_target_pairs={{0,10},{2,8},{4,14},{6,12},{8,2},{10,0},{12,6},{14,4},{1,11},{3,9}... | collective-permute-start | bytes 516104 | tf_op jit(solution)/shard_map/ppermute | solution.py:535
  230.1 7.4 %collective-permute-start.29 = (bf16[96,896]{1,0:T(8,128)(2,1)S(1)}, bf16[96,896]{1,0:T(8,128)(2,1)S(1)}, u32[]{:S(2)}, u32[]{:S(2)}) collective-permute-start(bf16[96,896]{1,0:T(8,128)(2,1)S(1)} %get-tuple-element.203), channel_id=1, source_target_pairs={{0,12},{2,14},{4,8},{6,10},{8,4},{10,6},{12,0},{14,2},{1,13},{3,15... | collective-permute-start | bytes 516104 | tf_op jit(solution)/shard_map/ppermute | solution.py:535
  230.1 10.1 %collective-permute-start.30 = (bf16[96,896]{1,0:T(8,128)(2,1)S(1)}, bf16[96,896]{1,0:T(8,128)(2,1)S(1)}, u32[]{:S(2)}, u32[]{:S(2)}) collective-permute-start(bf16[96,896]{1,0:T(8,128)(2,1)S(1)} %get-tuple-element.202), channel_id=1, source_target_pairs={{0,14},{2,12},{4,10},{6,8},{8,6},{10,4},{12,2},{14,0},{1,15},{3,13... | collective-permute-start | bytes 516104 | tf_op jit(solution)/shard_map/ppermute | solution.py:535
  247.7 16.0 %collective-permute-start.31 = (bf16[512,384]{1,0:T(8,128)(2,1)}, bf16[512,384]{1,0:T(8,128)(2,1)}, u32[]{:S(2)}, u32[]{:S(2)}) collective-permute-start(bf16[512,384]{1,0:T(8,128)(2,1)} %constant_dynamic-slice_fusion.5), channel_id=1, source_target_pairs={{0,4},{4,0},{1,5},{5,1},{2,6},{6,2},{3,7},{7,3},{8,12},{12,8},{9,1... | collective-permute-start | bytes 1179656 | tf_op jit(solution)/shard_map/ppermute | solution.py:83
  253.8 13.1 %collective-permute-start.32 = (bf16[96,768]{1,0:T(8,128)(2,1)}, bf16[96,768]{1,0:T(8,128)(2,1)}, u32[]{:S(2)}, u32[]{:S(2)}) collective-permute-start(bf16[96,768]{1,0:T(8,128)(2,1)} %get-tuple-element.226), channel_id=1, source_target_pairs={{0,2},{2,0},{4,6},{6,4},{8,10},{10,8},{12,14},{14,12},{1,3},{3,1},... | collective-permute-start | bytes 442376 | tf_op jit(solution)/shard_map/ppermute | solution.py:535
  254.5 13.0 %collective-permute-start.33 = (bf16[96,768]{1,0:T(8,128)(2,1)}, bf16[96,768]{1,0:T(8,128)(2,1)}, u32[]{:S(2)}, u32[]{:S(2)}) collective-permute-start(bf16[96,768]{1,0:T(8,128)(2,1)} %get-tuple-element.225), channel_id=1, source_target_pairs={{0,4},{2,6},{4,0},{6,2},{8,12},{10,14},{12,8},{14,10},{1,5},{3,7},... | collective-permute-start | bytes 442376 | tf_op jit(solution)/shard_map/ppermute | solution.py:535
  254.8 47.3 %collective-permute-start.34 = (bf16[96,768]{1,0:T(8,128)(2,1)}, bf16[96,768]{1,0:T(8,128)(2,1)}, u32[]{:S(2)}, u32[]{:S(2)}) collective-permute-start(bf16[96,768]{1,0:T(8,128)(2,1)} %get-tuple-element.224), channel_id=1, source_target_pairs={{0,6},{2,4},{4,2},{6,0},{8,14},{10,12},{12,10},{14,8},{1,7},{3,5},... | collective-permute-start | bytes 442376 | tf_op jit(solution)/shard_map/ppermute | solution.py:535
  257.3 44.9 %collective-permute-start.35 = (bf16[96,768]{1,0:T(8,128)(2,1)}, bf16[96,768]{1,0:T(8,128)(2,1)}, u32[]{:S(2)}, u32[]{:S(2)}) collective-permute-start(bf16[96,768]{1,0:T(8,128)(2,1)} %get-tuple-element.223), channel_id=1, source_target_pairs={{0,8},{2,10},{4,12},{6,14},{8,0},{10,2},{12,4},{14,6},{1,9},{3,11}... | collective-permute-start | bytes 442376 | tf_op jit(solution)/shard_map/ppermute | solution.py:535
  263.7 38.4 %collective-permute-start.36 = (bf16[96,768]{1,0:T(8,128)(2,1)}, bf16[96,768]{1,0:T(8,128)(2,1)S(1)}, u32[]{:S(2)}, u32[]{:S(2)}) collective-permute-start(bf16[96,768]{1,0:T(8,128)(2,1)} %get-tuple-element.222), channel_id=1, source_target_pairs={{0,10},{2,8},{4,14},{6,12},{8,2},{10,0},{12,6},{14,4},{1,11},{3,9}... | collective-permute-start | bytes 442376 | tf_op jit(solution)/shard_map/ppermute | solution.py:535
  266.9 35.3 %collective-permute-start.37 = (bf16[96,768]{1,0:T(8,128)(2,1)S(1)}, bf16[96,768]{1,0:T(8,128)(2,1)S(1)}, u32[]{:S(2)}, u32[]{:S(2)}) collective-permute-start(bf16[96,768]{1,0:T(8,128)(2,1)S(1)} %copy-done.41), channel_id=1, source_target_pairs={{0,12},{2,14},{4,8},{6,10},{8,4},{10,6},{12,0},{14,2},{1,13},{3,15... | collective-permute-start | bytes 442376 | tf_op jit(solution)/shard_map/ppermute | solution.py:535
  267.5 34.7 %collective-permute-start.38 = (bf16[96,768]{1,0:T(8,128)(2,1)S(1)}, bf16[96,768]{1,0:T(8,128)(2,1)S(1)}, u32[]{:S(2)}, u32[]{:S(2)}) collective-permute-start(bf16[96,768]{1,0:T(8,128)(2,1)S(1)} %get-tuple-element.220), channel_id=1, source_target_pairs={{0,14},{2,12},{4,10},{6,8},{8,6},{10,4},{12,2},{14,0},{1,15},{3,13... | collective-permute-start | bytes 442376 | tf_op jit(solution)/shard_map/ppermute | solution.py:535
  302.1 7.1 %collective-permute-start.40 = (bf16[2,2,4,24,768]{4,3,2,1,0:T(8,128)(2,1)S(1)}, bf16[2,2,4,24,768]{4,3,2,1,0:T(8,128)(2,1)S(1)}, u32[]{:S(2)}, u32[]{:S(2)}) collective-permute-start(bf16[2,2,4,24,768]{4,3,2,1,0:T(8,128)(2,1)S(1)} %bitcast.238), channel_id=1, source_target_pairs={{0,1},{1,0},{2,3},{3,2},{4,5},{5,4},{6,7},{7,6},{8,9},{9,8},{10,11... | collective-permute-start | bytes 1769480 | tf_op jit(solution)/shard_map/ppermute | solution.py:83
  303.9 5.6 %collective-permute-start.39 = (bf16[2,2,4,24,1280]{4,3,2,1,0:T(8,128)(2,1)S(1)}, bf16[2,2,4,24,1280]{4,3,2,1,0:T(8,128)(2,1)S(1)}, u32[]{:S(2)}, u32[]{:S(2)}) collective-permute-start(bf16[2,2,4,24,1280]{4,3,2,1,0:T(8,128)(2,1)S(1)} %bitcast.237), channel_id=1, source_target_pairs={{0,1},{1,0},{2,3},{3,2},{4,5},{5,4},{6,7},{7,6},{8,9},{9,8},{10,11... | collective-permute-start | bytes 2949128 | tf_op jit(solution)/shard_map/ppermute | solution.py:83
  310.2 12.0 %collective-permute-start.41 = (bf16[4,24,2048]{2,1,0:T(8,128)(2,1)S(1)}, bf16[4,24,2048]{2,1,0:T(8,128)(2,1)S(1)}, u32[]{:S(2)}, u32[]{:S(2)}) collective-permute-start(bf16[4,24,2048]{2,1,0:T(8,128)(2,1)S(1)} %get-tuple-element.199), channel_id=1, source_target_pairs={{0,2},{2,0},{4,6},{6,4},{1,3},{3,1},{5,7},{7,5},{8,10},{10,8},{12,... | collective-permute-start | bytes 1179656 | tf_op jit(solution)/shard_map/ppermute | solution.py:647
  313.6 16.0 %collective-permute-start.44 = (bf16[4,24,2048]{2,1,0:T(8,128)(2,1)S(1)}, bf16[4,24,2048]{2,1,0:T(8,128)(2,1)S(1)}, u32[]{:S(2)}, u32[]{:S(2)}) collective-permute-start(bf16[4,24,2048]{2,1,0:T(8,128)(2,1)S(1)} %get-tuple-element.198), channel_id=1, source_target_pairs={{0,6},{2,4},{4,2},{6,0},{1,7},{3,5},{5,3},{7,1},{8,14},{10,12},{12... | collective-permute-start | bytes 1179656 | tf_op jit(solution)/shard_map/ppermute | solution.py:647
  314.7 20.5 %collective-permute-start.43 = (bf16[4,24,2048]{2,1,0:T(8,128)(2,1)S(1)}, bf16[4,24,2048]{2,1,0:T(8,128)(2,1)S(1)}, u32[]{:S(2)}, u32[]{:S(2)}) collective-permute-start(bf16[4,24,2048]{2,1,0:T(8,128)(2,1)S(1)} %get-tuple-element.197), channel_id=1, source_target_pairs={{0,4},{2,6},{4,0},{6,2},{1,5},{3,7},{5,1},{7,3},{8,12},{10,14},{12... | collective-permute-start | bytes 1179656 | tf_op jit(solution)/shard_map/ppermute | solution.py:647
  324.7 28.6 %collective-permute-start.42 = (bf16[512,768]{1,0:T(8,128)(2,1)}, bf16[512,768]{1,0:T(8,128)(2,1)S(1)}, u32[]{:S(2)}, u32[]{:S(2)}) collective-permute-start(bf16[512,768]{1,0:T(8,128)(2,1)} %dynamic-slice_convert_fusion), channel_id=1, source_target_pairs={{0,4},{4,0},{1,5},{5,1},{2,6},{6,2},{3,7},{7,3},{8,12},{12,8},{9,1... | collective-permute-start | bytes 2359304 | tf_op jit(solution)/shard_map/ppermute | solution.py:83
  351.3 6.8 %collective-permute-start.47 = (bf16[24,3200]{1,0:T(8,128)(2,1)S(1)}, bf16[24,3200]{1,0:T(8,128)(2,1)S(1)}, u32[]{:S(2)}, u32[]{:S(2)}) collective-permute-start(bf16[24,3200]{1,0:T(8,128)(2,1)S(1)} %get-tuple-element.241), channel_id=1, source_target_pairs={{0,24},{8,0},{16,8},{24,16},{1,25},{9,1},{17,9},{25,17},{2,26},{10... | collective-permute-start | bytes 460808 | tf_op jit(solution)/shard_map/ppermute | solution.py:110
  352.5 13.2 %collective-permute-start.46 = (bf16[24,3200]{1,0:T(8,128)(2,1)S(1)}, bf16[24,3200]{1,0:T(8,128)(2,1)S(1)}, u32[]{:S(2)}, u32[]{:S(2)}) collective-permute-start(bf16[24,3200]{1,0:T(8,128)(2,1)S(1)} %get-tuple-element.242), channel_id=1, source_target_pairs={{0,16},{8,24},{16,0},{24,8},{1,17},{9,25},{17,1},{25,9},{2,18},{10... | collective-permute-start | bytes 460808 | tf_op jit(solution)/shard_map/ppermute | solution.py:110
  352.5 13.2 %collective-permute-start.45 = (bf16[24,3200]{1,0:T(8,128)(2,1)S(1)}, bf16[24,3200]{1,0:T(8,128)(2,1)S(1)}, u32[]{:S(2)}, u32[]{:S(2)}) collective-permute-start(bf16[24,3200]{1,0:T(8,128)(2,1)S(1)} %get-tuple-element.240), channel_id=1, source_target_pairs={{0,8},{8,16},{16,24},{24,0},{1,9},{9,17},{17,25},{25,1},{2,10},{10... | collective-permute-start | bytes 460808 | tf_op jit(solution)/shard_map/ppermute | solution.py:110
  354.0 28.9 %collective-permute-start.49 = (bf16[3,96,2048]{2,1,0:T(8,128)(2,1)S(1)}, bf16[3,96,2048]{2,1,0:T(8,128)(2,1)S(1)}, u32[]{:S(2)}, u32[]{:S(2)}) collective-permute-start(bf16[3,96,2048]{2,1,0:T(8,128)(2,1)S(1)} %get-tuple-element.191), channel_id=1, source_target_pairs={{0,4},{1,12},{4,0},{5,8},{8,5},{9,13},{12,1},{13,9},{2,6},{3,14},{... | collective-permute-start | bytes 3538952 | tf_op jit(solution)/shard_map/ppermute | solution.py:457
  355.5 27.4 %collective-permute-start.48 = (bf16[3,96,2048]{2,1,0:T(8,128)(2,1)S(1)}, bf16[3,96,2048]{2,1,0:T(8,128)(2,1)S(1)}, u32[]{:S(2)}, u32[]{:S(2)}) collective-permute-start(bf16[3,96,2048]{2,1,0:T(8,128)(2,1)S(1)} %get-tuple-element.192), channel_id=1, source_target_pairs={{1,8},{8,1},{3,10},{10,3},{5,12},{12,5},{7,14},{14,7},{17,24},{24,... | collective-permute-start | bytes 3538952 | tf_op jit(solution)/shard_map/ppermute | solution.py:448
  398.0 7.0 %collective-permute-start.50 = (f32[2,128]{1,0:T(2,128)S(1)}, f32[2,128]{1,0:T(2,128)S(1)}, u32[]{:S(2)}, u32[]{:S(2)}) collective-permute-start(f32[2,128]{1,0:T(2,128)S(1)} %pad_bitcast_fusion), channel_id=1, source_target_pairs={{0,1},{1,0},{2,3},{3,2},{4,5},{5,4},{6,7},{7,6},{8,9},{9,8},{10,11... | collective-permute-start | bytes 3080 | tf_op jit(solution)/shard_map/ppermute | solution.py:133
  405.0 3.6 collective-permute-start.52
  406.7 4.5 %collective-permute-start.53 = (f32[2,128]{1,0:T(2,128)S(1)}, f32[2,128]{1,0:T(2,128)S(1)}, u32[]{:S(2)}, u32[]{:S(2)}) collective-permute-start(f32[2,128]{1,0:T(2,128)S(1)} %fusion.119), channel_id=1, source_target_pairs={{0,6},{2,4},{4,2},{6,0},{1,7},{3,5},{5,3},{7,1},{8,14},{10,12},{12... | collective-permute-start | bytes 3080 | tf_op jit(solution)/shard_map/ppermute | solution.py:133
  408.2 3.6 collective-permute-start.51
  411.7 8.6 %collective-permute-start.55 = (f32[2,128]{1,0:T(2,128)S(1)}, f32[2,128]{1,0:T(2,128)S(1)}, u32[]{:S(2)}, u32[]{:S(2)}) collective-permute-start(f32[2,128]{1,0:T(2,128)S(1)} %add_add_fusion.1), channel_id=1, source_target_pairs={{0,16},{8,24},{16,0},{24,8},{1,17},{9,25},{17,1},{25,9},{2,18},{10... | collective-permute-start | bytes 3080 | tf_op jit(solution)/shard_map/ppermute | solution.py:133
  413.3 7.1 %collective-permute-start.56 = (f32[2,128]{1,0:T(2,128)S(1)}, f32[2,128]{1,0:T(2,128)S(1)}, u32[]{:S(2)}, u32[]{:S(2)}) collective-permute-start(f32[2,128]{1,0:T(2,128)S(1)} %add_add_fusion.1), channel_id=1, source_target_pairs={{0,24},{8,16},{16,8},{24,0},{1,25},{9,17},{17,9},{25,1},{2,26},{10... | collective-permute-start | bytes 3080 | tf_op jit(solution)/shard_map/ppermute | solution.py:133
  415.9 4.4 %collective-permute-start.54 = (f32[2,128]{1,0:T(2,128)S(1)}, f32[2,128]{1,0:T(2,128)S(1)}, u32[]{:S(2)}, u32[]{:S(2)}) collective-permute-start(f32[2,128]{1,0:T(2,128)S(1)} %add_add_fusion.1), channel_id=1, source_target_pairs={{0,8},{8,0},{16,24},{24,16},{1,9},{9,1},{17,25},{25,17},{2,10},{10... | collective-permute-start | bytes 3080 | tf_op jit(solution)/shard_map/ppermute | solution.py:133
  (98 other events, 726.3 us)
Sparse Core Ops, SparseCore 0:
  35.0 76.7 all-gather.2
  113.3 62.7 all-gather.4
  215.3 133.9 reduce-scatter.1

commit v5 on v4

--- a/solution.py
+++ b/solution.py
@@ -736,7 +736,7 @@
             expert_master, expert_first, expert_second, expert_sum
         )
 
-        expert_u = lax.optimization_barrier(expert_u)
+        expert_kept = lax.optimization_barrier(expert_u.astype(bf16)).astype(f32)
 
         def squares(attention_x, vector_x, expert_x):
             vector_parts = jnp.sum(vector_x * vector_x, axis=1)
@@ -792,7 +792,7 @@
             input_gradient[None],
             attention_master - ratios[0:4][:, None, None] * attention_u,
             vector_master - vector_ratio * vector_u,
-            expert_master - expert_ratio * expert_u,
+            expert_master - expert_ratio * expert_kept,
             mixing_master - ratios[count] * mixing_u,
             attention_m,
             vector_m,

time: 448 us -> 447 us (level)
    convert_element_type x0 -> x1, other arithmetic: none -> 8.74 us  [shards(): expert_kept = lax.optimization_barrier(expert_u.astype(bf16)).astype(f32)]
    add x1 -> x0, other arithmetic: 8.67 us -> none  [moments(): first_new / (1.0 - beta_one ** STEP)]
    unnamed x244 -> x240, local copies, waits for them, and re-layouts: 23.2 us -> 23.4 us
  transfers between devices with their start and end apart: 60 -> 60, of which waited for: 27 -> 26; matrix products, arithmetic and copies ran while one was open for 20% -> 20% of each run, Pallas kernels for 11% -> 11%
where the time goes in v5:
time: 447 us; the launch traced here: 441 us
  waiting for transfers between devices  130 us (29%)
  starting transfers between devices  87.5 us (20%)
  Pallas kernels  82.2 us (18%)
  other arithmetic  54 us (12%)
  local copies, waits for them, and re-layouts  51.8 us (12%)
  matrix products  19.6 us (4%)
  between operations  15.9 us (4%)
    ppermute x28, waiting for transfers between devices, exchange(): lax.ppermute(blocks[k], ep_axes, [(i, i ^ k) for i in range(NFFN)])  39 us
    ppermute x28, starting transfers between devices, exchange(): lax.ppermute(blocks[k], ep_axes, [(i, i ^ k) for i in range(NFFN)])  38.7 us
    pallas_call x1, Pallas kernels, expert_compute(): pl.pallas_call(expert_kernel, grid=(hidden // FF_COLUMNS,), in_specs=[pl....  32 us
    pallas_call x1, Pallas kernels, attention_backward(): pl.pallas_call(attention_backward_kernel, grid=(pairs,), in_specs=[full((...  31.3 us
    ppermute x2, waiting for transfers between devices, cross(): lax.ppermute(other_y, ('dp_near', 'seq', 'core'), moves)  28.2 us
    unnamed x240, local copies, waits for them, and re-layouts  23.4 us
    pallas_call x1, Pallas kernels, attention_forward(): pl.pallas_call(attention_forward_kernel, grid=(pairs,), in_specs=[full((l...  18.8 us
    ppermute x8, starting transfers between devices, swap(): return lax.ppermute(value, axis_name, [(0, 1), (1, 0)])  18.4 us
  transfers between devices with their start and end apart: 60, of which 26 were waited for; matrix products, arithmetic and copies ran while one was open for 20% of the time, Pallas kernels for 11%

profile of v5, /device:TPU:0, one launch (start us, length us, event | category | flops | bytes accessed | tf_op | source)
XLA Modules:
  0.0 441.1 jit_solution(17102077476587765466)
XLA Ops:
  9.8 3.0 collective-permute-start.1
  12.9 2.8 collective-permute-done.1
  15.7 1.9 collective-permute-start.2
  17.7 2.6 collective-permute-start.3
  21.6 2.7 convert_element_type.195
  28.6 3.6 collective-permute-done.3
  42.3 7.6 %collective-permute-done.5 = bf16[4,2,24,2048]{3,2,1,0:T(8,128)(2,1)S(1)} collective-permute-done((bf16[4,2,24,2048]{3,2,1,0:T(8,128)(2,1)}, bf16[4,2,24,2048]{3,2,1,0:T(8,128)(2,1)S(1)}, u32[]{:S(2)}, u32[]{:S(2)}) %collective-permute-start.5) | collective-permute-done | bytes 786464 | tf_op jit(solution)/shard_map/ppermute | solution.py:100
  50.0 10.4 %collective-permute-start.6 = (bf16[2,4,2,24,2048]{4,3,0,2,1:T(8,128)(2,1)S(1)}, bf16[2,4,2,24,2048]{4,3,0,2,1:T(8,128)(2,1)}, u32[]{:S(2)}, u32[]{:S(2)}) collective-permute-start(bf16[2,4,2,24,2048]{4,3,0,2,1:T(8,128)(2,1)S(1)} %bitcast_dynamic-update-slice_fusion.1), channel_id=1, source_target_pairs={{0,1},{1,0},{2,3},{3,2},{4,5},{5,4},{6,7},{7,6},{8,9},{9,8},{10,11... | collective-permute-start | bytes 4718600 | tf_op jit(solution)/shard_map/ppermute | solution.py:83
  61.0 1.6 fusion.34
  62.6 2.2 convolution_convert_fusion.1
  64.8 2.4 broadcast_select_fusion.3
  67.2 13.6 %collective-permute-done.23 = bf16[3,96,2048]{2,1,0:T(8,128)(2,1)} collective-permute-done((bf16[3,96,2048]{2,1,0:T(8,128)(2,1)}, bf16[3,96,2048]{2,1,0:T(8,128)(2,1)}, u32[]{:S(2)}, u32[]{:S(2)}) %collective-permute-start.23) | collective-permute-done | bytes 1179680 | tf_op jit(solution)/shard_map/ppermute | solution.py:457
  80.9 1.6 pad_maximum_fusion.2.x_ref
  84.9 1.5 collective-permute-start.8
  87.1 4.1 collective-permute-start.10
  91.3 1.6 select_bitcast_fusion.1
  97.6 1.8 collective-permute-start.12
  99.4 2.0 collective-permute-start.13
  103.6 18.8 %shard_map.298 = (bf16[1024,768]{1,0:T(8,128)(2,1)S(1)}, bf16[1024,384]{1,0:T(8,128)(2,1)S(1)}, bf16[1024,384]{1,0:T(8,128)(2,1)S(1)}, bf16[1024,384]{1,0:T(8,12...) custom-call(bf16[1024,768]{1,0:T(8,128)(2,1)S(1)} %pad_maximum_fusion.2.x_ref, ...), custom_call_target="tpu_custom_call" | custom-call | flops 3422552064 | bytes 6291456 | tf_op jit(solution)/shard_map/pallas_call | solution.py:197
  128.6 3.1 collective-permute-done.14
  132.0 2.3 multiply_reduce_fusion.4
  136.0 1.8 fusion.11
  140.8 1.5 collective-permute-start.17
  144.4 1.6 collective-permute-done.15
  148.0 2.2 collective-permute-start.21
  152.3 25.0 %collective-permute-done.19 = bf16[96,896]{1,0:T(8,128)(2,1)S(1)} collective-permute-done((bf16[96,896]{1,0:T(8,128)(2,1)S(1)}, bf16[96,896]{1,0:T(8,128)(2,1)S(1)}, u32[]{:S(2)}, u32[]{:S(2)}) %collective-permute-start.19) | collective-permute-done | bytes 172064 | tf_op jit(solution)/shard_map/ppermute | solution.py:535
  178.0 1.9 collective-permute-done.20
  180.6 1.9 collective-permute-done.21
  183.2 32.0 %shard_map.299 = (bf16[768,768]{1,0:T(8,128)(2,1)}, bf16[768,896]{1,0:T(8,128)(2,1)}, bf16[3,768,2048]{2,1,0:T(8,128)(2,1)}) custom-call(s32[1]{0:T(128)} %bitcast.34.flipped_ref, bf16[768,896]{1,0:T(8,128)(2,1)} %constant_dynamic-update-slice_fusion.10.taken_ref, bf16[768,768]{1,0:T(8,128)(2,1)} %copy-done.59, ...), custom_call_target="tpu_custom_call" | custom-call | flops 24159191040 | bytes 18874368 | tf_op jit(solution)/shard_map/pallas_call | solution.py:380
  222.0 2.6 collective-permute-start.26
  224.6 2.2 collective-permute-start.28
  228.0 2.8 collective-permute-start.30
  231.8 2.9 collective-permute-done.28
  236.0 2.2 collective-permute-done.30
  240.0 1.7 multiply_reduce_fusion.2
  242.2 2.9 convolution_convert_fusion.2
  245.8 1.7 collective-permute-start.31
  248.4 1.8 convolution_convert_fusion
  253.1 2.2 collective-permute-start.34
  255.5 2.3 constant_dynamic-slice_fusion.2
  261.5 1.8 collective-permute-start.36
  265.5 3.2 collective-permute-start.38
  268.8 31.3 %shard_map.300 = (bf16[768,1280]{1,0:T(8,128)(2,1)}, f32[1024,768]{1,0:T(8,128)}) custom-call(bf16[1024,768]{1,0:T(8,128)(2,1)S(1)} %copy-done.7, bf16[1024,768]{1,0:T(8,128)(2,1)} %copy-done.1, f32[768,128]{1,0:T(8,128)S(1)} %pad.14.vector_ref, bf16[1024,384]{1,0:T(8,128)(2,1)S(1)} %copy-done.9, bf16[1024,384]{1,0:T(8,128)(2,1)S(1)} %copy-done.11, ...), custom_call_target="tpu_custom_call" | custom-call | flops 7650410496 | bytes 9437184 | tf_op jit(solution)/shard_map/pallas_call | solution.py:271
  300.2 1.6 constant_dynamic-slice_fusion.4
  308.8 2.5 fusion.41
  312.7 1.7 collective-permute-start.43
  314.4 5.9 %collective-permute-done.41 = bf16[4,24,2048]{2,1,0:T(8,128)(2,1)S(1)} collective-permute-done((bf16[4,24,2048]{2,1,0:T(8,128)(2,1)S(1)}, bf16[4,24,2048]{2,1,0:T(8,128)(2,1)S(1)}, u32[]{:S(2)}, u32[]{:S(2)}) %collective-permute-start.41) | collective-permute-done | bytes 393248 | tf_op jit(solution)/shard_map/ppermute | solution.py:647
  320.4 1.5 dynamic-slice_convert_fusion
  322.3 5.4 %collective-permute-done.44 = bf16[4,24,2048]{2,1,0:T(8,128)(2,1)S(1)} collective-permute-done((bf16[4,24,2048]{2,1,0:T(8,128)(2,1)S(1)}, bf16[4,24,2048]{2,1,0:T(8,128)(2,1)S(1)}, u32[]{:S(2)}, u32[]{:S(2)}) %collective-permute-start.44) | collective-permute-done | bytes 393248 | tf_op jit(solution)/shard_map/ppermute | solution.py:647
  327.7 5.5 %collective-permute-done.43 = bf16[4,24,2048]{2,1,0:T(8,128)(2,1)S(1)} collective-permute-done((bf16[4,24,2048]{2,1,0:T(8,128)(2,1)S(1)}, bf16[4,24,2048]{2,1,0:T(8,128)(2,1)S(1)}, u32[]{:S(2)}, u32[]{:S(2)}) %collective-permute-start.43) | collective-permute-done | bytes 393248 | tf_op jit(solution)/shard_map/ppermute | solution.py:647
  333.5 15.8 %reduce-scatter.2.cloned.1.call-done = bf16[3,192,2048]{2,1,0:T(8,128)(2,1)} async-done(((bf16[3,768,2048]{2,1,0:T(8,128)(2,1)}), bf16[3,192,2048]{2,1,0:T(8,128)(2,1)}) %reduce-scatter.2.cloned.1.call-update) | async-done | bytes 2359312 | tf_op jit(solution)/shard_map/reduce_scatter | solution.py:590
  349.2 2.0 dynamic-slice_bitcast_fusion
  354.3 1.5 collective-permute-start.49
  358.1 7.7 %collective-permute-done.46 = bf16[24,3200]{1,0:T(8,128)(2,1)S(1)} collective-permute-done((bf16[24,3200]{1,0:T(8,128)(2,1)S(1)}, bf16[24,3200]{1,0:T(8,128)(2,1)S(1)}, u32[]{:S(2)}, u32[]{:S(2)}) %collective-permute-start.46) | collective-permute-done | bytes 153632 | tf_op jit(solution)/shard_map/ppermute | solution.py:110
  368.5 14.6 %collective-permute-done.49 = bf16[3,96,2048]{2,1,0:T(8,128)(2,1)S(1)} collective-permute-done((bf16[3,96,2048]{2,1,0:T(8,128)(2,1)S(1)}, bf16[3,96,2048]{2,1,0:T(8,128)(2,1)S(1)}, u32[]{:S(2)}, u32[]{:S(2)}) %collective-permute-start.49) | collective-permute-done | bytes 1179680 | tf_op jit(solution)/shard_map/ppermute | solution.py:457
  383.4 8.7 %fusion.124 = (bf16[2,3,96,2048]{3,2,1,0:T(8,128)(2,1)S(1)}, f32[2,3,96,2048]{3,2,1,0:T(8,128)}, f32[2,3,96,2048]{3,2,1,0:T(8,128)}, f32[2,3,96,2048]{3,2,1,0:T(8,128)}, f32[2,3]{1,0:T(2,128)S(1)}) fusion(f32[2,3,96,2048]{3,2,1,0:T(8,128)S(1)} %bitcast.223, bf16[1,3,96,2048]{3,2,1,0:T(8,128)(2,1)S(1)} %get-tuple-element.189, ...), kind=kLoop, calls=%fused_computation.359 | loop fusion | flops 21233658 | bytes 33030168 | tf_op jit(solution)/shard_map/convert_element_type | solution.py:739
  392.2 2.9 multiply_reduce_fusion
  395.6 2.6 concatenate.118
  398.2 6.1 %collective-permute-start.50 = (f32[2,128]{1,0:T(2,128)S(1)}, f32[2,128]{1,0:T(2,128)S(1)}, u32[]{:S(2)}, u32[]{:S(2)}) collective-permute-start(f32[2,128]{1,0:T(2,128)S(1)} %pad_bitcast_fusion), channel_id=1, source_target_pairs={{0,1},{1,0},{2,3},{3,2},{4,5},{5,4},{6,7},{7,6},{8,9},{9,8},{10,11... | collective-permute-start | bytes 3080 | tf_op jit(solution)/shard_map/ppermute | solution.py:133
  405.1 1.7 collective-permute-start.52
  408.7 2.6 collective-permute-done.53
  412.2 3.6 collective-permute-start.56
  415.9 3.8 fusion.18
  426.4 5.8 %multiply_subtract_fusion = f32[2,3,96,2048]{3,2,1,0:T(8,128)} fusion(f32[2,3,96,2048]{3,2,1,0:T(8,128)} %param.26, bf16[2,3,96,2048]{3,2,1,0:T(8,128)(2,1)S(1)} %get-tuple-element.176, f32[2,3]{1,0:T(2,128)S(1)} %constant_dynamic-slice_fusion), kind=kLoop, calls=%fused_computation.4 | loop fusion | flops 3538944 | bytes 11796504 | tf_op jit(solution)/shard_map/sub | solution.py:795
  (464 shorter events, 100.8 us)
Async XLA Ops:
  7.2 176.0 %all-gather.3.cloned.1.call-start = ((), (), s32[]{:S(2)}) async-start(), calls=%async_computation.1 | async-start | bytes 5898240 | tf_op jit(solution)/shard_map/all_gather | solution.py:478
  9.8 5.8 %collective-permute-start.1 = (bf16[24,2048]{1,0:T(8,128)(2,1)S(1)}, bf16[24,2048]{1,0:T(8,128)(2,1)S(1)}, u32[]{:S(2)}, u32[]{:S(2)}) collective-permute-start(bf16[24,2048]{1,0:T(8,128)(2,1)S(1)} %get-tuple-element.280), channel_id=1, source_target_pairs={{0,4},{4,0},{1,5},{5,1},{2,6},{6,2},{3,7},{7,3},{8,12},{12,8},{9,1... | collective-permute-start | bytes 294920 | tf_op jit(solution)/shard_map/ppermute | solution.py:83
  15.7 12.2 %collective-permute-start.2 = (bf16[2,24,2048]{2,1,0:T(8,128)(2,1)S(1)}, bf16[2,24,2048]{2,1,0:T(8,128)(2,1)S(1)}, u32[]{:S(2)}, u32[]{:S(2)}) collective-permute-start(bf16[2,24,2048]{2,1,0:T(8,128)(2,1)S(1)} %pad_maximum_fusion.10), channel_id=1, source_target_pairs={{0,8},{8,16},{16,24},{24,0},{1,9},{9,17},{17,25},{25,1},{2,10},{10... | collective-permute-start | bytes 589832 | tf_op jit(solution)/shard_map/ppermute | solution.py:100
  17.7 14.6 %collective-permute-start.3 = (bf16[2,24,2048]{2,1,0:T(8,128)(2,1)S(1)}, bf16[2,24,2048]{2,1,0:T(8,128)(2,1)S(1)}, u32[]{:S(2)}, u32[]{:S(2)}) collective-permute-start(bf16[2,24,2048]{2,1,0:T(8,128)(2,1)S(1)} %pad_maximum_fusion.10), channel_id=1, source_target_pairs={{0,16},{8,24},{16,0},{24,8},{1,17},{9,25},{17,1},{25,9},{2,18},{10... | collective-permute-start | bytes 589832 | tf_op jit(solution)/shard_map/ppermute | solution.py:100
  20.2 12.7 %collective-permute-start.4 = (bf16[2,24,2048]{2,1,0:T(8,128)(2,1)S(1)}, bf16[2,24,2048]{2,1,0:T(8,128)(2,1)S(1)}, u32[]{:S(2)}, u32[]{:S(2)}) collective-permute-start(bf16[2,24,2048]{2,1,0:T(8,128)(2,1)S(1)} %pad_maximum_fusion.10), channel_id=1, source_target_pairs={{0,24},{8,0},{16,8},{24,16},{1,25},{9,1},{17,9},{25,17},{2,26},{10... | collective-permute-start | bytes 589832 | tf_op jit(solution)/shard_map/ppermute | solution.py:100
  25.5 8.1 %collective-permute-start.22 = (bf16[3,96,2048]{2,1,0:T(8,128)(2,1)S(1)}, bf16[3,96,2048]{2,1,0:T(8,128)(2,1)S(1)}, u32[]{:S(2)}, u32[]{:S(2)}) collective-permute-start(bf16[3,96,2048]{2,1,0:T(8,128)(2,1)S(1)} %get-tuple-element.195), channel_id=1, source_target_pairs={{1,8},{8,1},{3,10},{10,3},{5,12},{12,5},{7,14},{14,7},{17,24},{24,... | collective-permute-start | bytes 3538952 | tf_op jit(solution)/shard_map/ppermute | solution.py:448
  34.8 148.4 %all-gather.5.cloned.1.call-start = ((), (), s32[]{:S(2)}) async-start(), calls=%async_computation.2 | async-start | bytes 5898240 | tf_op jit(solution)/shard_map/all_gather | solution.py:481
  34.9 29.9 %collective-permute-start = (bf16[512,768]{1,0:T(8,128)(2,1)S(1)}, bf16[512,768]{1,0:T(8,128)(2,1)}, u32[]{:S(2)}, u32[]{:S(2)}) collective-permute-start(bf16[512,768]{1,0:T(8,128)(2,1)S(1)} %bitcast.228), channel_id=1, source_target_pairs={{0,4},{4,0},{1,5},{5,1},{2,6},{6,2},{3,7},{7,3},{8,12},{12,8},{9,1... | collective-permute-start | bytes 2359304 | tf_op jit(solution)/shard_map/ppermute | solution.py:83
  37.7 12.2 %collective-permute-start.5 = (bf16[4,2,24,2048]{3,2,1,0:T(8,128)(2,1)}, bf16[4,2,24,2048]{3,2,1,0:T(8,128)(2,1)S(1)}, u32[]{:S(2)}, u32[]{:S(2)}) collective-permute-start(bf16[4,2,24,2048]{3,2,1,0:T(8,128)(2,1)} %bitcast_dynamic-update-slice_fusion.2), channel_id=1, source_target_pairs={{0,2},{2,0},{1,3},{3,1},{4,6},{6,4},{5,7},{7,5},{8,10},{10,8},{9,1... | collective-permute-start | bytes 2359304 | tf_op jit(solution)/shard_map/ppermute | solution.py:100
  40.3 40.4 %collective-permute-start.23 = (bf16[3,96,2048]{2,1,0:T(8,128)(2,1)}, bf16[3,96,2048]{2,1,0:T(8,128)(2,1)}, u32[]{:S(2)}, u32[]{:S(2)}) collective-permute-start(bf16[3,96,2048]{2,1,0:T(8,128)(2,1)} %get-tuple-element.194), channel_id=1, source_target_pairs={{0,4},{1,12},{4,0},{5,8},{8,5},{9,13},{12,1},{13,9},{2,6},{3,14},{... | collective-permute-start | bytes 3538952 | tf_op jit(solution)/shard_map/ppermute | solution.py:457
  50.0 41.3 %collective-permute-start.6 = (bf16[2,4,2,24,2048]{4,3,0,2,1:T(8,128)(2,1)S(1)}, bf16[2,4,2,24,2048]{4,3,0,2,1:T(8,128)(2,1)}, u32[]{:S(2)}, u32[]{:S(2)}) collective-permute-start(bf16[2,4,2,24,2048]{4,3,0,2,1:T(8,128)(2,1)S(1)} %bitcast_dynamic-update-slice_fusion.1), channel_id=1, source_target_pairs={{0,1},{1,0},{2,3},{3,2},{4,5},{5,4},{6,7},{7,6},{8,9},{9,8},{10,11... | collective-permute-start | bytes 4718600 | tf_op jit(solution)/shard_map/ppermute | solution.py:83
  61.0 177.2 %copy-start.66 = (s32[512,1]{0,1:T(1,128)}, s32[512,1]{0,1:T(1,128)S(1)}, u32[]{:S(2)}) copy-start(s32[512,1]{0,1:T(1,128)S(1)} %get-tuple-element.282) | copy-start | bytes 6148
  80.8 268.4 %reduce-scatter.2.cloned.1.call-start = ((), (), s32[]{:S(2)}) async-start(), calls=%async_computation.3 | async-start | bytes 11796480 | tf_op jit(solution)/shard_map/reduce_scatter | solution.py:590
  83.6 13.9 %collective-permute-start.7 = (bf16[96,768]{1,0:T(8,128)(2,1)}, bf16[96,768]{1,0:T(8,128)(2,1)}, u32[]{:S(2)}, u32[]{:S(2)}) collective-permute-start(bf16[96,768]{1,0:T(8,128)(2,1)} %get-tuple-element.239), channel_id=1, source_target_pairs={{0,2},{2,0},{4,6},{6,4},{8,10},{10,8},{12,14},{14,12},{1,3},{3,1},... | collective-permute-start | bytes 442376 | tf_op jit(solution)/shard_map/ppermute | solution.py:535
  84.9 14.6 %collective-permute-start.8 = (bf16[96,768]{1,0:T(8,128)(2,1)}, bf16[96,768]{1,0:T(8,128)(2,1)}, u32[]{:S(2)}, u32[]{:S(2)}) collective-permute-start(bf16[96,768]{1,0:T(8,128)(2,1)} %get-tuple-element.238), channel_id=1, source_target_pairs={{0,4},{2,6},{4,0},{6,2},{8,12},{10,14},{12,8},{14,10},{1,5},{3,7},... | collective-permute-start | bytes 442376 | tf_op jit(solution)/shard_map/ppermute | solution.py:535
  86.4 36.1 %collective-permute-start.9 = (bf16[96,768]{1,0:T(8,128)(2,1)}, bf16[96,768]{1,0:T(8,128)(2,1)}, u32[]{:S(2)}, u32[]{:S(2)}) collective-permute-start(bf16[96,768]{1,0:T(8,128)(2,1)} %get-tuple-element.237), channel_id=1, source_target_pairs={{0,6},{2,4},{4,2},{6,0},{8,14},{10,12},{12,10},{14,8},{1,7},{3,5},... | collective-permute-start | bytes 442376 | tf_op jit(solution)/shard_map/ppermute | solution.py:535
  87.1 35.3 %collective-permute-start.10 = (bf16[96,768]{1,0:T(8,128)(2,1)}, bf16[96,768]{1,0:T(8,128)(2,1)}, u32[]{:S(2)}, u32[]{:S(2)}) collective-permute-start(bf16[96,768]{1,0:T(8,128)(2,1)} %get-tuple-element.236), channel_id=1, source_target_pairs={{0,8},{2,10},{4,12},{6,14},{8,0},{10,2},{12,4},{14,6},{1,9},{3,11}... | collective-permute-start | bytes 442376 | tf_op jit(solution)/shard_map/ppermute | solution.py:535
  91.3 31.2 %collective-permute-start.11 = (bf16[96,768]{1,0:T(8,128)(2,1)}, bf16[96,768]{1,0:T(8,128)(2,1)}, u32[]{:S(2)}, u32[]{:S(2)}) collective-permute-start(bf16[96,768]{1,0:T(8,128)(2,1)} %get-tuple-element.235), channel_id=1, source_target_pairs={{0,10},{2,8},{4,14},{6,12},{8,2},{10,0},{12,6},{14,4},{1,11},{3,9}... | collective-permute-start | bytes 442376 | tf_op jit(solution)/shard_map/ppermute | solution.py:535
  97.6 24.9 %collective-permute-start.12 = (bf16[96,768]{1,0:T(8,128)(2,1)}, bf16[96,768]{1,0:T(8,128)(2,1)S(1)}, u32[]{:S(2)}, u32[]{:S(2)}) collective-permute-start(bf16[96,768]{1,0:T(8,128)(2,1)} %get-tuple-element.234), channel_id=1, source_target_pairs={{0,12},{2,14},{4,8},{6,10},{8,4},{10,6},{12,0},{14,2},{1,13},{3,15... | collective-permute-start | bytes 442376 | tf_op jit(solution)/shard_map/ppermute | solution.py:535
  99.4 23.1 %collective-permute-start.13 = (bf16[96,768]{1,0:T(8,128)(2,1)}, bf16[96,768]{1,0:T(8,128)(2,1)S(1)}, u32[]{:S(2)}, u32[]{:S(2)}) collective-permute-start(bf16[96,768]{1,0:T(8,128)(2,1)} %get-tuple-element.233), channel_id=1, source_target_pairs={{0,14},{2,12},{4,10},{6,8},{8,6},{10,4},{12,2},{14,0},{1,15},{3,13... | collective-permute-start | bytes 442376 | tf_op jit(solution)/shard_map/ppermute | solution.py:535
  122.5 9.2 %collective-permute-start.14 = (bf16[512,384]{1,0:T(8,128)(2,1)S(1)}, bf16[512,384]{1,0:T(8,128)(2,1)S(1)}, u32[]{:S(2)}, u32[]{:S(2)}) collective-permute-start(bf16[512,384]{1,0:T(8,128)(2,1)S(1)} %constant_dynamic-slice_fusion.6), channel_id=1, source_target_pairs={{0,4},{4,0},{1,5},{5,1},{2,6},{6,2},{3,7},{7,3},{8,12},{12,8},{9,1... | collective-permute-start | bytes 1179656 | tf_op jit(solution)/shard_map/ppermute | solution.py:83
  135.4 84.4 %copy-start.55 = (f32[512]{0:T(512)}, f32[512]{0:T(512)S(1)}, u32[]{:S(2)}) copy-start(f32[512]{0:T(512)S(1)} %get-tuple-element.168) | copy-start | bytes 6148
  135.4 84.4 %copy-start.57 = (f32[512]{0:T(512)}, f32[512]{0:T(512)S(1)}, u32[]{:S(2)}) copy-start(f32[512]{0:T(512)S(1)} %get-tuple-element.169) | copy-start | bytes 6148
  138.7 7.4 %collective-permute-start.15 = (bf16[96,896]{1,0:T(8,128)(2,1)S(1)}, bf16[96,896]{1,0:T(8,128)(2,1)S(1)}, u32[]{:S(2)}, u32[]{:S(2)}) collective-permute-start(bf16[96,896]{1,0:T(8,128)(2,1)S(1)} %get-tuple-element.217), channel_id=1, source_target_pairs={{0,2},{2,0},{4,6},{6,4},{8,10},{10,8},{12,14},{14,12},{1,3},{3,1},... | collective-permute-start | bytes 516104 | tf_op jit(solution)/shard_map/ppermute | solution.py:535
  139.3 8.7 %collective-permute-start.16 = (bf16[96,896]{1,0:T(8,128)(2,1)S(1)}, bf16[96,896]{1,0:T(8,128)(2,1)S(1)}, u32[]{:S(2)}, u32[]{:S(2)}) collective-permute-start(bf16[96,896]{1,0:T(8,128)(2,1)S(1)} %get-tuple-element.216), channel_id=1, source_target_pairs={{0,4},{2,6},{4,0},{6,2},{8,12},{10,14},{12,8},{14,10},{1,5},{3,7},... | collective-permute-start | bytes 516104 | tf_op jit(solution)/shard_map/ppermute | solution.py:535
  140.8 41.7 %copy-start.59 = (bf16[768,768]{1,0:T(8,128)(2,1)}, bf16[768,768]{1,0:T(8,128)(2,1)S(1)}, u32[]{:S(2)}) copy-start(bf16[768,768]{1,0:T(8,128)(2,1)S(1)} %constant_dynamic-update-slice_fusion.17.dout_ref) | copy-start | bytes 3538948
  140.8 10.1 %collective-permute-start.17 = (bf16[96,896]{1,0:T(8,128)(2,1)S(1)}, bf16[96,896]{1,0:T(8,128)(2,1)S(1)}, u32[]{:S(2)}, u32[]{:S(2)}) collective-permute-start(bf16[96,896]{1,0:T(8,128)(2,1)S(1)} %get-tuple-element.215), channel_id=1, source_target_pairs={{0,6},{2,4},{4,2},{6,0},{8,14},{10,12},{12,10},{14,8},{1,7},{3,5},... | collective-permute-start | bytes 516104 | tf_op jit(solution)/shard_map/ppermute | solution.py:535
  142.3 9.3 %collective-permute-start.18 = (bf16[96,896]{1,0:T(8,128)(2,1)S(1)}, bf16[96,896]{1,0:T(8,128)(2,1)S(1)}, u32[]{:S(2)}, u32[]{:S(2)}) collective-permute-start(bf16[96,896]{1,0:T(8,128)(2,1)S(1)} %get-tuple-element.214), channel_id=1, source_target_pairs={{0,8},{2,10},{4,12},{6,14},{8,0},{10,2},{12,4},{14,6},{1,9},{3,11}... | collective-permute-start | bytes 516104 | tf_op jit(solution)/shard_map/ppermute | solution.py:535
  143.0 34.3 %collective-permute-start.19 = (bf16[96,896]{1,0:T(8,128)(2,1)S(1)}, bf16[96,896]{1,0:T(8,128)(2,1)S(1)}, u32[]{:S(2)}, u32[]{:S(2)}) collective-permute-start(bf16[96,896]{1,0:T(8,128)(2,1)S(1)} %get-tuple-element.213), channel_id=1, source_target_pairs={{0,10},{2,8},{4,14},{6,12},{8,2},{10,0},{12,6},{14,4},{1,11},{3,9}... | collective-permute-start | bytes 516104 | tf_op jit(solution)/shard_map/ppermute | solution.py:535
  146.1 33.9 %collective-permute-start.20 = (bf16[96,896]{1,0:T(8,128)(2,1)S(1)}, bf16[96,896]{1,0:T(8,128)(2,1)S(1)}, u32[]{:S(2)}, u32[]{:S(2)}) collective-permute-start(bf16[96,896]{1,0:T(8,128)(2,1)S(1)} %get-tuple-element.212), channel_id=1, source_target_pairs={{0,12},{2,14},{4,8},{6,10},{8,4},{10,6},{12,0},{14,2},{1,13},{3,15... | collective-permute-start | bytes 516104 | tf_op jit(solution)/shard_map/ppermute | solution.py:535
  148.0 34.5 %collective-permute-start.21 = (bf16[96,896]{1,0:T(8,128)(2,1)S(1)}, bf16[96,896]{1,0:T(8,128)(2,1)S(1)}, u32[]{:S(2)}, u32[]{:S(2)}) collective-permute-start(bf16[96,896]{1,0:T(8,128)(2,1)S(1)} %get-tuple-element.211), channel_id=1, source_target_pairs={{0,14},{2,12},{4,10},{6,8},{8,6},{10,4},{12,2},{14,0},{1,15},{3,13... | collective-permute-start | bytes 516104 | tf_op jit(solution)/shard_map/ppermute | solution.py:535
  220.0 8.0 %collective-permute-start.24 = (bf16[96,896]{1,0:T(8,128)(2,1)S(1)}, bf16[96,896]{1,0:T(8,128)(2,1)S(1)}, u32[]{:S(2)}, u32[]{:S(2)}) collective-permute-start(bf16[96,896]{1,0:T(8,128)(2,1)S(1)} %get-tuple-element.209), channel_id=1, source_target_pairs={{0,2},{2,0},{4,6},{6,4},{8,10},{10,8},{12,14},{14,12},{1,3},{3,1},... | collective-permute-start | bytes 516104 | tf_op jit(solution)/shard_map/ppermute | solution.py:535
  220.7 7.3 %collective-permute-start.25 = (bf16[96,896]{1,0:T(8,128)(2,1)S(1)}, bf16[96,896]{1,0:T(8,128)(2,1)S(1)}, u32[]{:S(2)}, u32[]{:S(2)}) collective-permute-start(bf16[96,896]{1,0:T(8,128)(2,1)S(1)} %get-tuple-element.208), channel_id=1, source_target_pairs={{0,4},{2,6},{4,0},{6,2},{8,12},{10,14},{12,8},{14,10},{1,5},{3,7},... | collective-permute-start | bytes 516104 | tf_op jit(solution)/shard_map/ppermute | solution.py:535
  222.0 8.9 %collective-permute-start.26 = (bf16[96,896]{1,0:T(8,128)(2,1)S(1)}, bf16[96,896]{1,0:T(8,128)(2,1)S(1)}, u32[]{:S(2)}, u32[]{:S(2)}) collective-permute-start(bf16[96,896]{1,0:T(8,128)(2,1)S(1)} %get-tuple-element.207), channel_id=1, source_target_pairs={{0,6},{2,4},{4,2},{6,0},{8,14},{10,12},{12,10},{14,8},{1,7},{3,5},... | collective-permute-start | bytes 516104 | tf_op jit(solution)/shard_map/ppermute | solution.py:535
  224.6 7.2 %collective-permute-start.27 = (bf16[96,896]{1,0:T(8,128)(2,1)S(1)}, bf16[96,896]{1,0:T(8,128)(2,1)S(1)}, u32[]{:S(2)}, u32[]{:S(2)}) collective-permute-start(bf16[96,896]{1,0:T(8,128)(2,1)S(1)} %get-tuple-element.206), channel_id=1, source_target_pairs={{0,8},{2,10},{4,12},{6,14},{8,0},{10,2},{12,4},{14,6},{1,9},{3,11}... | collective-permute-start | bytes 516104 | tf_op jit(solution)/shard_map/ppermute | solution.py:535
  224.6 10.1 %collective-permute-start.28 = (bf16[96,896]{1,0:T(8,128)(2,1)S(1)}, bf16[96,896]{1,0:T(8,128)(2,1)S(1)}, u32[]{:S(2)}, u32[]{:S(2)}) collective-permute-start(bf16[96,896]{1,0:T(8,128)(2,1)S(1)} %get-tuple-element.205), channel_id=1, source_target_pairs={{0,10},{2,8},{4,14},{6,12},{8,2},{10,0},{12,6},{14,4},{1,11},{3,9}... | collective-permute-start | bytes 516104 | tf_op jit(solution)/shard_map/ppermute | solution.py:535
  228.0 8.0 %collective-permute-start.29 = (bf16[96,896]{1,0:T(8,128)(2,1)S(1)}, bf16[96,896]{1,0:T(8,128)(2,1)S(1)}, u32[]{:S(2)}, u32[]{:S(2)}) collective-permute-start(bf16[96,896]{1,0:T(8,128)(2,1)S(1)} %get-tuple-element.204), channel_id=1, source_target_pairs={{0,12},{2,14},{4,8},{6,10},{8,4},{10,6},{12,0},{14,2},{1,13},{3,15... | collective-permute-start | bytes 516104 | tf_op jit(solution)/shard_map/ppermute | solution.py:535
  228.0 10.2 %collective-permute-start.30 = (bf16[96,896]{1,0:T(8,128)(2,1)S(1)}, bf16[96,896]{1,0:T(8,128)(2,1)S(1)}, u32[]{:S(2)}, u32[]{:S(2)}) collective-permute-start(bf16[96,896]{1,0:T(8,128)(2,1)S(1)} %get-tuple-element.203), channel_id=1, source_target_pairs={{0,14},{2,12},{4,10},{6,8},{8,6},{10,4},{12,2},{14,0},{1,15},{3,13... | collective-permute-start | bytes 516104 | tf_op jit(solution)/shard_map/ppermute | solution.py:535
  245.8 15.6 %collective-permute-start.31 = (bf16[512,384]{1,0:T(8,128)(2,1)}, bf16[512,384]{1,0:T(8,128)(2,1)}, u32[]{:S(2)}, u32[]{:S(2)}) collective-permute-start(bf16[512,384]{1,0:T(8,128)(2,1)} %constant_dynamic-slice_fusion.5), channel_id=1, source_target_pairs={{0,4},{4,0},{1,5},{5,1},{2,6},{6,2},{3,7},{7,3},{8,12},{12,8},{9,1... | collective-permute-start | bytes 1179656 | tf_op jit(solution)/shard_map/ppermute | solution.py:83
  251.8 12.8 %collective-permute-start.32 = (bf16[96,768]{1,0:T(8,128)(2,1)}, bf16[96,768]{1,0:T(8,128)(2,1)}, u32[]{:S(2)}, u32[]{:S(2)}) collective-permute-start(bf16[96,768]{1,0:T(8,128)(2,1)} %get-tuple-element.227), channel_id=1, source_target_pairs={{0,2},{2,0},{4,6},{6,4},{8,10},{10,8},{12,14},{14,12},{1,3},{3,1},... | collective-permute-start | bytes 442376 | tf_op jit(solution)/shard_map/ppermute | solution.py:535
  252.2 13.3 %collective-permute-start.33 = (bf16[96,768]{1,0:T(8,128)(2,1)}, bf16[96,768]{1,0:T(8,128)(2,1)}, u32[]{:S(2)}, u32[]{:S(2)}) collective-permute-start(bf16[96,768]{1,0:T(8,128)(2,1)} %get-tuple-element.226), channel_id=1, source_target_pairs={{0,4},{2,6},{4,0},{6,2},{8,12},{10,14},{12,8},{14,10},{1,5},{3,7},... | collective-permute-start | bytes 442376 | tf_op jit(solution)/shard_map/ppermute | solution.py:535
  253.1 47.0 %collective-permute-start.34 = (bf16[96,768]{1,0:T(8,128)(2,1)}, bf16[96,768]{1,0:T(8,128)(2,1)}, u32[]{:S(2)}, u32[]{:S(2)}) collective-permute-start(bf16[96,768]{1,0:T(8,128)(2,1)} %get-tuple-element.225), channel_id=1, source_target_pairs={{0,6},{2,4},{4,2},{6,0},{8,14},{10,12},{12,10},{14,8},{1,7},{3,5},... | collective-permute-start | bytes 442376 | tf_op jit(solution)/shard_map/ppermute | solution.py:535
  255.3 44.9 %collective-permute-start.35 = (bf16[96,768]{1,0:T(8,128)(2,1)}, bf16[96,768]{1,0:T(8,128)(2,1)}, u32[]{:S(2)}, u32[]{:S(2)}) collective-permute-start(bf16[96,768]{1,0:T(8,128)(2,1)} %get-tuple-element.224), channel_id=1, source_target_pairs={{0,8},{2,10},{4,12},{6,14},{8,0},{10,2},{12,4},{14,6},{1,9},{3,11}... | collective-permute-start | bytes 442376 | tf_op jit(solution)/shard_map/ppermute | solution.py:535
  261.5 38.7 %collective-permute-start.36 = (bf16[96,768]{1,0:T(8,128)(2,1)}, bf16[96,768]{1,0:T(8,128)(2,1)S(1)}, u32[]{:S(2)}, u32[]{:S(2)}) collective-permute-start(bf16[96,768]{1,0:T(8,128)(2,1)} %get-tuple-element.223), channel_id=1, source_target_pairs={{0,10},{2,8},{4,14},{6,12},{8,2},{10,0},{12,6},{14,4},{1,11},{3,9}... | collective-permute-start | bytes 442376 | tf_op jit(solution)/shard_map/ppermute | solution.py:535
  264.7 35.6 %collective-permute-start.37 = (bf16[96,768]{1,0:T(8,128)(2,1)S(1)}, bf16[96,768]{1,0:T(8,128)(2,1)S(1)}, u32[]{:S(2)}, u32[]{:S(2)}) collective-permute-start(bf16[96,768]{1,0:T(8,128)(2,1)S(1)} %copy-done.41), channel_id=1, source_target_pairs={{0,12},{2,14},{4,8},{6,10},{8,4},{10,6},{12,0},{14,2},{1,13},{3,15... | collective-permute-start | bytes 442376 | tf_op jit(solution)/shard_map/ppermute | solution.py:535
  265.5 34.7 %collective-permute-start.38 = (bf16[96,768]{1,0:T(8,128)(2,1)S(1)}, bf16[96,768]{1,0:T(8,128)(2,1)S(1)}, u32[]{:S(2)}, u32[]{:S(2)}) collective-permute-start(bf16[96,768]{1,0:T(8,128)(2,1)S(1)} %get-tuple-element.221), channel_id=1, source_target_pairs={{0,14},{2,12},{4,10},{6,8},{8,6},{10,4},{12,2},{14,0},{1,15},{3,13... | collective-permute-start | bytes 442376 | tf_op jit(solution)/shard_map/ppermute | solution.py:535
  300.1 7.1 %collective-permute-start.40 = (bf16[2,2,4,24,768]{4,3,2,1,0:T(8,128)(2,1)S(1)}, bf16[2,2,4,24,768]{4,3,2,1,0:T(8,128)(2,1)S(1)}, u32[]{:S(2)}, u32[]{:S(2)}) collective-permute-start(bf16[2,2,4,24,768]{4,3,2,1,0:T(8,128)(2,1)S(1)} %bitcast.238), channel_id=1, source_target_pairs={{0,1},{1,0},{2,3},{3,2},{4,5},{5,4},{6,7},{7,6},{8,9},{9,8},{10,11... | collective-permute-start | bytes 1769480 | tf_op jit(solution)/shard_map/ppermute | solution.py:83
  302.0 5.6 %collective-permute-start.39 = (bf16[2,2,4,24,1280]{4,3,2,1,0:T(8,128)(2,1)S(1)}, bf16[2,2,4,24,1280]{4,3,2,1,0:T(8,128)(2,1)S(1)}, u32[]{:S(2)}, u32[]{:S(2)}) collective-permute-start(bf16[2,2,4,24,1280]{4,3,2,1,0:T(8,128)(2,1)S(1)} %bitcast.237), channel_id=1, source_target_pairs={{0,1},{1,0},{2,3},{3,2},{4,5},{5,4},{6,7},{7,6},{8,9},{9,8},{10,11... | collective-permute-start | bytes 2949128 | tf_op jit(solution)/shard_map/ppermute | solution.py:83
  308.2 12.0 %collective-permute-start.41 = (bf16[4,24,2048]{2,1,0:T(8,128)(2,1)S(1)}, bf16[4,24,2048]{2,1,0:T(8,128)(2,1)S(1)}, u32[]{:S(2)}, u32[]{:S(2)}) collective-permute-start(bf16[4,24,2048]{2,1,0:T(8,128)(2,1)S(1)} %get-tuple-element.200), channel_id=1, source_target_pairs={{0,2},{2,0},{4,6},{6,4},{1,3},{3,1},{5,7},{7,5},{8,10},{10,8},{12,... | collective-permute-start | bytes 1179656 | tf_op jit(solution)/shard_map/ppermute | solution.py:647
  311.3 16.4 %collective-permute-start.44 = (bf16[4,24,2048]{2,1,0:T(8,128)(2,1)S(1)}, bf16[4,24,2048]{2,1,0:T(8,128)(2,1)S(1)}, u32[]{:S(2)}, u32[]{:S(2)}) collective-permute-start(bf16[4,24,2048]{2,1,0:T(8,128)(2,1)S(1)} %get-tuple-element.199), channel_id=1, source_target_pairs={{0,6},{2,4},{4,2},{6,0},{1,7},{3,5},{5,3},{7,1},{8,14},{10,12},{12... | collective-permute-start | bytes 1179656 | tf_op jit(solution)/shard_map/ppermute | solution.py:647
  312.7 20.5 %collective-permute-start.43 = (bf16[4,24,2048]{2,1,0:T(8,128)(2,1)S(1)}, bf16[4,24,2048]{2,1,0:T(8,128)(2,1)S(1)}, u32[]{:S(2)}, u32[]{:S(2)}) collective-permute-start(bf16[4,24,2048]{2,1,0:T(8,128)(2,1)S(1)} %get-tuple-element.198), channel_id=1, source_target_pairs={{0,4},{2,6},{4,0},{6,2},{1,5},{3,7},{5,1},{7,3},{8,12},{10,14},{12... | collective-permute-start | bytes 1179656 | tf_op jit(solution)/shard_map/ppermute | solution.py:647
  321.9 31.5 %collective-permute-start.42 = (bf16[512,768]{1,0:T(8,128)(2,1)S(1)}, bf16[512,768]{1,0:T(8,128)(2,1)S(1)}, u32[]{:S(2)}, u32[]{:S(2)}) collective-permute-start(bf16[512,768]{1,0:T(8,128)(2,1)S(1)} %dynamic-slice_convert_fusion), channel_id=1, source_target_pairs={{0,4},{4,0},{1,5},{5,1},{2,6},{6,2},{3,7},{7,3},{8,12},{12,8},{9,1... | collective-permute-start | bytes 2359304 | tf_op jit(solution)/shard_map/ppermute | solution.py:83
  351.3 6.8 %collective-permute-start.47 = (bf16[24,3200]{1,0:T(8,128)(2,1)S(1)}, bf16[24,3200]{1,0:T(8,128)(2,1)S(1)}, u32[]{:S(2)}, u32[]{:S(2)}) collective-permute-start(bf16[24,3200]{1,0:T(8,128)(2,1)S(1)} %get-tuple-element.242), channel_id=1, source_target_pairs={{0,24},{8,0},{16,8},{24,16},{1,25},{9,1},{17,9},{25,17},{2,26},{10... | collective-permute-start | bytes 460808 | tf_op jit(solution)/shard_map/ppermute | solution.py:110
  352.5 13.2 %collective-permute-start.46 = (bf16[24,3200]{1,0:T(8,128)(2,1)S(1)}, bf16[24,3200]{1,0:T(8,128)(2,1)S(1)}, u32[]{:S(2)}, u32[]{:S(2)}) collective-permute-start(bf16[24,3200]{1,0:T(8,128)(2,1)S(1)} %get-tuple-element.243), channel_id=1, source_target_pairs={{0,16},{8,24},{16,0},{24,8},{1,17},{9,25},{17,1},{25,9},{2,18},{10... | collective-permute-start | bytes 460808 | tf_op jit(solution)/shard_map/ppermute | solution.py:110
  352.6 13.2 %collective-permute-start.45 = (bf16[24,3200]{1,0:T(8,128)(2,1)S(1)}, bf16[24,3200]{1,0:T(8,128)(2,1)S(1)}, u32[]{:S(2)}, u32[]{:S(2)}) collective-permute-start(bf16[24,3200]{1,0:T(8,128)(2,1)S(1)} %get-tuple-element.241), channel_id=1, source_target_pairs={{0,8},{8,16},{16,24},{24,0},{1,9},{9,17},{17,25},{25,1},{2,10},{10... | collective-permute-start | bytes 460808 | tf_op jit(solution)/shard_map/ppermute | solution.py:110
  354.3 28.8 %collective-permute-start.49 = (bf16[3,96,2048]{2,1,0:T(8,128)(2,1)S(1)}, bf16[3,96,2048]{2,1,0:T(8,128)(2,1)S(1)}, u32[]{:S(2)}, u32[]{:S(2)}) collective-permute-start(bf16[3,96,2048]{2,1,0:T(8,128)(2,1)S(1)} %get-tuple-element.192), channel_id=1, source_target_pairs={{0,4},{1,12},{4,0},{5,8},{8,5},{9,13},{12,1},{13,9},{2,6},{3,14},{... | collective-permute-start | bytes 3538952 | tf_op jit(solution)/shard_map/ppermute | solution.py:457
  355.8 27.3 %collective-permute-start.48 = (bf16[3,96,2048]{2,1,0:T(8,128)(2,1)S(1)}, bf16[3,96,2048]{2,1,0:T(8,128)(2,1)S(1)}, u32[]{:S(2)}, u32[]{:S(2)}) collective-permute-start(bf16[3,96,2048]{2,1,0:T(8,128)(2,1)S(1)} %get-tuple-element.193), channel_id=1, source_target_pairs={{1,8},{8,1},{3,10},{10,3},{5,12},{12,5},{7,14},{14,7},{17,24},{24,... | collective-permute-start | bytes 3538952 | tf_op jit(solution)/shard_map/ppermute | solution.py:448
  398.2 6.9 %collective-permute-start.50 = (f32[2,128]{1,0:T(2,128)S(1)}, f32[2,128]{1,0:T(2,128)S(1)}, u32[]{:S(2)}, u32[]{:S(2)}) collective-permute-start(f32[2,128]{1,0:T(2,128)S(1)} %pad_bitcast_fusion), channel_id=1, source_target_pairs={{0,1},{1,0},{2,3},{3,2},{4,5},{5,4},{6,7},{7,6},{8,9},{9,8},{10,11... | collective-permute-start | bytes 3080 | tf_op jit(solution)/shard_map/ppermute | solution.py:133
  405.1 3.6 collective-permute-start.52
  406.8 4.5 %collective-permute-start.53 = (f32[2,128]{1,0:T(2,128)S(1)}, f32[2,128]{1,0:T(2,128)S(1)}, u32[]{:S(2)}, u32[]{:S(2)}) collective-permute-start(f32[2,128]{1,0:T(2,128)S(1)} %fusion.119), channel_id=1, source_target_pairs={{0,6},{2,4},{4,2},{6,0},{1,7},{3,5},{5,3},{7,1},{8,14},{10,12},{12... | collective-permute-start | bytes 3080 | tf_op jit(solution)/shard_map/ppermute | solution.py:133
  408.3 3.6 collective-permute-start.51
  411.9 9.1 %collective-permute-start.55 = (f32[2,128]{1,0:T(2,128)S(1)}, f32[2,128]{1,0:T(2,128)S(1)}, u32[]{:S(2)}, u32[]{:S(2)}) collective-permute-start(f32[2,128]{1,0:T(2,128)S(1)} %add_add_fusion.1), channel_id=1, source_target_pairs={{0,16},{8,24},{16,0},{24,8},{1,17},{9,25},{17,1},{25,9},{2,18},{10... | collective-permute-start | bytes 3080 | tf_op jit(solution)/shard_map/ppermute | solution.py:133
  412.2 8.7 %collective-permute-start.56 = (f32[2,128]{1,0:T(2,128)S(1)}, f32[2,128]{1,0:T(2,128)S(1)}, u32[]{:S(2)}, u32[]{:S(2)}) collective-permute-start(f32[2,128]{1,0:T(2,128)S(1)} %add_add_fusion.1), channel_id=1, source_target_pairs={{0,24},{8,16},{16,8},{24,0},{1,25},{9,17},{17,9},{25,1},{2,26},{10... | collective-permute-start | bytes 3080 | tf_op jit(solution)/shard_map/ppermute | solution.py:133
  415.8 5.1 %collective-permute-start.54 = (f32[2,128]{1,0:T(2,128)S(1)}, f32[2,128]{1,0:T(2,128)S(1)}, u32[]{:S(2)}, u32[]{:S(2)}) collective-permute-start(f32[2,128]{1,0:T(2,128)S(1)} %add_add_fusion.1), channel_id=1, source_target_pairs={{0,8},{8,0},{16,24},{24,16},{1,9},{9,1},{17,25},{25,17},{2,10},{10... | collective-permute-start | bytes 3080 | tf_op jit(solution)/shard_map/ppermute | solution.py:133
  (96 other events, 685.6 us)
Sparse Core Ops, SparseCore 0:
  35.0 76.7 all-gather.2
  113.3 62.7 all-gather.4
  215.4 133.7 reduce-scatter.1
